TPU v7x, 512 devices: a whole 4x8x8 slice. The times are simulated.
512 devices in a mesh: dp: 64 (over y, z_hi, core), tensor: 8 (over z_lo, x).
Axes of the slice: x: 4, y: 8, z: 8 (z_hi: 4, z_lo: 2; z = z_hi * 2 + z_lo), core: 2. Of those that a mesh axis runs over, the one named last changes fastest.
Arguments:
- layer_input: bfloat16 [8192, 4096], P('dp', 'tensor'), may hold values from -6 to 6
- routed_delta: bfloat16 [8192, 8, 1024], P('dp', None, 'tensor'), may hold values from -1.5 to 1.5
- shared_delta: bfloat16 [8192, 1024], P(('dp', 'tensor')), may hold values from -6 to 6
- expert_weight: bfloat16 [128, 1024, 4096], P('dp', None, 'tensor'), may hold values from -0.1875 to 0.1875
- shared_weight: bfloat16 [1024, 4096], P('dp', 'tensor'), may hold values from -0.1875 to 0.1875
- routing: int32 [8192, 8], P('dp'), may hold values from 0 to 127, all different within a row; in each aligned block of 128 rows (0 to 127, 128 to 255, ...) at most 10 rows name the same one
- slot_expert: int32 [128], replicated, may hold values from 0 to 127, each once
Outputs:
- input_gradient: bfloat16 [8192, 4096], P('dp', 'tensor')
- expert_gradient: bfloat16 [128, 1024, 4096], P('dp', None, 'tensor')
- shared_gradient: float32 [1024, 4096], P('dp', 'tensor')
Inputs may be any that keep to these rules, and one draw needn't show every extreme that they name: `routing`: each row names 8 different experts; in each aligned block of 128 rows no expert is named more than 10 times, a bound that some block reaches. `slot_expert`: A permutation of the experts.
All inputs are finite; a program needn't handle non-finite values.
Results may differ from a plain program's by a relative error of at most 0.0047.
Values may be sent and summed in bfloat16 or wider, within the bound.
No kernel may reach another device: no remote copies, remote signals or barrier semaphores. Data moves between devices by JAX's collectives and lax.ppermute only.
A program may use at most 64 MiB of HBM per device.

v0:
```python
import jax
import jax.numpy as jnp
from jax import lax
from jax.sharding import PartitionSpec as P


def passed_along(block, axis, distance):
    devices = range(lax.axis_size(axis))
    route = [((i - distance) % len(devices), i) for i in devices]
    return lax.ppermute(block, axis, route)


def body(
    layer_input, routed_delta, shared_delta, expert_weight, shared_weight, routing, slot_expert
):
    tok_count, top_count = routing.shape
    expert_count = slot_expert.shape[0]
    local_count = expert_weight.shape[0]
    feature_count = layer_input.shape[1]
    dp_count = lax.axis_size("dp")
    my_index = lax.axis_index("dp")
    most_rows = max(2, (5 * tok_count * top_count + 4 * expert_count - 1) // (4 * expert_count))
    shared_all = lax.all_gather(shared_delta, "tensor", axis=0, tiled=True)
    columns = shared_all
    shared_term = jnp.dot(
        columns,
        lax.all_gather(shared_weight, "dp", axis=0, tiled=True),
        preferred_element_type=jnp.float32,
    )
    columns = shared_all
    shared_gradient = lax.psum_scatter(
        lax.dot_general(
            columns, layer_input, (((0,), (0,)), ((), ())), preferred_element_type=jnp.float32
        ),
        "dp",
        scatter_dimension=0,
        tiled=True,
    )
    storage = jnp.arange(expert_count, dtype=jnp.int32)
    matches = routing[:, :, None] == slot_expert[None, None, :]
    slot_of = jnp.sum(jnp.where(matches, storage[None, None, :], 0), axis=2)
    owner = slot_of // local_count
    within = slot_of % local_count
    block_count = local_count + 1
    distance = (my_index - owner) % dp_count
    moved = (within == 0) & (distance >= dp_count // 2)
    target = jnp.where(moved, (owner - 1) % dp_count, owner)
    block = jnp.where(moved, local_count, within)
    slot_key = (target * block_count + block).reshape(-1)
    key_range = jnp.arange(dp_count * block_count, dtype=jnp.int32)
    onehot = (slot_key[:, None] == key_range[None, :]).astype(jnp.int32)
    slot_rank = jnp.sum(jnp.cumsum(onehot, axis=0) * onehot, axis=1) - 1
    slot_pos = slot_key * most_rows + slot_rank
    buffer_rows = dp_count * block_count * most_rows
    flat_count = tok_count * top_count
    slot_at = (
        jnp.full((buffer_rows,), flat_count, jnp.int32)
        .at[slot_pos]
        .set(jnp.arange(flat_count, dtype=jnp.int32))
    )
    inputs_padded = jnp.concatenate(
        [layer_input, jnp.zeros((1, feature_count), layer_input.dtype)], axis=0
    )
    send_inputs = inputs_padded[slot_at // top_count].reshape(
        dp_count, block_count, most_rows, feature_count
    )
    deltas_whole = lax.all_gather(routed_delta, "tensor", axis=2, tiled=True)
    hidden_count = deltas_whole.shape[2]
    deltas_flat = jnp.concatenate(
        [
            deltas_whole.reshape(flat_count, hidden_count),
            jnp.zeros((1, hidden_count), routed_delta.dtype),
        ],
        axis=0,
    )
    send_deltas = deltas_flat[slot_at].reshape(dp_count, block_count, most_rows, hidden_count)
    arrived_inputs, arrived_delta = (
        lax.all_to_all(send_inputs, "dp", split_axis=0, concat_axis=0, tiled=True),
        lax.all_to_all(send_deltas, "dp", split_axis=0, concat_axis=0, tiled=True),
    )
    borrowed = passed_along(expert_weight[0], "dp", -1)
    weights_all = jnp.concatenate([expert_weight, borrowed[None]], axis=0)
    partial_value = jnp.einsum(
        "sbmh,sbmd->bhd", arrived_delta, arrived_inputs, preferred_element_type=jnp.float32
    )
    outgoing = jnp.einsum(
        "sbmh,bhd->sbmd", arrived_delta, weights_all, preferred_element_type=jnp.float32
    ).astype(jnp.bfloat16)
    returned = lax.all_to_all(outgoing, "dp", split_axis=0, concat_axis=0, tiled=True)
    routed_rows = returned.reshape(buffer_rows, feature_count)[slot_pos].reshape(
        tok_count, top_count, feature_count
    )
    routed_sum = jnp.sum(routed_rows.astype(jnp.float32), axis=1)
    input_gradient = (routed_sum + shared_term).astype(jnp.bfloat16)
    owned = partial_value[:local_count]
    handed = passed_along(partial_value[local_count], "dp", 1)
    owned = owned.at[0].add(handed)
    return (input_gradient, owned.astype(jnp.bfloat16), shared_gradient)


def solution(mesh):
    return jax.shard_map(
        body,
        mesh=mesh,
        in_specs=(
            P("dp", "tensor"),
            P("dp", None, "tensor"),
            P(("dp", "tensor"), None),
            P("dp", None, "tensor"),
            P("dp", "tensor"),
            P("dp", None),
            P(),
        ),
        out_specs=(P("dp", "tensor"), P("dp", None, "tensor"), P("dp", "tensor")),
        check_vma=False,
    )
```

profile of v0, /device:TPU:1, one launch (start us, length us, event | category | flops | bytes accessed | tf_op | source)
XLA Modules:
  0.0 564.5 jit_solution(18359680222103138052)
XLA Ops:
  8.7 0.8 copy.34
  9.5 3.0 select_reduce_fusion
  14.2 4.3 scatter_custom_fusion
  18.5 44.6 %all-gather.3.cloned.1.call-done = bf16[128,8,1024]{2,1,0:T(8,128)(2,1)} async-done(((bf16[128,8,128]{2,1,0:T(8,128)(2,1)}), bf16[128,8,1024]{2,1,0:T(8,128)(2,1)}) %all-gather.3.cloned.1.call-update) | async-done | bytes 2097168 | tf_op jit(solution)/shard_map/all_gather | solution.py:67
  63.1 1.8 concatenate.12
  64.9 7.3 %gather_fusion = bf16[1920,1024]{1,0:T(8,128)(2,1)} fusion(bf16[1025,1024]{1,0:T(8,128)(2,1)S(1)} %concatenate.12, s32[2048]{0:T(1024)S(1)} %pad_clamp_fusion.1), kind=kCustom, calls=%fused_computation | custom fusion | bytes 7872000 | tf_op jit(solution)/shard_map/gather | solution.py:76
  72.2 8.1 %reshape.310 = bf16[64,3,10,1024]{3,2,1,0:T(8,128)(2,1)} reshape(bf16[1920,1024]{1,0:T(8,128)(2,1)} %gather_fusion) | data formatting | bytes 7864320 | tf_op jit(solution)/shard_map/reshape | solution.py:76
  80.3 9.1 %copy.37 = bf16[64,3,10,1024]{3,1,2,0:T(4,128)(2,1)} copy(bf16[64,3,10,1024]{3,2,1,0:T(8,128)(2,1)} %reshape.310) | data formatting | bytes 7864320 | tf_op jit(solution)/shard_map/reshape | solution.py:76
  89.5 17.2 %all-to-all-start = ((bf16[64,3,10,1024]{3,1,2,0:T(4,128)(2,1)}), bf16[64,3,10,1024]{3,1,2,0:T(4,128)(2,1)}, u32[]{:S(2)}, u32[]{:S(2)}) async-start(bf16[64,3,10,1024]{3,1,2,0:T(4,128)(2,1)} %copy.37), calls=%async_computation | async-start | bytes 10485760 | tf_op jit(solution)/shard_map/all_to_all | solution.py:79
  106.7 6.8 %gather_fusion.2 = bf16[1920,512]{1,0:T(8,128)(2,1)} fusion(bf16[129,512]{1,0:T(8,128)(2,1)S(1)} %concatenate.13, s32[2048]{0:T(1024)S(1)} %pad_clamp_fusion), kind=kCustom, calls=%fused_computation.2 | custom fusion | bytes 3939840 | tf_op jit(solution)/shard_map/gather | solution.py:64
  113.5 3.4 reshape.312
  116.9 3.5 copy.41
  120.4 131.4 %all-to-all-done = bf16[64,3,10,1024]{3,1,2,0:T(4,128)(2,1)} async-done(((bf16[64,3,10,1024]{3,1,2,0:T(4,128)(2,1)}), bf16[64,3,10,1024]{3,1,2,0:T(4,128)(2,1)}, u32[]{:S(2)}, u32[]{:S(2)}) %all-to-all-start) | async-done | bytes 3932192 | tf_op jit(solution)/shard_map/all_to_all | solution.py:79
  251.8 25.6 %all-to-all-start.2 = ((bf16[64,3,10,512]{3,1,2,0:T(4,128)(2,1)}), bf16[64,3,10,512]{3,1,2,0:T(4,128)(2,1)S(1)}, u32[]{:S(2)}, u32[]{:S(2)}) async-start(bf16[64,3,10,512]{3,1,2,0:T(4,128)(2,1)} %copy.41), calls=%async_computation.2 | async-start | bytes 5242880 | tf_op jit(solution)/shard_map/all_to_all | solution.py:78
  277.9 1.3 slice_bitcast_fusion.1
  279.2 2.4 collective-permute-start
  281.6 80.5 %all_gather.10 = bf16[128,1024]{1,0:T(8,128)(2,1)S(1)} all-gather(bf16[16,1024]{1,0:T(8,128)(2,1)S(1)} %copy-done.2), channel_id=1, replica_groups=mesh['dp'=64,'tensor'=8] {'tensor'}, dimensions={0}, use_global_device_ids=true | all-gather | bytes 294912 | tf_op jit(solution)/shard_map/all_gather | solution.py:23
  362.1 7.5 %convert_bitcast_fusion = bf16[64,3,10,512]{3,0,2,1:T(8,128)(2,1)S(1)} fusion(bf16[64,3,10,1024]{3,1,2,0:T(4,128)(2,1)} %all-to-all-done, bf16[1,1024,512]{2,1,0:T(8,128)(2,1)S(1)} %bitcast.49, bf16[2,1024,512]{2,1,0:T(8,128)(2,1)} %param.12), kind=kOutput, calls=%fused_computation.17 | convolution fusion | flops 2020540416 | bytes 9043968 | tf_op jit(solution)/shard_map/sbmh,bhd->sbmd/dot_general | solution.py:86
  369.7 3.2 copy.39
  372.9 1.6 copy-done
  374.5 15.0 %all-to-all-start.1 = ((bf16[64,3,10,512]{3,1,2,0:T(4,128)(2,1)}), bf16[64,3,10,512]{3,1,2,0:T(4,128)(2,1)S(1)}, u32[]{:S(2)}, u32[]{:S(2)}) async-start(bf16[64,3,10,512]{3,1,2,0:T(4,128)(2,1)} %copy.39), calls=%async_computation.1 | async-start | bytes 5242880 | tf_op jit(solution)/shard_map/all_to_all | solution.py:89
  389.6 1.8 fusion.49
  391.4 9.0 %fusion.6 = f32[3,1024,512]{2,1,0:T(8,128)S(1)} fusion(bf16[64,3,10,1024]{3,1,2,0:T(4,128)(2,1)} %all-to-all-done, bf16[64,3,10,512]{3,1,2,0:T(4,128)(2,1)} %copy-done), kind=kOutput, calls=%fused_computation.11 | convolution fusion | flops 2013265920 | bytes 12189696 | tf_op jit(solution)/shard_map/sbmh,sbmd->bhd/dot_general | solution.py:83
  400.6 4.5 collective-permute-start.1
  405.1 1.6 slice.52
  406.7 88.3 %collective-permute-done.1 = f32[1024,512]{1,0:T(8,128)S(1)} collective-permute-done((f32[1024,512]{1,0:T(8,128)S(1)}, f32[1024,512]{1,0:T(8,128)S(1)}, u32[]{:S(2)}, u32[]{:S(2)}) %collective-permute-start.1) | collective-permute-done | bytes 2097184 | tf_op jit(solution)/shard_map/ppermute | solution.py:10
  495.0 1.3 fusion.9
  496.3 2.6 copy.40
  498.9 3.7 reshape.311
  502.6 4.0 gather_fusion.1
  507.3 2.2 fusion.13
  509.5 47.6 %reduce-scatter.2.cloned.1.call-done = f32[16,512]{1,0:T(8,128)} async-done(((f32[1024,512]{1,0:T(8,128)}), f32[16,512]{1,0:T(8,128)}) %reduce-scatter.2.cloned.1.call-update) | async-done | bytes 32784 | tf_op jit(solution)/shard_map/reduce_scatter | solution.py:31
  (38 shorter events, 3.8 us)
Async XLA Ops:
  8.0 55.1 %all-gather.3.cloned.1.call-start = ((), (), s32[]{:S(2)}) async-start(), calls=%async_computation.4 | async-start | bytes 2359296 | tf_op jit(solution)/shard_map/all_gather | solution.py:67
  89.4 17.2 %copy-start.1 = (bf16[128,512]{1,0:T(8,128)(2,1)S(1)}, bf16[128,512]{1,0:T(8,128)(2,1)}, u32[]{:S(2)}) copy-start(bf16[128,512]{1,0:T(8,128)(2,1)} %param.9) | copy-start | bytes 393220
  89.5 162.3 %all-to-all-start = ((bf16[64,3,10,1024]{3,1,2,0:T(4,128)(2,1)}), bf16[64,3,10,1024]{3,1,2,0:T(4,128)(2,1)}, u32[]{:S(2)}, u32[]{:S(2)}) async-start(bf16[64,3,10,1024]{3,1,2,0:T(4,128)(2,1)} %copy.37), calls=%async_computation | async-start | bytes 10485760 | tf_op jit(solution)/shard_map/all_to_all | solution.py:79
  120.4 161.2 %copy-start.2 = (bf16[16,1024]{1,0:T(8,128)(2,1)S(1)}, bf16[16,1024]{1,0:T(8,128)(2,1)}, u32[]{:S(2)}) copy-start(bf16[16,1024]{1,0:T(8,128)(2,1)} %param.11) | copy-start | bytes 98308
  251.8 121.2 %all-to-all-start.2 = ((bf16[64,3,10,512]{3,1,2,0:T(4,128)(2,1)}), bf16[64,3,10,512]{3,1,2,0:T(4,128)(2,1)S(1)}, u32[]{:S(2)}, u32[]{:S(2)}) async-start(bf16[64,3,10,512]{3,1,2,0:T(4,128)(2,1)} %copy.41), calls=%async_computation.2 | async-start | bytes 5242880 | tf_op jit(solution)/shard_map/all_to_all | solution.py:78
  277.3 230.0 %all-gather.5.cloned.1.call-start = ((), (), s32[]{:S(2)}) async-start(), calls=%async_computation.5 | async-start | bytes 1064960 | tf_op jit(solution)/shard_map/all_gather | solution.py:27
  279.2 82.9 %collective-permute-start = (bf16[1024,512]{1,0:T(8,128)(2,1)S(1)}, bf16[1024,512]{1,0:T(8,128)(2,1)S(1)}, u32[]{:S(2)}, u32[]{:S(2)}) collective-permute-start(bf16[1024,512]{1,0:T(8,128)(2,1)S(1)} %slice_bitcast_fusion.1), channel_id=1, source_target_pairs={{8,0},{16,8},{24,16},{32,24},{40,32},{48,40},{56,48},{64,56},{72,6... | collective-permute-start | bytes 3145736 | tf_op jit(solution)/shard_map/ppermute | solution.py:10
  372.9 1.6 copy-start
  374.5 121.8 %all-to-all-start.1 = ((bf16[64,3,10,512]{3,1,2,0:T(4,128)(2,1)}), bf16[64,3,10,512]{3,1,2,0:T(4,128)(2,1)S(1)}, u32[]{:S(2)}, u32[]{:S(2)}) async-start(bf16[64,3,10,512]{3,1,2,0:T(4,128)(2,1)} %copy.39), calls=%async_computation.1 | async-start | bytes 5242880 | tf_op jit(solution)/shard_map/all_to_all | solution.py:89
  389.5 167.5 %reduce-scatter.2.cloned.1.call-start = ((), (), s32[]{:S(2)}) async-start(), calls=%async_computation.6 | async-start | bytes 2129920 | tf_op jit(solution)/shard_map/reduce_scatter | solution.py:31
  400.6 94.3 %collective-permute-start.1 = (f32[1024,512]{1,0:T(8,128)S(1)}, f32[1024,512]{1,0:T(8,128)S(1)}, u32[]{:S(2)}, u32[]{:S(2)}) collective-permute-start(f32[1024,512]{1,0:T(8,128)S(1)} %slice_bitcast_fusion), channel_id=1, source_target_pairs={{504,0},{0,8},{8,16},{16,24},{24,32},{32,40},{40,48},{48,56},{56,6... | collective-permute-start | bytes 6291464 | tf_op jit(solution)/shard_map/ppermute | solution.py:10
Sparse Core Ops, SparseCore 0:
  10.8 52.2 all-gather.2
Sparse Core Ops, SparseCore 1:
  281.1 116.7 all-gather.4
  402.9 154.1 reduce-scatter.1
where the time goes:
time: 569 us; the launch traced here: 565 us
  waiting for transfers between devices  313 us (55%)
  blocking collectives  80.5 us (14%)
  starting transfers between devices  64.7 us (11%)
  local copies, waits for them, and re-layouts  64.2 us (11%)
  matrix products  20.6 us (4%)
  between operations  15.7 us (3%)
  other arithmetic  5.69 us (1%)
    all_to_all x1, waiting for transfers between devices, body(): lax.all_to_all(send_deltas, 'dp', split_axis=0, concat_axis=0, tiled=True)  131 us
    ppermute x2, waiting for transfers between devices, passed_along(): return lax.ppermute(block, axis, route)  88.3 us
    all_gather x1, blocking collectives, body(): shared_all = lax.all_gather(shared_delta, 'tensor', axis=0, tiled=True)  80.5 us
    reduce_scatter x1, waiting for transfers between devices, body(): lax.psum_scatter(lax.dot_general(columns, layer_input, (((0,), (0,)), (()...  47.6 us
    all_gather x1, waiting for transfers between devices, body(): deltas_whole = lax.all_gather(routed_delta, 'tensor', axis=2, tiled=True)  44.6 us
    all_to_all x1, starting transfers between devices, body(): lax.all_to_all(send_inputs, 'dp', split_axis=0, concat_axis=0, tiled=True)  25.6 us
    reshape x2, local copies, waits for them, and re-layouts, body(): deltas_flat[slot_at].reshape(dp_count, block_count, most_rows, hidden_count)  17.2 us
    all_to_all x1, starting transfers between devices, body(): lax.all_to_all(send_deltas, 'dp', split_axis=0, concat_axis=0, tiled=True)  17.2 us
  transfers between devices with their start and end apart: 8, of which 4 were waited for; matrix products, arithmetic and copies ran while one was open for 11% of the time, Pallas kernels for 0%

commit v1 on v0

v1 whole, which is shorter than its diff:
```python
import functools

import jax
import jax.numpy as jnp
from jax import lax
from jax.experimental import pallas as pl
from jax.experimental.pallas import tpu as pltpu
from jax.sharding import PartitionSpec as P

MOST = 10
LANES = 128
BLOCK = 16
BF16 = jnp.bfloat16
F32 = jnp.float32
VMEM_LIMIT = 48 * 1024 * 1024


def dot(a, b, contract=((1,), (0,))):
    return lax.dot_general(a, b, (contract, ((), ())), preferred_element_type=F32)


class Plan:
    def __init__(self, slots, columns, group):
        self.slots, self.columns, self.group = slots, columns, group
        self.rows = slots * MOST
        self.padded = -(-self.rows // 8) * 8
        self.blocks = columns // LANES
        self.packed = self.blocks * self.rows
        self.slot_rows = group * MOST

    def wide_index(self, width):
        at = lax.broadcasted_iota(jnp.int32, (self.group * self.padded, width), 0)
        dest = at // self.padded
        return dest, at - dest * self.padded

    def packed_index(self, width):
        at = lax.broadcasted_iota(jnp.int32, (self.group * self.packed, width), 0)
        dest = at // self.packed
        at = at - dest * self.packed
        block = at // self.rows
        return dest, block, at - block * self.rows

    def expand(self, dest, at):
        slot = lax.broadcasted_iota(jnp.int32, dest.shape, 1)
        return one_hot(slot == jnp.where(at < self.rows, dest * self.slots + at // MOST, -1))

    def rank(self, at):
        return jnp.where(at < self.rows, at % MOST, -5).astype(F32)

    def slot_from_wide(self):
        shape = (self.slots * self.slot_rows, self.group * self.padded)
        at = lax.broadcasted_iota(jnp.int32, shape, 0)
        slot = at // self.slot_rows
        at = at - slot * self.slot_rows
        source = (at // MOST) * self.padded + slot * MOST + at % MOST
        return one_hot(lax.broadcasted_iota(jnp.int32, shape, 1) == source)

    def packed_from_slot(self):
        dest, _, at = self.packed_index(self.slots * self.slot_rows)
        source = (at // MOST) * self.slot_rows + dest * MOST + at % MOST
        return one_hot(lax.broadcasted_iota(jnp.int32, dest.shape, 1) == source)

    def block_mask(self):
        _, block, _ = self.packed_index(self.columns)
        return one_hot(lax.broadcasted_iota(jnp.int32, block.shape, 1) // LANES == block)


def one_hot(hit):
    return jnp.where(hit, 1.0, 0.0).astype(BF16)


ANYWHERE = pl.BlockSpec(memory_space=pl.ANY)
IN_VMEM = pl.BlockSpec(memory_space=pltpu.VMEM)
IN_SMEM = pl.BlockSpec(memory_space=pltpu.SMEM)


def call(kernel, outs, *args, index=(), scratch=(), after=()):
    given = len(index) + len(args)

    def run(*refs):
        kernel(*refs[:given], *refs[given + len(after) :])

    return pl.pallas_call(
        run,
        out_shape=outs,
        in_specs=[IN_SMEM] * len(index) + [IN_VMEM] * len(args) + [ANYWHERE] * len(after),
        scratch_shapes=list(scratch),
        compiler_params=pltpu.CompilerParams(vmem_limit_bytes=VMEM_LIMIT),
    )(*index, *args, *after)


def ready(values, after):
    return pl.pallas_call(
        lambda *refs: None,
        out_shape=tuple(jax.ShapeDtypeStruct(v.shape, v.dtype) for v in values),
        in_specs=[ANYWHERE] * (len(values) + len(after)),
        out_specs=tuple(ANYWHERE for _ in values),
        input_output_aliases={i: i for i in range(len(values))},
    )(*values, *after)


def select_deltas(plan, groups, top, route_ref, slot_ref, delta_ref, out_ref, place_ref):
    flat = route_ref.shape[1]
    tokens = flat // top
    hit = slot_ref[...] == route_ref[...]
    spread = one_hot(
        lax.broadcasted_iota(jnp.int32, (tokens, flat), 0) == lax.broadcasted_iota(jnp.int32, (tokens, flat), 1) // top
    )
    member = dot(one_hot(hit), spread, ((1,), (1,)))
    before = one_hot(
        lax.broadcasted_iota(jnp.int32, (tokens, tokens), 0) < lax.broadcasted_iota(jnp.int32, (tokens, tokens), 1)
    )
    ahead = dot(member.astype(BF16), before)
    place_ref[...] = jnp.where(member > 0.5, ahead, -1.0).astype(BF16)
    place_flat = jnp.where(hit, dot(ahead.astype(BF16), spread), -1.0).astype(BF16)
    slots, rows = plan.group * plan.slots, plan.group * plan.padded
    expand = plan.expand(*plan.wide_index(slots))
    rank = plan.rank(plan.wide_index(1)[1])
    for g in range(groups):
        value = dot(expand, place_flat[g * slots : (g + 1) * slots])
        out_ref[g * rows : (g + 1) * rows, :] = dot(one_hot(value == rank), delta_ref[...]).astype(BF16)


def by_block(plan, wide, block):
    total = wide[:, :LANES]
    for c in range(1, plan.blocks):
        total = jnp.where(block == c, wide[:, c * LANES : (c + 1) * LANES], total)
    return total.astype(BF16)


def widened(plan, packed, mask):
    return jnp.concatenate([packed] * plan.blocks, axis=1) * mask


def select_inputs(plan, groups, place_ref, input_ref, out_ref, chosen_ref):
    slots, rows = plan.group * plan.slots, plan.group * plan.packed
    dest, _, at = plan.packed_index(slots)
    expand = plan.expand(dest, at)
    _, block, at = plan.packed_index(LANES)
    rank = plan.rank(at)
    for g in range(groups):
        value = dot(expand, place_ref[g * slots : (g + 1) * slots, :])
        chosen = one_hot(value == rank)
        chosen_ref[g * rows : (g + 1) * rows, :] = chosen
        out_ref[g * rows : (g + 1) * rows, :] = by_block(plan, dot(chosen, input_ref[...]), block)


def place_of(index_ref, block, size):
    return pl.ds(pl.multiple_of(index_ref[block] * size, size), size)


def shared_partial(place_ref, delta_ref, input_ref, keep_ref, give_ref, sum_ref):
    sum_ref[...] = dot(delta_ref[...], input_ref[...], ((0,), (0,)))
    core = place_ref[1]
    rows = BLOCK
    for b in range(sum_ref.shape[0] // (2 * rows)):
        at = slice(b * rows, (b + 1) * rows)
        keep_ref[at, :] = sum_ref[pl.ds(pl.multiple_of((2 * b + core) * rows, rows), rows), :]
        give_ref[at, :] = sum_ref[pl.ds(pl.multiple_of((2 * b + 1 - core) * rows, rows), rows), :]


def shared_rows(place_ref, delta_ref, weight_ref, out_ref, sorted_ref):
    for k in range(weight_ref.shape[0] // BLOCK):
        z, core = (place_ref[0] - (k // 2) % 4) & 3, place_ref[1] ^ (k % 2)
        source = pl.multiple_of((k // 8 * 8 + z * 2 + core) * BLOCK, BLOCK)
        sorted_ref[k * BLOCK : (k + 1) * BLOCK, :] = weight_ref[pl.ds(source, BLOCK), :]
    out_ref[...] = dot(delta_ref[...], sorted_ref[...])


def project(plan, groups, index_ref, *refs):
    delta_refs, (weight_ref, out_ref, slot_delta_ref, value_ref, sorted_ref) = refs[:-5], refs[-5:]
    wide_rows, rows, part = plan.group * plan.padded, plan.group * plan.packed, plan.slot_rows
    for m in range(len(delta_refs)):
        for s in range(plan.slots):
            sorted_ref[s, m * LANES : (m + 1) * LANES, :] = weight_ref[s, place_of(index_ref, m, LANES), :]
    sort = plan.slot_from_wide()
    for g in range(groups):
        delta = jnp.concatenate([ref[g * wide_rows : (g + 1) * wide_rows, :] for ref in delta_refs], axis=1)
        delta = dot(sort, delta).astype(BF16)
        for s in range(plan.slots):
            slot_delta_ref[s, g * part : (g + 1) * part, :] = delta[s * part : (s + 1) * part]
    for s in range(plan.slots):
        value_ref[s] = dot(slot_delta_ref[s], sorted_ref[s]).astype(BF16)
    unsort = plan.packed_from_slot()
    block = plan.packed_index(LANES)[1]
    for g in range(groups):
        value = jnp.concatenate([value_ref[s, g * part : (g + 1) * part, :] for s in range(plan.slots)], axis=0)
        out_ref[g * rows : (g + 1) * rows, :] = by_block(plan, dot(unsort, value), block)


def weight_gradient(plan, groups, index_ref, slot_delta_ref, input_ref, out_ref, sorted_ref):
    rows, part = plan.group * plan.packed, plan.slot_rows
    unsort = plan.packed_from_slot()
    mask = plan.block_mask()
    for g in range(groups):
        wide = widened(plan, input_ref[g * rows : (g + 1) * rows, :], mask)
        wide = dot(unsort, wide, ((0,), (0,))).astype(BF16)
        for s in range(plan.slots):
            sorted_ref[s, g * part : (g + 1) * part, :] = wide[s * part : (s + 1) * part]
    for s in range(plan.slots):
        value = dot(slot_delta_ref[s], sorted_ref[s], ((0,), (0,))).astype(BF16)
        for m in range(value.shape[0] // LANES):
            out_ref[s, place_of(index_ref, m, LANES), :] = value[m * LANES : (m + 1) * LANES]


def combine(plan, groups, returned_ref, chosen_ref, shared_ref, out_ref):
    rows = plan.group * plan.packed
    mask = plan.block_mask()
    total = shared_ref[...]
    for g in range(groups):
        at = slice(g * rows, (g + 1) * rows)
        total = total + dot(chosen_ref[at, :], widened(plan, returned_ref[at, :], mask), ((0,), (0,)))
    out_ref[...] = total.astype(BF16)


def group_sum(block, groups):
    return lax.psum_scatter(block, "dp", scatter_dimension=0, axis_index_groups=groups, tiled=True)


def moved(block, axis, target):
    return lax.ppermute(block, axis, [(i, target(i)) for i in range(lax.axis_size(axis))])


def along_x(distance):
    return lambda i: (i & 4) | ((i + distance) & 3)


def along_z(distance):
    return lambda i: (i & ~6) | ((i + 2 * distance) & 6)


def other_core(i):
    return i ^ 1


def over_tensor(block):
    copies = jnp.broadcast_to(block[None], (lax.axis_size("tensor"),) + block.shape)
    return lax.all_to_all(copies, "tensor", split_axis=0, concat_axis=0, tiled=True)


def body(layer_input, routed_delta, shared_delta, expert_weight, shared_weight, routing, slot_expert):
    tokens, top = routing.shape
    slots, hidden, columns = expert_weight.shape
    shared_hidden = shared_delta.shape[1]
    dp_count = lax.axis_size("dp")
    group = 8
    groups = dp_count // group
    plan = Plan(slots, columns, group)
    wide_rows, packed_rows = dp_count * plan.padded, dp_count * plan.packed
    along_y = [[8 * y + r for y in range(dp_count // 8)] for r in range(8)]
    mine = lax.axis_index("dp")
    my_z, my_core = (mine >> 1) & 3, mine & 1
    my_place = jnp.stack([my_z, my_core])
    own = lax.axis_index("tensor")
    holders = jnp.stack([(own & 4) ^ flip | ((own + step) & 3) for step in (0, -1, 1, 2) for flip in (0, 4)])

    def exchanged(block):
        parts = block.reshape(dp_count, -1, LANES)
        return lax.all_to_all(parts, "dp", split_axis=0, concat_axis=0, tiled=True).reshape(block.shape)

    def to_right(block):
        return moved(block, "tensor", along_x(1))

    def to_left(block):
        return moved(block, "tensor", along_x(-1))

    shared_all = over_tensor(shared_delta).reshape(tokens, shared_hidden)
    send_deltas, place = call(
        functools.partial(select_deltas, plan, groups, top),
        (
            jax.ShapeDtypeStruct((wide_rows, LANES), BF16),
            jax.ShapeDtypeStruct((slot_expert.shape[0], tokens), BF16),
        ),
        routing.reshape(1, tokens * top),
        slot_expert.reshape(-1, 1),
        routed_delta.reshape(tokens * top, LANES),
    )

    send_deltas, own_weight = ready((send_deltas, shared_weight), (shared_all,))
    arrived_deltas = exchanged(send_deltas)
    send_inputs, chosen = call(
        functools.partial(select_inputs, plan, groups),
        (
            jax.ShapeDtypeStruct((packed_rows, LANES), BF16),
            jax.ShapeDtypeStruct((packed_rows, tokens), BF16),
        ),
        place,
        layer_input,
    )
    keep, give = call(
        shared_partial,
        tuple(jax.ShapeDtypeStruct((shared_hidden // 2, columns), F32) for _ in range(2)),
        shared_all,
        layer_input,
        index=(my_place,),
        scratch=[pltpu.VMEM((shared_hidden, columns), F32)],
        after=(place,),
    )
    shared_part = keep + moved(give, "dp", other_core)
    weight_part = [own_weight] + [moved(own_weight, "dp", along_z(distance)) for distance in (1, 2, 3)]
    arrived_deltas, send_inputs, *weight_part = ready(
        (arrived_deltas, send_inputs, *weight_part), (shared_part,)
    )

    partner_deltas = moved(arrived_deltas, "tensor", lambda i: i ^ 4)
    own_left, own_right = to_right(arrived_deltas), to_left(arrived_deltas)
    partner_deltas, send_inputs, own_left = ready((partner_deltas, send_inputs, own_left), (own_right,))
    arrived_inputs = exchanged(send_inputs)
    partner_left, partner_right = to_right(partner_deltas), to_left(partner_deltas)
    deltas = [
        arrived_deltas,
        partner_deltas,
        own_left,
        partner_left,
        own_right,
        partner_right,
        to_right(own_left),
        to_left(partner_right),
    ]
    shared_part = group_sum(shared_part, along_y).reshape(4, BLOCK, columns)
    weight_part = jnp.stack(weight_part)
    weight_part = jnp.stack([weight_part, moved(weight_part, "dp", other_core)], axis=1)
    outgoing, slot_deltas = call(
        functools.partial(project, plan, groups),
        (
            jax.ShapeDtypeStruct((packed_rows, LANES), BF16),
            jax.ShapeDtypeStruct((slots, dp_count * MOST, hidden), BF16),
        ),
        *deltas,
        expert_weight,
        index=(holders,),
        scratch=[
            pltpu.VMEM((slots, dp_count * MOST, columns), BF16),
            pltpu.VMEM(expert_weight.shape, BF16),
        ],
        after=(weight_part,),
    )
    (outgoing,) = ready((outgoing,), (shared_part,))

    returned = exchanged(outgoing)
    expert_gradient = call(
        functools.partial(weight_gradient, plan, groups),
        jax.ShapeDtypeStruct(expert_weight.shape, BF16),
        slot_deltas,
        arrived_inputs,
        index=(holders,),
        scratch=[pltpu.VMEM((slots, dp_count * MOST, columns), BF16)],
    )
    shared_gradient = lax.dynamic_index_in_dim(shared_part, my_z, 0, keepdims=False)
    for distance in (1, 2, 3):
        part = lax.dynamic_index_in_dim(shared_part, (my_z + distance) & 3, 0, keepdims=False)
        shared_gradient = shared_gradient + moved(part, "dp", along_z(distance))
    weight_all = lax.all_gather(
        weight_part.reshape(8 * BLOCK, columns), "dp", axis=0, axis_index_groups=along_y, tiled=True
    )
    shared_term = call(
        shared_rows,
        jax.ShapeDtypeStruct((tokens, columns), F32),
        shared_all,
        weight_all,
        index=(my_place,),
        scratch=[pltpu.VMEM((shared_hidden, columns), BF16)],
        after=(expert_gradient, shared_gradient),
    )
    input_gradient = call(
        functools.partial(combine, plan, groups),
        jax.ShapeDtypeStruct((tokens, columns), BF16),
        returned,
        chosen,
        shared_term,
    )
    return input_gradient, expert_gradient, shared_gradient


def solution(mesh):
    return jax.shard_map(
        body,
        mesh=mesh,
        in_specs=(
            P("dp", "tensor"),
            P("dp", None, "tensor"),
            P(("dp", "tensor"), None),
            P("dp", None, "tensor"),
            P("dp", "tensor"),
            P("dp", None),
            P(),
        ),
        out_specs=(P("dp", "tensor"), P("dp", None, "tensor"), P("dp", "tensor")),
        check_vma=False,
    )
```

time: 569 us -> 221 us (0.39)
  waiting for transfers between devices: 313 us -> 60.4 us
  blocking collectives: 80.5 us -> 0 us
  local copies, waits for them, and re-layouts: 64.2 us -> 15.8 us
  starting transfers between devices: 64.7 us -> 102 us
  Pallas kernels: 0 us -> 22.3 us
  matrix products: 20.6 us -> 0 us
    all_to_all x3 -> x4, waiting for transfers between devices: 131 us -> 0.17 us  [the longest x1 0.16 us: over_tensor(): lax.all_to_all(copies, 'tensor', split_axis=0, concat_axis=0, tiled=True)]
    all_gather x1 -> x0, blocking collectives: 80.5 us -> none  [body(): shared_all = lax.all_gather(shared_delta, 'tensor', axis=0, tiled=True)]
    ppermute x2 -> x15, waiting for transfers between devices: 88.3 us -> 34.8 us  [moved(): lax.ppermute(block, axis, [(i, target(i)) for i in range(lax.axis_size(ax...]
    ppermute x2 -> x15, starting transfers between devices: 6.82 us -> 58.2 us  [moved(): lax.ppermute(block, axis, [(i, target(i)) for i in range(lax.axis_size(ax...]
    all_gather x2 -> x1, waiting for transfers between devices: 44.6 us -> 9.53 us  [body(): lax.all_gather(weight_part.reshape(8 * BLOCK, columns), 'dp', axis=0, axi...]
    reduce_scatter x1, waiting for transfers between devices: 47.6 us -> 14.5 us  [group_sum(): lax.psum_scatter(block, 'dp', scatter_dimension=0, axis_index_groups=grou...]
    reshape x5 -> x2, local copies, waits for them, and re-layouts: 27.9 us -> 0.86 us  [the longest x1 0.76 us: body(): slot_expert.reshape(-1, 1)]
    pallas_call x0 -> x11, Pallas kernels: none -> 22.3 us  [the longest x7 22.3 us: call(): pl.pallas_call(run, out_shape=outs, in_specs=[IN_SMEM] * len(index) + [IN...]
  transfers between devices with their start and end apart: 8 -> 21, of which waited for: 4 -> 11; matrix products, arithmetic and copies ran while one was open for 11% -> 2% of each run, Pallas kernels for 0% -> 8%
where the time goes in v1:
time: 221 us; the launch traced here: 219 us
  starting transfers between devices  102 us (46%)
  waiting for transfers between devices  60.4 us (27%)
  Pallas kernels  22.3 us (10%)
  local copies, waits for them, and re-layouts  15.8 us (7%)
  between operations  14.5 us (7%)
  other arithmetic  3.34 us (2%)
    ppermute x15, starting transfers between devices, moved(): lax.ppermute(block, axis, [(i, target(i)) for i in range(lax.axis_size(ax...  58.2 us
    all_to_all x3, starting transfers between devices, exchanged(): lax.all_to_all(parts, 'dp', split_axis=0, concat_axis=0, tiled=True)  37.5 us
    ppermute x15, waiting for transfers between devices, moved(): lax.ppermute(block, axis, [(i, target(i)) for i in range(lax.axis_size(ax...  34.8 us
    pallas_call x7, Pallas kernels, call(): pl.pallas_call(run, out_shape=outs, in_specs=[IN_SMEM] * len(index) + [IN...  22.3 us
    reduce_scatter x1, waiting for transfers between devices, group_sum(): lax.psum_scatter(block, 'dp', scatter_dimension=0, axis_index_groups=grou...  14.5 us
    unnamed x64, local copies, waits for them, and re-layouts  13.4 us
    all_gather x1, waiting for transfers between devices, body(): lax.all_gather(weight_part.reshape(8 * BLOCK, columns), 'dp', axis=0, axi...  9.53 us
    all_to_all x1, starting transfers between devices, over_tensor(): lax.all_to_all(copies, 'tensor', split_axis=0, concat_axis=0, tiled=True)  6.66 us
  transfers between devices with their start and end apart: 21, of which 11 were waited for; matrix products, arithmetic and copies ran while one was open for 2% of the time, Pallas kernels for 8%

profile of v1, /device:TPU:1, one launch (start us, length us, event | category | flops | bytes accessed | tf_op | source)
XLA Modules:
  0.0 218.8 jit_solution(17748616839182225650)
XLA Ops:
  10.0 6.7 %all-to-all-start = ((bf16[8,16,1024]{2,1,0:T(8,128)(2,1)}), bf16[8,16,1024]{2,1,0:T(8,128)(2,1)S(1)}, u32[]{:S(2)}, u32[]{:S(2)}) async-start(bf16[8,16,1024]{2,1,0:T(8,128)(2,1)} %broadcast_in_dim.2), calls=%async_computation | async-start | bytes 524288 | tf_op jit(solution)/shard_map/all_to_all | solution.py:238
  19.3 2.5 %shard_map.94 = (bf16[1536,128]{1,0:T(8,128)(2,1)S(1)}, bf16[128,128]{1,0:T(8,128)(2,1)S(1)}) custom-call(s32[1,1024]{1,0:T(1,128)S(1)} %reshape.43.refs_0_, s32[128,1]{1,0:T(8,128)S(1)} %copy.26.refs_1_, bf16[1024,128]{1,0:T(8,128)(2,1)S(1)} %bitcast.52), custom_call_target="tpu_custom_call" | custom-call | tf_op jit(solution)/shard_map/pallas_call | solution.py:83
  22.8 2.1 shard_map.97
  24.9 6.6 %collective-permute-start.3 = (f32[512,512]{1,0:T(8,128)}, f32[512,512]{1,0:T(8,128)}, u32[]{:S(2)}, u32[]{:S(2)}) collective-permute-start(f32[512,512]{1,0:T(8,128)} %get-tuple-element.28), channel_id=1, source_target_pairs={{0,8},{8,0},{16,24},{24,16},{32,40},{40,32},{48,56},{56,48},{64,72... | collective-permute-start | bytes 3145736 | tf_op jit(solution)/shard_map/ppermute | solution.py:221
  31.5 12.7 %all-to-all-start.1 = ((bf16[64,24,128]{2,1,0:T(8,128)(2,1)}), bf16[64,24,128]{2,1,0:T(8,128)(2,1)S(1)}, u32[]{:S(2)}, u32[]{:S(2)}) async-start(bf16[64,24,128]{2,1,0:T(8,128)(2,1)} %bitcast.50), calls=%async_computation.1 | async-start | bytes 786432 | tf_op jit(solution)/shard_map/all_to_all | solution.py:259
  44.3 4.2 %collective-permute-start = (bf16[16,512]{1,0:T(8,128)(2,1)}, bf16[16,512]{1,0:T(8,128)(2,1)S(1)}, u32[]{:S(2)}, u32[]{:S(2)}) collective-permute-start(bf16[16,512]{1,0:T(8,128)(2,1)} %get-tuple-element.26.refs_2_), channel_id=1, source_target_pairs={{0,16},{8,24},{16,32},{24,40},{32,48},{40,56},{48,0},{56,8},{64,80... | collective-permute-start | bytes 49160 | tf_op jit(solution)/shard_map/ppermute | solution.py:221
  48.5 5.2 %collective-permute-start.1 = (bf16[16,512]{1,0:T(8,128)(2,1)}, bf16[16,512]{1,0:T(8,128)(2,1)S(1)}, u32[]{:S(2)}, u32[]{:S(2)}) collective-permute-start(bf16[16,512]{1,0:T(8,128)(2,1)} %get-tuple-element.26.refs_2_), channel_id=1, source_target_pairs={{0,32},{8,40},{16,48},{24,56},{32,0},{40,8},{48,16},{56,24},{64,96... | collective-permute-start | bytes 49160 | tf_op jit(solution)/shard_map/ppermute | solution.py:221
  53.7 5.2 %collective-permute-start.2 = (bf16[16,512]{1,0:T(8,128)(2,1)}, bf16[16,512]{1,0:T(8,128)(2,1)S(1)}, u32[]{:S(2)}, u32[]{:S(2)}) collective-permute-start(bf16[16,512]{1,0:T(8,128)(2,1)} %get-tuple-element.26.refs_2_), channel_id=1, source_target_pairs={{0,48},{8,56},{16,0},{24,8},{32,16},{40,24},{48,32},{56,40},{64,11... | collective-permute-start | bytes 49160 | tf_op jit(solution)/shard_map/ppermute | solution.py:221
  58.9 3.2 %shard_map.96 = (bf16[5120,128]{1,0:T(8,128)(2,1)S(1)}, bf16[5120,128]{1,0:T(8,128)(2,1)S(1)}) custom-call(bf16[128,128]{1,0:T(8,128)(2,1)S(1)} %get-tuple-element.24.refs_0_.refs_3_, bf16[128,512]{1,0:T(8,128)(2,1)S(1)} %copy-done.20), custom_call_target="tpu_custom_call" | custom-call | tf_op jit(solution)/shard_map/pallas_call | solution.py:83
  63.2 3.2 %add.51.refs_6_ = f32[512,512]{1,0:T(8,128)} add(f32[512,512]{1,0:T(8,128)} %copy-done.18, f32[512,512]{1,0:T(8,128)} %collective-permute-done.3) | non-fusion elementwise | flops 262144 | bytes 3145728 | tf_op jit(solution)/shard_map/add | solution.py:299
  67.2 3.5 %collective-permute-start.6 = (bf16[1536,128]{1,0:T(8,128)(2,1)}, bf16[1536,128]{1,0:T(8,128)(2,1)S(1)}, u32[]{:S(2)}, u32[]{:S(2)}) collective-permute-start(bf16[1536,128]{1,0:T(8,128)(2,1)} %get-tuple-element.29.refs_1_), channel_id=1, source_target_pairs={{0,3},{1,0},{2,1},{3,2},{4,7},{5,4},{6,5},{7,6},{8,11},{9,8},{10,9... | collective-permute-start | bytes 1179656 | tf_op jit(solution)/shard_map/ppermute | solution.py:221
  70.8 3.1 %collective-permute-start.4 = (bf16[1536,128]{1,0:T(8,128)(2,1)}, bf16[1536,128]{1,0:T(8,128)(2,1)S(1)}, u32[]{:S(2)}, u32[]{:S(2)}) collective-permute-start(bf16[1536,128]{1,0:T(8,128)(2,1)} %get-tuple-element.29.refs_1_), channel_id=1, source_target_pairs={{0,4},{1,5},{2,6},{3,7},{4,0},{5,1},{6,2},{7,3},{8,12},{9,13},{10,... | collective-permute-start | bytes 1179656 | tf_op jit(solution)/shard_map/ppermute | solution.py:221
  75.8 2.9 %collective-permute-done.6.refs_3_.refs_5_ = bf16[1536,128]{1,0:T(8,128)(2,1)S(1)} collective-permute-done((bf16[1536,128]{1,0:T(8,128)(2,1)}, bf16[1536,128]{1,0:T(8,128)(2,1)S(1)}, u32[]{:S(2)}, u32[]{:S(2)}) %collective-permute-start.6) | collective-permute-done | bytes 393248 | tf_op jit(solution)/shard_map/ppermute | solution.py:221
  78.7 3.3 %collective-permute-done.4.refs_0_ = bf16[1536,128]{1,0:T(8,128)(2,1)S(1)} collective-permute-done((bf16[1536,128]{1,0:T(8,128)(2,1)}, bf16[1536,128]{1,0:T(8,128)(2,1)S(1)}, u32[]{:S(2)}, u32[]{:S(2)}) %collective-permute-start.4) | collective-permute-done | bytes 393248 | tf_op jit(solution)/shard_map/ppermute | solution.py:221
  82.0 4.0 %collective-permute-done.5.refs_2_ = bf16[1536,128]{1,0:T(8,128)(2,1)S(1)} collective-permute-done((bf16[1536,128]{1,0:T(8,128)(2,1)}, bf16[1536,128]{1,0:T(8,128)(2,1)S(1)}, u32[]{:S(2)}, u32[]{:S(2)}) %collective-permute-start.5) | collective-permute-done | bytes 393248 | tf_op jit(solution)/shard_map/ppermute | solution.py:221
  86.8 10.1 %all-to-all-start.3 = ((bf16[64,80,128]{2,1,0:T(8,128)(2,1)}), bf16[64,80,128]{2,1,0:T(8,128)(2,1)S(1)}, u32[]{:S(2)}, u32[]{:S(2)}) async-start(bf16[64,80,128]{2,1,0:T(8,128)(2,1)} %bitcast.42), calls=%async_computation.4 | async-start | bytes 2621440 | tf_op jit(solution)/shard_map/all_to_all | solution.py:259
  99.7 3.4 %collective-permute-start.7 = (bf16[1536,128]{1,0:T(8,128)(2,1)S(1)}, bf16[1536,128]{1,0:T(8,128)(2,1)}, u32[]{:S(2)}, u32[]{:S(2)}) collective-permute-start(bf16[1536,128]{1,0:T(8,128)(2,1)S(1)} %copy-done.12), channel_id=1, source_target_pairs={{0,1},{1,2},{2,3},{3,0},{4,5},{5,6},{6,7},{7,4},{8,9},{9,10},{10,1... | collective-permute-start | bytes 1179656 | tf_op jit(solution)/shard_map/ppermute | solution.py:221
  103.1 1.9 collective-permute-start.9
  105.0 5.0 %collective-permute-done.8.refs_6_ = bf16[1536,128]{1,0:T(8,128)(2,1)S(1)} collective-permute-done((bf16[1536,128]{1,0:T(8,128)(2,1)S(1)}, bf16[1536,128]{1,0:T(8,128)(2,1)S(1)}, u32[]{:S(2)}, u32[]{:S(2)}) %collective-permute-start.8) | collective-permute-done | bytes 393248 | tf_op jit(solution)/shard_map/ppermute | solution.py:221
  110.0 3.3 %collective-permute-start.10 = (bf16[1536,128]{1,0:T(8,128)(2,1)S(1)}, bf16[1536,128]{1,0:T(8,128)(2,1)}, u32[]{:S(2)}, u32[]{:S(2)}) collective-permute-start(bf16[1536,128]{1,0:T(8,128)(2,1)S(1)} %collective-permute-done.8.refs_6_), channel_id=1, source_target_pairs={{0,3},{1,0},{2,1},{3,2},{4,7},{5,4},{6,5},{7,6},{8,11},{9,8},{10,9... | collective-permute-start | bytes 1179656 | tf_op jit(solution)/shard_map/ppermute | solution.py:221
  113.4 3.3 %collective-permute-start.11 = (bf16[4,16,512]{2,1,0:T(8,128)(2,1)S(1)}, bf16[4,16,512]{2,1,0:T(8,128)(2,1)S(1)}, u32[]{:S(2)}, u32[]{:S(2)}) collective-permute-start(bf16[4,16,512]{2,1,0:T(8,128)(2,1)S(1)} %get-tuple-element.45), channel_id=1, source_target_pairs={{0,8},{8,0},{16,24},{24,16},{32,40},{40,32},{48,56},{56,48},{64,72... | collective-permute-start | bytes 196616 | tf_op jit(solution)/shard_map/ppermute | solution.py:221
  117.5 4.1 %collective-permute-done.9.refs_7_ = bf16[1536,128]{1,0:T(8,128)(2,1)} collective-permute-done((bf16[1536,128]{1,0:T(8,128)(2,1)S(1)}, bf16[1536,128]{1,0:T(8,128)(2,1)}, u32[]{:S(2)}, u32[]{:S(2)}) %collective-permute-start.9) | collective-permute-done | bytes 393248 | tf_op jit(solution)/shard_map/ppermute | solution.py:221
  121.6 6.1 %shard_map.100 = (bf16[5120,128]{1,0:T(8,128)(2,1)S(1)}, bf16[2,640,1024]{2,1,0:T(8,128)(2,1)}) custom-call(s32[8]{0:T(128)S(1)} %stack.68.refs_0_, bf16[1536,128]{1,0:T(8,128)(2,1)S(1)} %copy-done.6, bf16[1536,128]{1,0:T(8,128)(2,1)S(1)} %copy-done.12, bf16[1536,128]{1,0:T(8,128)(2,1)S(1)} %copy-done.14, bf16[1536,128]{1,0:T(8,128)(2,1)} %collective-permute-done.7.refs_4_, ...), custom_call_target="tpu_custom_call" | custom-call | tf_op jit(solution)/shard_map/pallas_call | solution.py:83
  128.8 14.5 %reduce-scatter.2.cloned.1.call-done = f32[64,512]{1,0:T(8,128)} async-done(((f32[512,512]{1,0:T(8,128)}), f32[64,512]{1,0:T(8,128)}) %reduce-scatter.2.cloned.1.call-update) | async-done | bytes 131088 | tf_op jit(solution)/shard_map/reduce_scatter | solution.py:217
  143.3 14.6 %all-to-all-start.2 = ((bf16[64,80,128]{2,1,0:T(8,128)(2,1)}), bf16[64,80,128]{2,1,0:T(8,128)(2,1)S(1)}, u32[]{:S(2)}, u32[]{:S(2)}) async-start(bf16[64,80,128]{2,1,0:T(8,128)(2,1)} %bitcast.44), calls=%async_computation.3 | async-start | bytes 2621440 | tf_op jit(solution)/shard_map/all_to_all | solution.py:259
  158.7 4.2 %collective-permute-start.12 = (f32[16,512]{1,0:T(8,128)S(1)}, f32[16,512]{1,0:T(8,128)S(1)}, u32[]{:S(2)}, u32[]{:S(2)}) collective-permute-start(f32[16,512]{1,0:T(8,128)S(1)} %get-tuple-element.41), channel_id=1, source_target_pairs={{0,16},{8,24},{16,32},{24,40},{32,48},{40,56},{48,0},{56,8},{64,80... | collective-permute-start | bytes 98312 | tf_op jit(solution)/shard_map/ppermute | solution.py:221
  162.9 5.2 %collective-permute-start.13 = (f32[16,512]{1,0:T(8,128)S(1)}, f32[16,512]{1,0:T(8,128)S(1)}, u32[]{:S(2)}, u32[]{:S(2)}) collective-permute-start(f32[16,512]{1,0:T(8,128)S(1)} %get-tuple-element.43), channel_id=1, source_target_pairs={{0,32},{8,40},{16,48},{24,56},{32,0},{40,8},{48,16},{56,24},{64,96... | collective-permute-start | bytes 98312 | tf_op jit(solution)/shard_map/ppermute | solution.py:221
  168.1 5.2 %collective-permute-start.14 = (f32[16,512]{1,0:T(8,128)S(1)}, f32[16,512]{1,0:T(8,128)S(1)}, u32[]{:S(2)}, u32[]{:S(2)}) collective-permute-start(f32[16,512]{1,0:T(8,128)S(1)} %get-tuple-element.42), channel_id=1, source_target_pairs={{0,48},{8,56},{16,0},{24,8},{32,16},{40,24},{48,32},{56,40},{64,11... | collective-permute-start | bytes 98312 | tf_op jit(solution)/shard_map/ppermute | solution.py:221
  174.4 13.8 %collective-permute-done.13 = f32[16,512]{1,0:T(8,128)S(1)} collective-permute-done((f32[16,512]{1,0:T(8,128)S(1)}, f32[16,512]{1,0:T(8,128)S(1)}, u32[]{:S(2)}, u32[]{:S(2)}) %collective-permute-start.13) | collective-permute-done | bytes 32800 | tf_op jit(solution)/shard_map/ppermute | solution.py:221
  190.0 5.4 %shard_map.102.refs_3_ = bf16[2,1024,512]{2,1,0:T(8,128)(2,1)} custom-call(s32[8]{0:T(128)S(1)} %stack.68.refs_0_, bf16[2,640,1024]{2,1,0:T(8,128)(2,1)S(1)} %copy-done.7, bf16[5120,128]{1,0:T(8,128)(2,1)S(1)} %bitcast.45), custom_call_target="tpu_custom_call" | custom-call | tf_op jit(solution)/shard_map/pallas_call | solution.py:83
  195.5 9.5 %all-gather.2.cloned.1.call-done.refs_2_ = bf16[1024,512]{1,0:T(8,128)(2,1)} async-done(((bf16[128,512]{1,0:T(8,128)(2,1)}), bf16[1024,512]{1,0:T(8,128)(2,1)}) %all-gather.2.cloned.1.call-update) | async-done | bytes 1048592 | tf_op jit(solution)/shard_map/all_gather | solution.py:353
  210.0 2.0 shard_map.104
  (97 shorter events, 24.0 us)
Async XLA Ops:
  7.2 15.6 %copy-start.20 = (bf16[128,512]{1,0:T(8,128)(2,1)S(1)}, bf16[128,512]{1,0:T(8,128)(2,1)}, u32[]{:S(2)}) copy-start(bf16[128,512]{1,0:T(8,128)(2,1)} %refs_2_.1) | copy-start | bytes 393220
  10.0 12.7 %all-to-all-start = ((bf16[8,16,1024]{2,1,0:T(8,128)(2,1)}), bf16[8,16,1024]{2,1,0:T(8,128)(2,1)S(1)}, u32[]{:S(2)}, u32[]{:S(2)}) async-start(bf16[8,16,1024]{2,1,0:T(8,128)(2,1)} %broadcast_in_dim.2), calls=%async_computation | async-start | bytes 524288 | tf_op jit(solution)/shard_map/all_to_all | solution.py:238
  24.9 28.8 %copy-start.18 = (f32[512,512]{1,0:T(8,128)}, f32[512,512]{1,0:T(8,128)S(1)}, u32[]{:S(2)}) copy-start(f32[512,512]{1,0:T(8,128)S(1)} %get-tuple-element.27) | copy-start | bytes 3145732
  24.9 38.3 %collective-permute-start.3 = (f32[512,512]{1,0:T(8,128)}, f32[512,512]{1,0:T(8,128)}, u32[]{:S(2)}, u32[]{:S(2)}) collective-permute-start(f32[512,512]{1,0:T(8,128)} %get-tuple-element.28), channel_id=1, source_target_pairs={{0,8},{8,0},{16,24},{24,16},{32,40},{40,32},{48,56},{56,48},{64,72... | collective-permute-start | bytes 3145736 | tf_op jit(solution)/shard_map/ppermute | solution.py:221
  31.5 34.9 %all-to-all-start.1 = ((bf16[64,24,128]{2,1,0:T(8,128)(2,1)}), bf16[64,24,128]{2,1,0:T(8,128)(2,1)S(1)}, u32[]{:S(2)}, u32[]{:S(2)}) async-start(bf16[64,24,128]{2,1,0:T(8,128)(2,1)} %bitcast.50), calls=%async_computation.1 | async-start | bytes 786432 | tf_op jit(solution)/shard_map/all_to_all | solution.py:259
  44.3 22.1 %collective-permute-start = (bf16[16,512]{1,0:T(8,128)(2,1)}, bf16[16,512]{1,0:T(8,128)(2,1)S(1)}, u32[]{:S(2)}, u32[]{:S(2)}) collective-permute-start(bf16[16,512]{1,0:T(8,128)(2,1)} %get-tuple-element.26.refs_2_), channel_id=1, source_target_pairs={{0,16},{8,24},{16,32},{24,40},{32,48},{40,56},{48,0},{56,8},{64,80... | collective-permute-start | bytes 49160 | tf_op jit(solution)/shard_map/ppermute | solution.py:221
  48.5 17.9 %collective-permute-start.1 = (bf16[16,512]{1,0:T(8,128)(2,1)}, bf16[16,512]{1,0:T(8,128)(2,1)S(1)}, u32[]{:S(2)}, u32[]{:S(2)}) collective-permute-start(bf16[16,512]{1,0:T(8,128)(2,1)} %get-tuple-element.26.refs_2_), channel_id=1, source_target_pairs={{0,32},{8,40},{16,48},{24,56},{32,0},{40,8},{48,16},{56,24},{64,96... | collective-permute-start | bytes 49160 | tf_op jit(solution)/shard_map/ppermute | solution.py:221
  53.7 12.7 %collective-permute-start.2 = (bf16[16,512]{1,0:T(8,128)(2,1)}, bf16[16,512]{1,0:T(8,128)(2,1)S(1)}, u32[]{:S(2)}, u32[]{:S(2)}) collective-permute-start(bf16[16,512]{1,0:T(8,128)(2,1)} %get-tuple-element.26.refs_2_), channel_id=1, source_target_pairs={{0,48},{8,56},{16,0},{24,8},{32,16},{40,24},{48,32},{56,40},{64,11... | collective-permute-start | bytes 49160 | tf_op jit(solution)/shard_map/ppermute | solution.py:221
  67.2 11.5 %collective-permute-start.6 = (bf16[1536,128]{1,0:T(8,128)(2,1)}, bf16[1536,128]{1,0:T(8,128)(2,1)S(1)}, u32[]{:S(2)}, u32[]{:S(2)}) collective-permute-start(bf16[1536,128]{1,0:T(8,128)(2,1)} %get-tuple-element.29.refs_1_), channel_id=1, source_target_pairs={{0,3},{1,0},{2,1},{3,2},{4,7},{5,4},{6,5},{7,6},{8,11},{9,8},{10,9... | collective-permute-start | bytes 1179656 | tf_op jit(solution)/shard_map/ppermute | solution.py:221
  70.8 11.2 %collective-permute-start.4 = (bf16[1536,128]{1,0:T(8,128)(2,1)}, bf16[1536,128]{1,0:T(8,128)(2,1)S(1)}, u32[]{:S(2)}, u32[]{:S(2)}) collective-permute-start(bf16[1536,128]{1,0:T(8,128)(2,1)} %get-tuple-element.29.refs_1_), channel_id=1, source_target_pairs={{0,4},{1,5},{2,6},{3,7},{4,0},{5,1},{6,2},{7,3},{8,12},{9,13},{10,... | collective-permute-start | bytes 1179656 | tf_op jit(solution)/shard_map/ppermute | solution.py:221
  73.9 12.2 %collective-permute-start.5 = (bf16[1536,128]{1,0:T(8,128)(2,1)}, bf16[1536,128]{1,0:T(8,128)(2,1)S(1)}, u32[]{:S(2)}, u32[]{:S(2)}) collective-permute-start(bf16[1536,128]{1,0:T(8,128)(2,1)} %get-tuple-element.29.refs_1_), channel_id=1, source_target_pairs={{0,1},{1,2},{2,3},{3,0},{4,5},{5,6},{6,7},{7,4},{8,9},{9,10},{10,1... | collective-permute-start | bytes 1179656 | tf_op jit(solution)/shard_map/ppermute | solution.py:221
  86.8 16.2 %copy-start.14 = (bf16[1536,128]{1,0:T(8,128)(2,1)S(1)}, bf16[1536,128]{1,0:T(8,128)(2,1)}, u32[]{:S(2)}) copy-start(bf16[1536,128]{1,0:T(8,128)(2,1)} %get-tuple-element.32.refs_3_) | copy-start | bytes 1179652
  86.8 26.5 %copy-start.24 = (bf16[16,512]{1,0:T(8,128)(2,1)S(1)}, bf16[16,512]{1,0:T(8,128)(2,1)}, u32[]{:S(2)}) copy-start(bf16[16,512]{1,0:T(8,128)(2,1)} %get-tuple-element.33) | copy-start | bytes 49156
  86.8 26.5 %copy-start.26 = (bf16[16,512]{1,0:T(8,128)(2,1)S(1)}, bf16[16,512]{1,0:T(8,128)(2,1)}, u32[]{:S(2)}) copy-start(bf16[16,512]{1,0:T(8,128)(2,1)} %get-tuple-element.34) | copy-start | bytes 49156
  86.8 26.5 %copy-start.28 = (bf16[16,512]{1,0:T(8,128)(2,1)S(1)}, bf16[16,512]{1,0:T(8,128)(2,1)}, u32[]{:S(2)}) copy-start(bf16[16,512]{1,0:T(8,128)(2,1)} %get-tuple-element.35) | copy-start | bytes 49156
  86.8 26.5 %copy-start.30 = (bf16[16,512]{1,0:T(8,128)(2,1)S(1)}, bf16[16,512]{1,0:T(8,128)(2,1)}, u32[]{:S(2)}) copy-start(bf16[16,512]{1,0:T(8,128)(2,1)} %get-tuple-element.36) | copy-start | bytes 49156
  86.8 56.4 %all-to-all-start.3 = ((bf16[64,80,128]{2,1,0:T(8,128)(2,1)}), bf16[64,80,128]{2,1,0:T(8,128)(2,1)S(1)}, u32[]{:S(2)}, u32[]{:S(2)}) async-start(bf16[64,80,128]{2,1,0:T(8,128)(2,1)} %bitcast.42), calls=%async_computation.4 | async-start | bytes 2621440 | tf_op jit(solution)/shard_map/all_to_all | solution.py:259
  97.0 24.6 %copy-start.6 = (bf16[1536,128]{1,0:T(8,128)(2,1)S(1)}, bf16[1536,128]{1,0:T(8,128)(2,1)}, u32[]{:S(2)}) copy-start(bf16[1536,128]{1,0:T(8,128)(2,1)} %get-tuple-element.29.refs_1_) | copy-start | bytes 1179652
  97.0 24.6 %copy-start.10 = (bf16[1536,128]{1,0:T(8,128)(2,1)S(1)}, bf16[1536,128]{1,0:T(8,128)(2,1)}, u32[]{:S(2)}) copy-start(bf16[1536,128]{1,0:T(8,128)(2,1)} %copy-done.9) | copy-start | bytes 1179652
  97.0 46.2 %reduce-scatter.2.cloned.1.call-start = ((), (), s32[]{:S(2)}) async-start(), calls=%async_computation.5 | async-start | bytes 1179648 | tf_op jit(solution)/shard_map/reduce_scatter | solution.py:217
  97.7 12.2 %collective-permute-start.8 = (bf16[1536,128]{1,0:T(8,128)(2,1)S(1)}, bf16[1536,128]{1,0:T(8,128)(2,1)S(1)}, u32[]{:S(2)}, u32[]{:S(2)}) collective-permute-start(bf16[1536,128]{1,0:T(8,128)(2,1)S(1)} %copy-done.12), channel_id=1, source_target_pairs={{0,3},{1,0},{2,1},{3,2},{4,7},{5,4},{6,5},{7,6},{8,11},{9,8},{10,9... | collective-permute-start | bytes 1179656 | tf_op jit(solution)/shard_map/ppermute | solution.py:221
  99.7 17.8 %collective-permute-start.7 = (bf16[1536,128]{1,0:T(8,128)(2,1)S(1)}, bf16[1536,128]{1,0:T(8,128)(2,1)}, u32[]{:S(2)}, u32[]{:S(2)}) collective-permute-start(bf16[1536,128]{1,0:T(8,128)(2,1)S(1)} %copy-done.12), channel_id=1, source_target_pairs={{0,1},{1,2},{2,3},{3,0},{4,5},{5,6},{6,7},{7,4},{8,9},{9,10},{10,1... | collective-permute-start | bytes 1179656 | tf_op jit(solution)/shard_map/ppermute | solution.py:221
  103.1 18.5 %collective-permute-start.9 = (bf16[1536,128]{1,0:T(8,128)(2,1)S(1)}, bf16[1536,128]{1,0:T(8,128)(2,1)}, u32[]{:S(2)}, u32[]{:S(2)}) collective-permute-start(bf16[1536,128]{1,0:T(8,128)(2,1)S(1)} %copy-done.14), channel_id=1, source_target_pairs={{0,1},{1,2},{2,3},{3,0},{4,5},{5,6},{6,7},{7,4},{8,9},{9,10},{10,1... | collective-permute-start | bytes 1179656 | tf_op jit(solution)/shard_map/ppermute | solution.py:221
  110.0 11.6 %collective-permute-start.10 = (bf16[1536,128]{1,0:T(8,128)(2,1)S(1)}, bf16[1536,128]{1,0:T(8,128)(2,1)}, u32[]{:S(2)}, u32[]{:S(2)}) collective-permute-start(bf16[1536,128]{1,0:T(8,128)(2,1)S(1)} %collective-permute-done.8.refs_6_), channel_id=1, source_target_pairs={{0,3},{1,0},{2,1},{3,2},{4,7},{5,4},{6,5},{7,6},{8,11},{9,8},{10,9... | collective-permute-start | bytes 1179656 | tf_op jit(solution)/shard_map/ppermute | solution.py:221
  113.4 4.1 %collective-permute-start.11 = (bf16[4,16,512]{2,1,0:T(8,128)(2,1)S(1)}, bf16[4,16,512]{2,1,0:T(8,128)(2,1)S(1)}, u32[]{:S(2)}, u32[]{:S(2)}) collective-permute-start(bf16[4,16,512]{2,1,0:T(8,128)(2,1)S(1)} %get-tuple-element.45), channel_id=1, source_target_pairs={{0,8},{8,0},{16,24},{24,16},{32,40},{40,32},{48,56},{56,48},{64,72... | collective-permute-start | bytes 196616 | tf_op jit(solution)/shard_map/ppermute | solution.py:221
  143.3 15.4 %copy-start.23 = (f32[64,512]{1,0:T(8,128)S(1)}, f32[64,512]{1,0:T(8,128)}, u32[]{:S(2)}) copy-start(f32[64,512]{1,0:T(8,128)} %reduce-scatter.2.cloned.1.call-done) | copy-start | bytes 393220
  143.3 65.4 %all-to-all-start.2 = ((bf16[64,80,128]{2,1,0:T(8,128)(2,1)}), bf16[64,80,128]{2,1,0:T(8,128)(2,1)S(1)}, u32[]{:S(2)}, u32[]{:S(2)}) async-start(bf16[64,80,128]{2,1,0:T(8,128)(2,1)} %bitcast.44), calls=%async_computation.3 | async-start | bytes 2621440 | tf_op jit(solution)/shard_map/all_to_all | solution.py:259
  157.9 47.1 %all-gather.2.cloned.1.call-start = ((), (), s32[]{:S(2)}) async-start(), calls=%async_computation.6 | async-start | bytes 1179648 | tf_op jit(solution)/shard_map/all_gather | solution.py:353
  158.7 15.7 %collective-permute-start.12 = (f32[16,512]{1,0:T(8,128)S(1)}, f32[16,512]{1,0:T(8,128)S(1)}, u32[]{:S(2)}, u32[]{:S(2)}) collective-permute-start(f32[16,512]{1,0:T(8,128)S(1)} %get-tuple-element.41), channel_id=1, source_target_pairs={{0,16},{8,24},{16,32},{24,40},{32,48},{40,56},{48,0},{56,8},{64,80... | collective-permute-start | bytes 98312 | tf_op jit(solution)/shard_map/ppermute | solution.py:221
  162.9 25.3 %collective-permute-start.13 = (f32[16,512]{1,0:T(8,128)S(1)}, f32[16,512]{1,0:T(8,128)S(1)}, u32[]{:S(2)}, u32[]{:S(2)}) collective-permute-start(f32[16,512]{1,0:T(8,128)S(1)} %get-tuple-element.43), channel_id=1, source_target_pairs={{0,32},{8,40},{16,48},{24,56},{32,0},{40,8},{48,16},{56,24},{64,96... | collective-permute-start | bytes 98312 | tf_op jit(solution)/shard_map/ppermute | solution.py:221
  168.1 20.1 %collective-permute-start.14 = (f32[16,512]{1,0:T(8,128)S(1)}, f32[16,512]{1,0:T(8,128)S(1)}, u32[]{:S(2)}, u32[]{:S(2)}) collective-permute-start(f32[16,512]{1,0:T(8,128)S(1)} %get-tuple-element.42), channel_id=1, source_target_pairs={{0,48},{8,56},{16,0},{24,8},{32,16},{40,24},{48,32},{56,40},{64,11... | collective-permute-start | bytes 98312 | tf_op jit(solution)/shard_map/ppermute | solution.py:221
  188.2 16.7 %copy-start.22 = (f32[16,512]{1,0:T(8,128)}, f32[16,512]{1,0:T(8,128)S(1)}, u32[]{:S(2)}) copy-start(f32[16,512]{1,0:T(8,128)S(1)} %fusion.1.refs_4_) | copy-start | bytes 98308
  (20 other events, 72.6 us)
Sparse Core Ops, SparseCore 0:
  100.7 42.5 reduce-scatter.1
  161.4 43.5 all-gather.1

commit v2 on v1

v2 whole, which is shorter than its diff:
```python
import functools

import jax
import jax.numpy as jnp
from jax import lax
from jax.experimental import pallas as pl
from jax.experimental.pallas import tpu as pltpu
from jax.sharding import PartitionSpec as P

MOST = 10
LANES = 128
BLOCK = 16
BF16 = jnp.bfloat16
F32 = jnp.float32
VMEM_LIMIT = 48 * 1024 * 1024


def dot(a, b, contract=((1,), (0,))):
    return lax.dot_general(a, b, (contract, ((), ())), preferred_element_type=F32)


class Plan:
    def __init__(self, slots, columns, group):
        self.slots, self.columns, self.group = slots, columns, group
        self.rows = slots * MOST
        self.padded = -(-self.rows // 8) * 8
        self.blocks = columns // LANES
        self.packed = self.blocks * self.rows
        self.slot_rows = group * MOST

    def wide_index(self, width):
        at = lax.broadcasted_iota(jnp.int32, (self.group * self.padded, width), 0)
        dest = at // self.padded
        return dest, at - dest * self.padded

    def packed_index(self, width):
        at = lax.broadcasted_iota(jnp.int32, (self.group * self.packed, width), 0)
        dest = at // self.packed
        at = at - dest * self.packed
        block = at // self.rows
        return dest, block, at - block * self.rows

    def expand(self, dest, at):
        slot = lax.broadcasted_iota(jnp.int32, dest.shape, 1)
        return one_hot(slot == jnp.where(at < self.rows, dest * self.slots + at // MOST, -1))

    def rank(self, at):
        return jnp.where(at < self.rows, at % MOST, -5).astype(F32)

    def slot_from_wide(self):
        shape = (self.slots * self.slot_rows, self.group * self.padded)
        at = lax.broadcasted_iota(jnp.int32, shape, 0)
        slot = at // self.slot_rows
        at = at - slot * self.slot_rows
        source = (at // MOST) * self.padded + slot * MOST + at % MOST
        return one_hot(lax.broadcasted_iota(jnp.int32, shape, 1) == source)

    def packed_from_slot(self):
        dest, _, at = self.packed_index(self.slots * self.slot_rows)
        source = (at // MOST) * self.slot_rows + dest * MOST + at % MOST
        return one_hot(lax.broadcasted_iota(jnp.int32, dest.shape, 1) == source)

    def block_mask(self):
        _, block, _ = self.packed_index(self.columns)
        return one_hot(lax.broadcasted_iota(jnp.int32, block.shape, 1) // LANES == block)


def one_hot(hit):
    return jnp.where(hit, 1.0, 0.0).astype(BF16)


ANYWHERE = pl.BlockSpec(memory_space=pl.ANY)
IN_VMEM = pl.BlockSpec(memory_space=pltpu.VMEM)
IN_SMEM = pl.BlockSpec(memory_space=pltpu.SMEM)


def call(kernel, outs, *args, index=(), scratch=(), after=(), out_specs=None):
    given = len(index) + len(args)

    def run(*refs):
        kernel(*refs[:given], *refs[given + len(after) :])

    return pl.pallas_call(
        run,
        out_shape=outs,
        in_specs=[IN_SMEM] * len(index) + [IN_VMEM] * len(args) + [ANYWHERE] * len(after),
        out_specs=jax.tree.map(lambda _: IN_VMEM, outs) if out_specs is None else out_specs,
        scratch_shapes=list(scratch),
        compiler_params=pltpu.CompilerParams(vmem_limit_bytes=VMEM_LIMIT),
    )(*index, *args, *after)


def ready(*values):
    return pl.pallas_call(
        lambda *refs: None,
        out_shape=tuple(jax.ShapeDtypeStruct(v.shape, v.dtype) for v in values),
        in_specs=[ANYWHERE] * len(values),
        out_specs=tuple(ANYWHERE for _ in values),
        input_output_aliases={i: i for i in range(len(values))},
    )(*values)


def by_block(plan, wide, block):
    total = wide[:, :LANES]
    for c in range(1, plan.blocks):
        total = jnp.where(block == c, wide[:, c * LANES : (c + 1) * LANES], total)
    return total.astype(BF16)


def widened(plan, packed, mask):
    return jnp.concatenate([packed] * plan.blocks, axis=1) * mask


def places(route_ref, slot_ref):
    top, tokens = route_ref.shape
    flat = tokens * top
    spread = lax.broadcasted_iota(jnp.int32, (tokens, flat), 0) == lax.broadcasted_iota(jnp.int32, (tokens, flat), 1) // top
    tiled = one_hot(
        lax.broadcasted_iota(jnp.int32, (top, flat), 0) == lax.broadcasted_iota(jnp.int32, (top, flat), 1) % top
    )
    routes = dot(route_ref[...].astype(F32).astype(BF16), tiled, ((0,), (0,)))
    route_row = jnp.sum(jnp.where(spread, routes, 0.0), axis=0, keepdims=True)
    spread = one_hot(spread)
    shape = (slot_ref.shape[1], slot_ref.shape[1])
    same = lax.broadcasted_iota(jnp.int32, shape, 0) == lax.broadcasted_iota(jnp.int32, shape, 1)
    slot_column = jnp.sum(jnp.where(same, slot_ref[...].astype(F32), 0.0), axis=1, keepdims=True)
    hit = slot_column == route_row
    member = dot(one_hot(hit), spread, ((1,), (1,)))
    before = one_hot(
        lax.broadcasted_iota(jnp.int32, (tokens, tokens), 0) < lax.broadcasted_iota(jnp.int32, (tokens, tokens), 1)
    )
    ahead = dot(member.astype(BF16), before)
    place = jnp.where(member > 0.5, ahead, -1.0).astype(BF16)
    place_flat = jnp.where(hit, dot(ahead.astype(BF16), spread), -1.0).astype(BF16)
    return place, place_flat


def prepare(
    plan, groups,
    route_ref, slot_ref, delta_ref, input_ref, shared_ref,
    out_ref, shared_out_ref,
):
    shared_out_ref[...] = shared_ref[...]
    place, place_flat = places(route_ref, slot_ref)
    slots, rows, dests = plan.group * plan.slots, plan.group * plan.packed, plan.group
    wide_expand = plan.expand(*plan.wide_index(slots))
    wide_rank = plan.rank(plan.wide_index(1)[1])
    dest, _, at = plan.packed_index(slots)
    packed_expand = plan.expand(dest, at)
    _, block, at = plan.packed_index(LANES)
    packed_rank = plan.rank(at)
    for g in range(groups):
        value = dot(packed_expand, place[g * slots : (g + 1) * slots])
        chosen = one_hot(value == packed_rank)
        picked = by_block(plan, dot(chosen, input_ref[...]), block)
        out_ref[g * dests : (g + 1) * dests, : plan.packed, :] = picked.reshape(dests, plan.packed, LANES)
        value = dot(wide_expand, place_flat[g * slots : (g + 1) * slots])
        picked = dot(one_hot(value == wide_rank), delta_ref[...]).astype(BF16)
        out_ref[g * dests : (g + 1) * dests, plan.packed :, :] = picked.reshape(dests, plan.padded, LANES)


def place_at(block, size):
    return pl.ds(pl.multiple_of(block * size, size), size)


def place_of(index_ref, block, size):
    return place_at(index_ref[block], size)


def shared_partial(place_ref, holder_ref, *refs):
    part_refs, (input_ref, weight_ref, all_ref, keep_ref, give_ref, weight_out_ref, sum_ref) = refs[:-7], refs[-7:]
    weight_out_ref[...] = weight_ref[...]
    for m, ref in enumerate(part_refs):
        all_ref[place_of(holder_ref, m, BLOCK), :] = ref[...]
    sum_ref[...] = dot(all_ref[...], input_ref[...], ((0,), (0,)))
    core = place_ref[1]
    for b in range(sum_ref.shape[0] // (2 * BLOCK)):
        at = slice(b * BLOCK, (b + 1) * BLOCK)
        keep_ref[at, :] = sum_ref[place_at(2 * b + core, BLOCK), :]
        give_ref[at, :] = sum_ref[place_at(2 * b + 1 - core, BLOCK), :]


def join_along_y(place_ref, part_ref, weight_ref, *refs):
    out_refs, sum_ref = refs[:-1], refs[-1]
    rows = sum_ref.shape[0]
    total = part_ref[0, :rows, :].astype(F32)
    for y in range(1, part_ref.shape[0]):
        total = total + part_ref[y, :rows, :].astype(F32)
    sum_ref[...] = total
    for y in range(part_ref.shape[0]):
        weight_ref[y * rows : (y + 1) * rows, :] = part_ref[y, rows:, :]
    for step, ref in enumerate(out_refs):
        ref[...] = sum_ref[place_at((place_ref[0] + step) & 3, BLOCK), :]


def shared_rows(plan, groups, place_ref, delta_ref, weight_ref, route_ref, slot_ref, out_ref, chosen_ref, sorted_ref):
    place = places(route_ref, slot_ref)[0]
    slots, rows = plan.group * plan.slots, plan.group * plan.packed
    dest, _, at = plan.packed_index(slots)
    expand, rank = plan.expand(dest, at), plan.rank(plan.packed_index(LANES)[2])
    for g in range(groups):
        value = dot(expand, place[g * slots : (g + 1) * slots])
        chosen_ref[g * rows : (g + 1) * rows, :] = one_hot(value == rank)
    for k in range(weight_ref.shape[0] // BLOCK):
        core, z = place_ref[1] ^ (k % 2), (place_ref[0] - (k // 2) % 4) & 3
        sorted_ref[k * BLOCK : (k + 1) * BLOCK, :] = weight_ref[place_at((core * 8 + k // 8) * 4 + z, BLOCK), :]
    out_ref[...] = dot(delta_ref[...], sorted_ref[...])


def arrange(plan, groups, arrived_ref, keep_ref, got_ref, *refs):
    weight_refs, (delta_ref, part_ref) = refs[:-2], refs[-2:]
    sort = plan.slot_from_wide()
    part = plan.slot_rows
    for g in range(groups):
        wide = arrived_ref[g * plan.group : (g + 1) * plan.group, plan.packed :, :]
        wide = dot(sort, wide.reshape(plan.group * plan.padded, LANES)).astype(BF16)
        for s in range(plan.slots):
            delta_ref[s, g * part : (g + 1) * part, :] = wide[s * part : (s + 1) * part]
    count = part_ref.shape[0]
    rows = keep_ref.shape[0] // count
    for y in range(count):
        at = slice(y * rows, (y + 1) * rows)
        part_ref[y, :rows, :] = (keep_ref[at, :] + got_ref[at, :]).astype(BF16)
        for step, ref in enumerate(weight_refs):
            part_ref[y, rows + step * BLOCK : rows + (step + 1) * BLOCK, :] = ref[...]


def project(plan, groups, index_ref, *refs):
    delta_refs, (weight_ref, out_ref, kept_at, value_ref, sorted_ref, sems) = refs[:-6], refs[-6:]
    copies = [pltpu.make_async_copy(ref, kept_at.at[m], sems.at[m]) for m, ref in enumerate(delta_refs)]
    for copy in copies:
        copy.start()
    rows, part = plan.group * plan.packed, plan.slot_rows
    for s in range(plan.slots):
        for m in range(len(delta_refs)):
            sorted_ref[s, m * LANES : (m + 1) * LANES, :] = weight_ref[s, place_of(index_ref, m, LANES), :]
        delta = jnp.concatenate([ref[s] for ref in delta_refs], axis=1)
        value_ref[s] = dot(delta, sorted_ref[s]).astype(BF16)
    unsort = plan.packed_from_slot()
    block = plan.packed_index(LANES)[1]
    for g in range(groups):
        value = jnp.concatenate([value_ref[s, g * part : (g + 1) * part, :] for s in range(plan.slots)], axis=0)
        out_ref[g * rows : (g + 1) * rows, :] = by_block(plan, dot(unsort, value), block)
    for copy in copies:
        copy.wait()


def weight_gradient(plan, groups, index_ref, delta_ref, input_ref, out_ref, sorted_ref):
    rows, part = plan.group * plan.packed, plan.slot_rows
    unsort = plan.packed_from_slot()
    mask = plan.block_mask()
    for g in range(groups):
        packed = input_ref[g * plan.group : (g + 1) * plan.group, : plan.packed, :].reshape(rows, LANES)
        wide = dot(unsort, widened(plan, packed, mask), ((0,), (0,))).astype(BF16)
        for s in range(plan.slots):
            sorted_ref[s, g * part : (g + 1) * part, :] = wide[s * part : (s + 1) * part]
    for s in range(plan.slots):
        delta = jnp.concatenate([delta_ref[m, s] for m in range(delta_ref.shape[0])], axis=1)
        value = dot(delta, sorted_ref[s], ((0,), (0,))).astype(BF16)
        for m in range(delta_ref.shape[0]):
            out_ref[s, place_of(index_ref, m, LANES), :] = value[m * LANES : (m + 1) * LANES]


def combine(plan, groups, returned_ref, chosen_ref, shared_ref, *refs):
    part_refs, (out_ref, sum_ref) = refs[:4], refs[4:]
    rows = plan.group * plan.packed
    mask = plan.block_mask()
    total = shared_ref[...]
    for g in range(groups):
        at = slice(g * rows, (g + 1) * rows)
        total = total + dot(chosen_ref[at, :], widened(plan, returned_ref[at, :], mask), ((0,), (0,)))
    out_ref[...] = total.astype(BF16)
    sum_ref[...] = part_refs[0][...] + part_refs[1][...] + part_refs[2][...] + part_refs[3][...]


def moved(block, axis, target):
    return lax.ppermute(block, axis, [(i, target(i)) for i in range(lax.axis_size(axis))])


def along_x(distance):
    return lambda i: (i & 4) | ((i + distance) & 3)


def other_z(i):
    return i ^ 4


def along_z(distance):
    return lambda i: (i & ~6) | ((i + 2 * distance) & 6)


def other_core(i):
    return i ^ 1


def to_right(block):
    return moved(block, "tensor", along_x(1))


def to_left(block):
    return moved(block, "tensor", along_x(-1))


def body(layer_input, routed_delta, shared_delta, expert_weight, shared_weight, routing, slot_expert):
    tokens, top = routing.shape
    slots, hidden, columns = expert_weight.shape
    shared_hidden = shared_delta.shape[1]
    dp_count = lax.axis_size("dp")
    group = 8
    groups = dp_count // group
    plan = Plan(slots, columns, group)
    packed_rows = dp_count * plan.packed
    mine = lax.axis_index("dp")
    my_place = jnp.stack([(mine >> 1) & 3, mine & 1])
    along_y = [[8 * y + r for y in range(dp_count // 8)] for r in range(8)]
    own = lax.axis_index("tensor")
    holders = jnp.stack([(own & 4) ^ flip | ((own + step) & 3) for step in (0, -1, 1, 2) for flip in (0, 4)])
    value_rows = pltpu.VMEM((slots, dp_count * MOST, columns), BF16)

    def exchanged(block, groups=None):
        return lax.all_to_all(block, "dp", split_axis=0, concat_axis=0, axis_index_groups=groups, tiled=True)

    sent, own_delta = call(
        functools.partial(prepare, plan, groups),
        (
            jax.ShapeDtypeStruct((dp_count, plan.packed + plan.padded, LANES), BF16),
            jax.ShapeDtypeStruct(shared_delta.shape, BF16),
        ),
        routing.T,
        slot_expert.reshape(1, -1),
        routed_delta.reshape(tokens * top, LANES),
        layer_input,
        shared_delta,
    )
    sent, other_delta = ready(sent, moved(shared_delta, "tensor", other_z))
    arrived = exchanged(sent)

    pair = (own_delta, other_delta)
    shared_all, keep, give, own_weight = call(
        shared_partial,
        (
            jax.ShapeDtypeStruct((tokens, shared_hidden), BF16),
            jax.ShapeDtypeStruct((shared_hidden // 2, columns), F32),
            jax.ShapeDtypeStruct((shared_hidden // 2, columns), F32),
            jax.ShapeDtypeStruct(shared_weight.shape, BF16),
        ),
        *pair,
        *[to_right(part) for part in pair],
        *[to_left(part) for part in pair],
        *[moved(part, "tensor", along_x(2)) for part in pair],
        layer_input,
        shared_weight,
        index=(my_place, holders),
        scratch=[pltpu.VMEM((shared_hidden, columns), F32)],
    )
    got = moved(give, "dp", other_core)
    weights = [own_weight] + [moved(own_weight, "dp", along_z(step)) for step in (1, 2, 3)]

    own_deltas, parts = call(
        functools.partial(arrange, plan, groups),
        (
            jax.ShapeDtypeStruct((slots, dp_count * MOST, LANES), BF16),
            jax.ShapeDtypeStruct((8, 8 * BLOCK, columns), BF16),
        ),
        arrived,
        keep,
        got,
        *weights,
    )
    partner_deltas = moved(own_deltas, "tensor", other_z)
    own_left, own_right = to_right(own_deltas), to_left(own_deltas)
    partner_left, partner_right = to_right(partner_deltas), to_left(partner_deltas)
    deltas = [
        own_deltas,
        partner_deltas,
        own_left,
        partner_left,
        own_right,
        partner_right,
        to_right(own_left),
        to_left(partner_right),
    ]
    parts = exchanged(parts, along_y)
    outgoing, kept_deltas = call(
        functools.partial(project, plan, groups),
        (
            jax.ShapeDtypeStruct((packed_rows, LANES), BF16),
            jax.ShapeDtypeStruct((len(deltas),) + own_deltas.shape, BF16),
        ),
        *deltas,
        expert_weight,
        index=(holders,),
        scratch=[value_rows, pltpu.VMEM(expert_weight.shape, BF16), pltpu.SemaphoreType.DMA((len(deltas),))],
        out_specs=(IN_VMEM, ANYWHERE),
    )

    returned = exchanged(outgoing.reshape(dp_count, plan.packed, LANES)).reshape(packed_rows, LANES)
    expert_gradient = call(
        functools.partial(weight_gradient, plan, groups),
        jax.ShapeDtypeStruct(expert_weight.shape, BF16),
        kept_deltas,
        arrived,
        index=(holders,),
        scratch=[value_rows],
    )
    weight_part, *shared_parts = call(
        join_along_y,
        (jax.ShapeDtypeStruct((32 * BLOCK, columns), BF16),)
        + tuple(jax.ShapeDtypeStruct((BLOCK, columns), F32) for _ in range(4)),
        parts,
        index=(my_place,),
        scratch=[pltpu.VMEM((4 * BLOCK, columns), F32)],
    )
    weight_all = jnp.concatenate([weight_part, moved(weight_part, "dp", other_core)], axis=0)
    shared_term, chosen = call(
        functools.partial(shared_rows, plan, groups),
        (jax.ShapeDtypeStruct((tokens, columns), F32), jax.ShapeDtypeStruct((packed_rows, tokens), BF16)),
        shared_all,
        weight_all,
        routing.T,
        slot_expert.reshape(1, -1),
        index=(my_place,),
        scratch=[pltpu.VMEM((shared_hidden, columns), BF16)],
        after=(expert_gradient,),
    )
    shared_parts = shared_parts[:1] + [
        moved(part, "dp", along_z(step)) for step, part in enumerate(shared_parts) if step
    ]
    input_gradient, shared_gradient = call(
        functools.partial(combine, plan, groups),
        (
            jax.ShapeDtypeStruct((tokens, columns), BF16),
            jax.ShapeDtypeStruct(shared_weight.shape, F32),
        ),
        returned,
        chosen,
        shared_term,
        *shared_parts,
    )
    return input_gradient, expert_gradient, shared_gradient


def solution(mesh):
    return jax.shard_map(
        body,
        mesh=mesh,
        in_specs=(
            P("dp", "tensor"),
            P("dp", None, "tensor"),
            P(("dp", "tensor"), None),
            P("dp", None, "tensor"),
            P("dp", "tensor"),
            P("dp", None),
            P(),
        ),
        out_specs=(P("dp", "tensor"), P("dp", None, "tensor"), P("dp", "tensor")),
        check_vma=False,
    )
```

time: 221 us -> 183 us (0.83)
  waiting for transfers between devices: 60.4 us -> 26 us
  between operations: 14.5 us -> 1.06 us
  starting transfers between devices: 102 us -> 115 us
  other arithmetic: 3.34 us -> 0.15 us
  local copies, waits for them, and re-layouts: 15.8 us -> 18.1 us
    ppermute x15 -> x22, starting transfers between devices: 58.2 us -> 79.6 us  [moved(): lax.ppermute(block, axis, [(i, target(i)) for i in range(lax.axis_size(ax...]
    reduce_scatter x1 -> x0, waiting for transfers between devices: 14.5 us -> none  [group_sum(): lax.psum_scatter(block, 'dp', scatter_dimension=0, axis_index_groups=grou...]
    all_gather x1 -> x0, waiting for transfers between devices: 9.53 us -> none  [body(): lax.all_gather(weight_part.reshape(8 * BLOCK, columns), 'dp', axis=0, axi...]
    ppermute x15 -> x22, waiting for transfers between devices: 34.8 us -> 26 us  [moved(): lax.ppermute(block, axis, [(i, target(i)) for i in range(lax.axis_size(ax...]
    all_to_all x4 -> x3, starting transfers between devices: 44.2 us -> 35.6 us  [exchanged(): lax.all_to_all(block, 'dp', split_axis=0, concat_axis=0, axis_index_group...]
    unnamed x64 -> x46, local copies, waits for them, and re-layouts: 13.4 us -> 18 us
    add x2 -> x0, other arithmetic: 3.23 us -> none  [the longest x1 3.22 us: body(): shared_part = keep + moved(give, 'dp', other_core)]
    pallas_call x7 -> x8, Pallas kernels: 22.3 us -> 21.7 us  [call(): pl.pallas_call(run, out_shape=outs, in_specs=[IN_SMEM] * len(index) + [IN...]
  transfers between devices with their start and end apart: 21 -> 25, of which waited for: 11 -> 7; matrix products, arithmetic and copies ran while one was open for 2% -> 0% of each run, Pallas kernels for 8% -> 11%
where the time goes in v2:
time: 183 us; the launch traced here: 182 us
  starting transfers between devices  115 us (63%)
  waiting for transfers between devices  26 us (14%)
  Pallas kernels  21.7 us (12%)
  local copies, waits for them, and re-layouts  18.1 us (10%)
    ppermute x22, starting transfers between devices, moved(): lax.ppermute(block, axis, [(i, target(i)) for i in range(lax.axis_size(ax...  79.6 us
    all_to_all x3, starting transfers between devices, exchanged(): lax.all_to_all(block, 'dp', split_axis=0, concat_axis=0, axis_index_group...  35.6 us
    ppermute x22, waiting for transfers between devices, moved(): lax.ppermute(block, axis, [(i, target(i)) for i in range(lax.axis_size(ax...  26 us
    pallas_call x8, Pallas kernels, call(): pl.pallas_call(run, out_shape=outs, in_specs=[IN_SMEM] * len(index) + [IN...  21.7 us
    unnamed x46, local copies, waits for them, and re-layouts  18 us
  transfers between devices with their start and end apart: 25, of which 7 were waited for; matrix products, arithmetic and copies ran while one was open for 0% of the time, Pallas kernels for 11%

profile of v2, /device:TPU:1, one launch (start us, length us, event | category | flops | bytes accessed | tf_op | source)
XLA Modules:
  0.0 182.1 jit_solution(18443867759575895539)
XLA Ops:
  0.6 4.8 %collective-permute-start = (bf16[16,1024]{1,0:T(8,128)(2,1)}, bf16[16,1024]{1,0:T(8,128)(2,1)S(1)}, u32[]{:S(2)}, u32[]{:S(2)}) collective-permute-start(bf16[16,1024]{1,0:T(8,128)(2,1)} %refs_4_.1), channel_id=1, source_target_pairs={{0,4},{1,5},{2,6},{3,7},{4,0},{5,1},{6,2},{7,3},{8,12},{9,13},{10,... | collective-permute-start | bytes 98312 | tf_op jit(solution)/shard_map/ppermute | solution.py:277
  9.4 5.7 %shard_map.94 = (bf16[64,104,128]{2,1,0:T(8,128)(2,1)S(1)}, bf16[16,1024]{1,0:T(8,128)(2,1)S(1)}) custom-call(s32[8,128]{1,0:T(8,128)S(1)} %bitcast.18, s32[1,128]{1,0:T(1,128)S(1)} %bitcast.20, bf16[1024,128]{1,0:T(8,128)(2,1)S(1)} %bitcast.17, bf16[128,512]{1,0:T(8,128)(2,1)S(1)} %copy-done.12, bf16[16,1024]{1,0:T(8,128)(2,1)S(1)} %copy-done.17), custom_call_target="tpu_custom_call" | custom-call | tf_op jit(solution)/shard_map/pallas_call | solution.py:83
  16.9 16.3 %all-to-all-start = ((bf16[64,104,128]{2,1,0:T(8,128)(2,1)}), bf16[64,104,128]{2,1,0:T(8,128)(2,1)S(1)}, u32[]{:S(2)}, u32[]{:S(2)}) async-start(bf16[64,104,128]{2,1,0:T(8,128)(2,1)} %get-tuple-element.25), calls=%async_computation | async-start | bytes 3407872 | tf_op jit(solution)/shard_map/all_to_all | solution.py:321
  33.2 3.1 %collective-permute-start.1 = (bf16[16,1024]{1,0:T(8,128)(2,1)S(1)}, bf16[16,1024]{1,0:T(8,128)(2,1)S(1)}, u32[]{:S(2)}, u32[]{:S(2)}) collective-permute-start(bf16[16,1024]{1,0:T(8,128)(2,1)S(1)} %get-tuple-element.26.refs_2_), channel_id=1, source_target_pairs={{0,1},{1,2},{2,3},{3,0},{4,5},{5,6},{6,7},{7,4},{8,9},{9,10},{10,1... | collective-permute-start | bytes 98312 | tf_op jit(solution)/shard_map/ppermute | solution.py:277
  36.4 3.4 %collective-permute-start.3 = (bf16[16,1024]{1,0:T(8,128)(2,1)S(1)}, bf16[16,1024]{1,0:T(8,128)(2,1)S(1)}, u32[]{:S(2)}, u32[]{:S(2)}) collective-permute-start(bf16[16,1024]{1,0:T(8,128)(2,1)S(1)} %get-tuple-element.26.refs_2_), channel_id=1, source_target_pairs={{0,3},{1,0},{2,1},{3,2},{4,7},{5,4},{6,5},{7,6},{8,11},{9,8},{10,9... | collective-permute-start | bytes 98312 | tf_op jit(solution)/shard_map/ppermute | solution.py:277
  39.7 3.4 %collective-permute-start.5 = (bf16[16,1024]{1,0:T(8,128)(2,1)S(1)}, bf16[16,1024]{1,0:T(8,128)(2,1)S(1)}, u32[]{:S(2)}, u32[]{:S(2)}) collective-permute-start(bf16[16,1024]{1,0:T(8,128)(2,1)S(1)} %get-tuple-element.26.refs_2_), channel_id=1, source_target_pairs={{0,2},{1,3},{2,0},{3,1},{4,6},{5,7},{6,4},{7,5},{8,10},{9,11},{10,... | collective-permute-start | bytes 98312 | tf_op jit(solution)/shard_map/ppermute | solution.py:277
  43.2 2.2 %collective-permute-start.2 = (bf16[16,1024]{1,0:T(8,128)(2,1)S(1)}, bf16[16,1024]{1,0:T(8,128)(2,1)S(1)}, u32[]{:S(2)}, u32[]{:S(2)}) collective-permute-start(bf16[16,1024]{1,0:T(8,128)(2,1)S(1)} %copy-done.16), channel_id=1, source_target_pairs={{0,1},{1,2},{2,3},{3,0},{4,5},{5,6},{6,7},{7,4},{8,9},{9,10},{10,1... | collective-permute-start | bytes 98312 | tf_op jit(solution)/shard_map/ppermute | solution.py:277
  45.4 4.3 %collective-permute-start.4 = (bf16[16,1024]{1,0:T(8,128)(2,1)S(1)}, bf16[16,1024]{1,0:T(8,128)(2,1)S(1)}, u32[]{:S(2)}, u32[]{:S(2)}) collective-permute-start(bf16[16,1024]{1,0:T(8,128)(2,1)S(1)} %copy-done.16), channel_id=1, source_target_pairs={{0,3},{1,0},{2,1},{3,2},{4,7},{5,4},{6,5},{7,6},{8,11},{9,8},{10,9... | collective-permute-start | bytes 98312 | tf_op jit(solution)/shard_map/ppermute | solution.py:277
  52.1 4.1 %collective-permute-done.6.refs_9_ = bf16[16,1024]{1,0:T(8,128)(2,1)S(1)} collective-permute-done((bf16[16,1024]{1,0:T(8,128)(2,1)S(1)}, bf16[16,1024]{1,0:T(8,128)(2,1)S(1)}, u32[]{:S(2)}, u32[]{:S(2)}) %collective-permute-start.6) | collective-permute-done | bytes 32800 | tf_op jit(solution)/shard_map/ppermute | solution.py:277
  57.3 4.6 %collective-permute-start.7 = (f32[512,512]{1,0:T(8,128)S(1)}, f32[512,512]{1,0:T(8,128)S(1)}, u32[]{:S(2)}, u32[]{:S(2)}) collective-permute-start(f32[512,512]{1,0:T(8,128)S(1)} %get-tuple-element.29), channel_id=1, source_target_pairs={{0,8},{8,0},{16,24},{24,16},{32,40},{40,32},{48,56},{56,48},{64,72... | collective-permute-start | bytes 3145736 | tf_op jit(solution)/shard_map/ppermute | solution.py:277
  62.0 5.3 %collective-permute-start.10 = (bf16[16,512]{1,0:T(8,128)(2,1)S(1)}, bf16[16,512]{1,0:T(8,128)(2,1)S(1)}, u32[]{:S(2)}, u32[]{:S(2)}) collective-permute-start(bf16[16,512]{1,0:T(8,128)(2,1)S(1)} %get-tuple-element.30.refs_3_), channel_id=1, source_target_pairs={{0,48},{8,56},{16,0},{24,8},{32,16},{40,24},{48,32},{56,40},{64,11... | collective-permute-start | bytes 49160 | tf_op jit(solution)/shard_map/ppermute | solution.py:277
  69.2 6.1 %collective-permute-start.9 = (bf16[16,512]{1,0:T(8,128)(2,1)S(1)}, bf16[16,512]{1,0:T(8,128)(2,1)S(1)}, u32[]{:S(2)}, u32[]{:S(2)}) collective-permute-start(bf16[16,512]{1,0:T(8,128)(2,1)S(1)} %get-tuple-element.30.refs_3_), channel_id=1, source_target_pairs={{0,32},{8,40},{16,48},{24,56},{32,0},{40,8},{48,16},{56,24},{64,96... | collective-permute-start | bytes 49160 | tf_op jit(solution)/shard_map/ppermute | solution.py:277
  75.3 2.3 %collective-permute-done.9.refs_5_ = bf16[16,512]{1,0:T(8,128)(2,1)S(1)} collective-permute-done((bf16[16,512]{1,0:T(8,128)(2,1)S(1)}, bf16[16,512]{1,0:T(8,128)(2,1)S(1)}, u32[]{:S(2)}, u32[]{:S(2)}) %collective-permute-start.9) | collective-permute-done | bytes 16416 | tf_op jit(solution)/shard_map/ppermute | solution.py:277
  81.3 6.5 %all-to-all-start.2 = ((bf16[8,128,512]{2,1,0:T(8,128)(2,1)}), bf16[8,128,512]{2,1,0:T(8,128)(2,1)S(1)}, u32[]{:S(2)}, u32[]{:S(2)}) async-start(bf16[8,128,512]{2,1,0:T(8,128)(2,1)} %copy-done.9), calls=%async_computation.2 | async-start | bytes 2097152 | tf_op jit(solution)/shard_map/all_to_all | solution.py:321
  87.8 2.2 %collective-permute-start.11 = (bf16[2,640,128]{2,1,0:T(8,128)(2,1)S(1)}, bf16[2,640,128]{2,1,0:T(8,128)(2,1)S(1)}, u32[]{:S(2)}, u32[]{:S(2)}) collective-permute-start(bf16[2,640,128]{2,1,0:T(8,128)(2,1)S(1)} %get-tuple-element.31.refs_1_), channel_id=1, source_target_pairs={{0,4},{1,5},{2,6},{3,7},{4,0},{5,1},{6,2},{7,3},{8,12},{9,13},{10,... | collective-permute-start | bytes 983048 | tf_op jit(solution)/shard_map/ppermute | solution.py:277
  90.0 2.6 %collective-permute-start.12 = (bf16[2,640,128]{2,1,0:T(8,128)(2,1)S(1)}, bf16[2,640,128]{2,1,0:T(8,128)(2,1)S(1)}, u32[]{:S(2)}, u32[]{:S(2)}) collective-permute-start(bf16[2,640,128]{2,1,0:T(8,128)(2,1)S(1)} %get-tuple-element.31.refs_1_), channel_id=1, source_target_pairs={{0,1},{1,2},{2,3},{3,0},{4,5},{5,6},{6,7},{7,4},{8,9},{9,10},{10,1... | collective-permute-start | bytes 983048 | tf_op jit(solution)/shard_map/ppermute | solution.py:277
  92.5 4.6 %collective-permute-done.11.refs_2_ = bf16[2,640,128]{2,1,0:T(8,128)(2,1)S(1)} collective-permute-done((bf16[2,640,128]{2,1,0:T(8,128)(2,1)S(1)}, bf16[2,640,128]{2,1,0:T(8,128)(2,1)S(1)}, u32[]{:S(2)}, u32[]{:S(2)}) %collective-permute-start.11) | collective-permute-done | bytes 327712 | tf_op jit(solution)/shard_map/ppermute | solution.py:277
  97.1 4.9 %collective-permute-start.15 = (bf16[2,640,128]{2,1,0:T(8,128)(2,1)S(1)}, bf16[2,640,128]{2,1,0:T(8,128)(2,1)S(1)}, u32[]{:S(2)}, u32[]{:S(2)}) collective-permute-start(bf16[2,640,128]{2,1,0:T(8,128)(2,1)S(1)} %collective-permute-done.11.refs_2_), channel_id=1, source_target_pairs={{0,3},{1,0},{2,1},{3,2},{4,7},{5,4},{6,5},{7,6},{8,11},{9,8},{10,9... | collective-permute-start | bytes 983048 | tf_op jit(solution)/shard_map/ppermute | solution.py:277
  102.0 2.3 %collective-permute-start.14 = (bf16[2,640,128]{2,1,0:T(8,128)(2,1)S(1)}, bf16[2,640,128]{2,1,0:T(8,128)(2,1)S(1)}, u32[]{:S(2)}, u32[]{:S(2)}) collective-permute-start(bf16[2,640,128]{2,1,0:T(8,128)(2,1)S(1)} %get-tuple-element.31.refs_1_), channel_id=1, source_target_pairs={{0,3},{1,0},{2,1},{3,2},{4,7},{5,4},{6,5},{7,6},{8,11},{9,8},{10,9... | collective-permute-start | bytes 983048 | tf_op jit(solution)/shard_map/ppermute | solution.py:277
  104.3 3.0 %collective-permute-start.13 = (bf16[2,640,128]{2,1,0:T(8,128)(2,1)S(1)}, bf16[2,640,128]{2,1,0:T(8,128)(2,1)S(1)}, u32[]{:S(2)}, u32[]{:S(2)}) collective-permute-start(bf16[2,640,128]{2,1,0:T(8,128)(2,1)S(1)} %collective-permute-done.11.refs_2_), channel_id=1, source_target_pairs={{0,1},{1,2},{2,3},{3,0},{4,5},{5,6},{6,7},{7,4},{8,9},{9,10},{10,1... | collective-permute-start | bytes 983048 | tf_op jit(solution)/shard_map/ppermute | solution.py:277
  109.3 4.6 %collective-permute-start.17 = (bf16[2,640,128]{2,1,0:T(8,128)(2,1)S(1)}, bf16[2,640,128]{2,1,0:T(8,128)(2,1)S(1)}, u32[]{:S(2)}, u32[]{:S(2)}) collective-permute-start(bf16[2,640,128]{2,1,0:T(8,128)(2,1)S(1)} %collective-permute-done.15.refs_6_), channel_id=1, source_target_pairs={{0,3},{1,0},{2,1},{3,2},{4,7},{5,4},{6,5},{7,6},{8,11},{9,8},{10,9... | collective-permute-start | bytes 983048 | tf_op jit(solution)/shard_map/ppermute | solution.py:277
  114.3 7.0 %collective-permute-done.16.refs_7_ = bf16[2,640,128]{2,1,0:T(8,128)(2,1)S(1)} collective-permute-done((bf16[2,640,128]{2,1,0:T(8,128)(2,1)S(1)}, bf16[2,640,128]{2,1,0:T(8,128)(2,1)S(1)}, u32[]{:S(2)}, u32[]{:S(2)}) %collective-permute-start.16) | collective-permute-done | bytes 327712 | tf_op jit(solution)/shard_map/ppermute | solution.py:277
  123.0 4.0 %shard_map.98 = (bf16[5120,128]{1,0:T(8,128)(2,1)S(1)}, bf16[8,2,640,128]{3,2,1,0:T(8,128)(2,1)}) custom-call(s32[8]{0:T(128)S(1)} %stack.44.refs_1_.refs_0_, bf16[2,640,128]{2,1,0:T(8,128)(2,1)S(1)} %get-tuple-element.31.refs_1_, bf16[2,640,128]{2,1,0:T(8,128)(2,1)S(1)} %collective-permute-done.11.refs_2_, ...), custom_call_target="tpu_custom_call" | custom-call | tf_op jit(solution)/shard_map/pallas_call | solution.py:83
  129.1 12.8 %all-to-all-start.1 = ((bf16[64,80,128]{2,1,0:T(8,128)(2,1)}), bf16[64,80,128]{2,1,0:T(8,128)(2,1)S(1)}, u32[]{:S(2)}, u32[]{:S(2)}) async-start(bf16[64,80,128]{2,1,0:T(8,128)(2,1)} %bitcast.16), calls=%async_computation.1 | async-start | bytes 2621440 | tf_op jit(solution)/shard_map/all_to_all | solution.py:321
  143.7 2.4 %collective-permute-start.18 = (bf16[512,512]{1,0:T(8,128)(2,1)S(1)}, bf16[512,512]{1,0:T(8,128)(2,1)S(1)}, u32[]{:S(2)}, u32[]{:S(2)}) collective-permute-start(bf16[512,512]{1,0:T(8,128)(2,1)S(1)} %get-tuple-element.35), channel_id=1, source_target_pairs={{0,8},{8,0},{16,24},{24,16},{32,40},{40,32},{48,56},{56,48},{64,72... | collective-permute-start | bytes 1572872 | tf_op jit(solution)/shard_map/ppermute | solution.py:277
  147.8 5.4 %shard_map.100.refs_5_ = bf16[2,1024,512]{2,1,0:T(8,128)(2,1)} custom-call(s32[8]{0:T(128)S(1)} %stack.44.refs_1_.refs_0_, bf16[8,2,640,128]{3,2,1,0:T(8,128)(2,1)S(1)} %copy-done.4, bf16[64,104,128]{2,1,0:T(8,128)(2,1)S(1)} %all-to-all-done.refs_0_.refs_2_), custom_call_target="tpu_custom_call" | custom-call | tf_op jit(solution)/shard_map/pallas_call | solution.py:83
  153.3 4.2 %collective-permute-start.19 = (f32[16,512]{1,0:T(8,128)S(1)}, f32[16,512]{1,0:T(8,128)S(1)}, u32[]{:S(2)}, u32[]{:S(2)}) collective-permute-start(f32[16,512]{1,0:T(8,128)S(1)} %get-tuple-element.40), channel_id=1, source_target_pairs={{0,16},{8,24},{16,32},{24,40},{32,48},{40,56},{48,0},{56,8},{64,80... | collective-permute-start | bytes 98312 | tf_op jit(solution)/shard_map/ppermute | solution.py:277
  157.5 5.2 %collective-permute-start.20 = (f32[16,512]{1,0:T(8,128)S(1)}, f32[16,512]{1,0:T(8,128)S(1)}, u32[]{:S(2)}, u32[]{:S(2)}) collective-permute-start(f32[16,512]{1,0:T(8,128)S(1)} %get-tuple-element.41), channel_id=1, source_target_pairs={{0,32},{8,40},{16,48},{24,56},{32,0},{40,8},{48,16},{56,24},{64,96... | collective-permute-start | bytes 98312 | tf_op jit(solution)/shard_map/ppermute | solution.py:277
  162.7 5.2 %collective-permute-start.21 = (f32[16,512]{1,0:T(8,128)S(1)}, f32[16,512]{1,0:T(8,128)S(1)}, u32[]{:S(2)}, u32[]{:S(2)}) collective-permute-start(f32[16,512]{1,0:T(8,128)S(1)} %get-tuple-element.42), channel_id=1, source_target_pairs={{0,48},{8,56},{16,0},{24,8},{32,16},{40,24},{48,32},{56,40},{64,11... | collective-permute-start | bytes 98312 | tf_op jit(solution)/shard_map/ppermute | solution.py:277
  168.1 2.3 %shard_map.101 = (f32[128,512]{1,0:T(8,128)S(1)}, bf16[5120,128]{1,0:T(8,128)(2,1)S(1)}) custom-call(s32[2]{0:T(128)S(1)} %pad_add_fusion.refs_0_, bf16[128,1024]{1,0:T(8,128)(2,1)S(1)} %get-tuple-element.33.refs_1_, bf16[1024,512]{1,0:T(8,128)(2,1)S(1)} %pad_maximum_fusion.refs_2_, s32[8,128]{1,0:T(8,128)S(1)} %bitcast.19, s32[1,128]{1,0:T(1,128)S(1)} %bitcast.21, ...), custom_call_target="tpu_custom_call" | custom-call | tf_op jit(solution)/shard_map/pallas_call | solution.py:83
  171.4 5.2 %collective-permute-done.19.refs_4_ = f32[16,512]{1,0:T(8,128)S(1)} collective-permute-done((f32[16,512]{1,0:T(8,128)S(1)}, f32[16,512]{1,0:T(8,128)S(1)}, u32[]{:S(2)}, u32[]{:S(2)}) %collective-permute-start.19) | collective-permute-done | bytes 32800 | tf_op jit(solution)/shard_map/ppermute | solution.py:277
  176.6 2.2 %collective-permute-done.20.refs_5_ = f32[16,512]{1,0:T(8,128)S(1)} collective-permute-done((f32[16,512]{1,0:T(8,128)S(1)}, f32[16,512]{1,0:T(8,128)S(1)}, u32[]{:S(2)}, u32[]{:S(2)}) %collective-permute-start.20) | collective-permute-done | bytes 32800 | tf_op jit(solution)/shard_map/ppermute | solution.py:277
  (76 shorter events, 29.0 us)
Async XLA Ops:
  0.6 15.7 %collective-permute-start = (bf16[16,1024]{1,0:T(8,128)(2,1)}, bf16[16,1024]{1,0:T(8,128)(2,1)S(1)}, u32[]{:S(2)}, u32[]{:S(2)}) collective-permute-start(bf16[16,1024]{1,0:T(8,128)(2,1)} %refs_4_.1), channel_id=1, source_target_pairs={{0,4},{1,5},{2,6},{3,7},{4,0},{5,1},{6,2},{7,3},{8,12},{9,13},{10,... | collective-permute-start | bytes 98312 | tf_op jit(solution)/shard_map/ppermute | solution.py:277
  16.9 26.3 %copy-start.16 = (bf16[16,1024]{1,0:T(8,128)(2,1)S(1)}, bf16[16,1024]{1,0:T(8,128)(2,1)}, u32[]{:S(2)}) copy-start(bf16[16,1024]{1,0:T(8,128)(2,1)} %get-tuple-element.27.refs_3_) | copy-start | bytes 98308
  16.9 39.3 %copy-start.13 = (bf16[128,512]{1,0:T(8,128)(2,1)S(1)}, bf16[128,512]{1,0:T(8,128)(2,1)}, u32[]{:S(2)}) copy-start(bf16[128,512]{1,0:T(8,128)(2,1)} %refs_10_.1) | copy-start | bytes 393220
  16.9 39.3 %copy-start.20 = (bf16[16,512]{1,0:T(8,128)(2,1)S(1)}, bf16[16,512]{1,0:T(8,128)(2,1)}, u32[]{:S(2)}) copy-start(bf16[16,512]{1,0:T(8,128)(2,1)} %refs_11_.1) | copy-start | bytes 49156
  16.9 61.8 %all-to-all-start = ((bf16[64,104,128]{2,1,0:T(8,128)(2,1)}), bf16[64,104,128]{2,1,0:T(8,128)(2,1)S(1)}, u32[]{:S(2)}, u32[]{:S(2)}) async-start(bf16[64,104,128]{2,1,0:T(8,128)(2,1)} %get-tuple-element.25), calls=%async_computation | async-start | bytes 3407872 | tf_op jit(solution)/shard_map/all_to_all | solution.py:321
  33.2 16.5 %collective-permute-start.1 = (bf16[16,1024]{1,0:T(8,128)(2,1)S(1)}, bf16[16,1024]{1,0:T(8,128)(2,1)S(1)}, u32[]{:S(2)}, u32[]{:S(2)}) collective-permute-start(bf16[16,1024]{1,0:T(8,128)(2,1)S(1)} %get-tuple-element.26.refs_2_), channel_id=1, source_target_pairs={{0,1},{1,2},{2,3},{3,0},{4,5},{5,6},{6,7},{7,4},{8,9},{9,10},{10,1... | collective-permute-start | bytes 98312 | tf_op jit(solution)/shard_map/ppermute | solution.py:277
  36.4 15.7 %collective-permute-start.3 = (bf16[16,1024]{1,0:T(8,128)(2,1)S(1)}, bf16[16,1024]{1,0:T(8,128)(2,1)S(1)}, u32[]{:S(2)}, u32[]{:S(2)}) collective-permute-start(bf16[16,1024]{1,0:T(8,128)(2,1)S(1)} %get-tuple-element.26.refs_2_), channel_id=1, source_target_pairs={{0,3},{1,0},{2,1},{3,2},{4,7},{5,4},{6,5},{7,6},{8,11},{9,8},{10,9... | collective-permute-start | bytes 98312 | tf_op jit(solution)/shard_map/ppermute | solution.py:277
  39.7 12.3 %collective-permute-start.5 = (bf16[16,1024]{1,0:T(8,128)(2,1)S(1)}, bf16[16,1024]{1,0:T(8,128)(2,1)S(1)}, u32[]{:S(2)}, u32[]{:S(2)}) collective-permute-start(bf16[16,1024]{1,0:T(8,128)(2,1)S(1)} %get-tuple-element.26.refs_2_), channel_id=1, source_target_pairs={{0,2},{1,3},{2,0},{3,1},{4,6},{5,7},{6,4},{7,5},{8,10},{9,11},{10,... | collective-permute-start | bytes 98312 | tf_op jit(solution)/shard_map/ppermute | solution.py:277
  43.2 8.8 %collective-permute-start.2 = (bf16[16,1024]{1,0:T(8,128)(2,1)S(1)}, bf16[16,1024]{1,0:T(8,128)(2,1)S(1)}, u32[]{:S(2)}, u32[]{:S(2)}) collective-permute-start(bf16[16,1024]{1,0:T(8,128)(2,1)S(1)} %copy-done.16), channel_id=1, source_target_pairs={{0,1},{1,2},{2,3},{3,0},{4,5},{5,6},{6,7},{7,4},{8,9},{9,10},{10,1... | collective-permute-start | bytes 98312 | tf_op jit(solution)/shard_map/ppermute | solution.py:277
  45.4 6.6 %collective-permute-start.4 = (bf16[16,1024]{1,0:T(8,128)(2,1)S(1)}, bf16[16,1024]{1,0:T(8,128)(2,1)S(1)}, u32[]{:S(2)}, u32[]{:S(2)}) collective-permute-start(bf16[16,1024]{1,0:T(8,128)(2,1)S(1)} %copy-done.16), channel_id=1, source_target_pairs={{0,3},{1,0},{2,1},{3,2},{4,7},{5,4},{6,5},{7,6},{8,11},{9,8},{10,9... | collective-permute-start | bytes 98312 | tf_op jit(solution)/shard_map/ppermute | solution.py:277
  49.7 6.5 %collective-permute-start.6 = (bf16[16,1024]{1,0:T(8,128)(2,1)S(1)}, bf16[16,1024]{1,0:T(8,128)(2,1)S(1)}, u32[]{:S(2)}, u32[]{:S(2)}) collective-permute-start(bf16[16,1024]{1,0:T(8,128)(2,1)S(1)} %copy-done.16), channel_id=1, source_target_pairs={{0,2},{1,3},{2,0},{3,1},{4,6},{5,7},{6,4},{7,5},{8,10},{9,11},{10,... | collective-permute-start | bytes 98312 | tf_op jit(solution)/shard_map/ppermute | solution.py:277
  57.3 20.3 %collective-permute-start.7 = (f32[512,512]{1,0:T(8,128)S(1)}, f32[512,512]{1,0:T(8,128)S(1)}, u32[]{:S(2)}, u32[]{:S(2)}) collective-permute-start(f32[512,512]{1,0:T(8,128)S(1)} %get-tuple-element.29), channel_id=1, source_target_pairs={{0,8},{8,0},{16,24},{24,16},{32,40},{40,32},{48,56},{56,48},{64,72... | collective-permute-start | bytes 3145736 | tf_op jit(solution)/shard_map/ppermute | solution.py:277
  62.0 13.3 %collective-permute-start.10 = (bf16[16,512]{1,0:T(8,128)(2,1)S(1)}, bf16[16,512]{1,0:T(8,128)(2,1)S(1)}, u32[]{:S(2)}, u32[]{:S(2)}) collective-permute-start(bf16[16,512]{1,0:T(8,128)(2,1)S(1)} %get-tuple-element.30.refs_3_), channel_id=1, source_target_pairs={{0,48},{8,56},{16,0},{24,8},{32,16},{40,24},{48,32},{56,40},{64,11... | collective-permute-start | bytes 49160 | tf_op jit(solution)/shard_map/ppermute | solution.py:277
  67.3 8.0 %collective-permute-start.8 = (bf16[16,512]{1,0:T(8,128)(2,1)S(1)}, bf16[16,512]{1,0:T(8,128)(2,1)S(1)}, u32[]{:S(2)}, u32[]{:S(2)}) collective-permute-start(bf16[16,512]{1,0:T(8,128)(2,1)S(1)} %get-tuple-element.30.refs_3_), channel_id=1, source_target_pairs={{0,16},{8,24},{16,32},{24,40},{32,48},{40,56},{48,0},{56,8},{64,80... | collective-permute-start | bytes 49160 | tf_op jit(solution)/shard_map/ppermute | solution.py:277
  69.2 8.4 %collective-permute-start.9 = (bf16[16,512]{1,0:T(8,128)(2,1)S(1)}, bf16[16,512]{1,0:T(8,128)(2,1)S(1)}, u32[]{:S(2)}, u32[]{:S(2)}) collective-permute-start(bf16[16,512]{1,0:T(8,128)(2,1)S(1)} %get-tuple-element.30.refs_3_), channel_id=1, source_target_pairs={{0,32},{8,40},{16,48},{24,56},{32,0},{40,8},{48,16},{56,24},{64,96... | collective-permute-start | bytes 49160 | tf_op jit(solution)/shard_map/ppermute | solution.py:277
  81.3 46.8 %all-to-all-start.2 = ((bf16[8,128,512]{2,1,0:T(8,128)(2,1)}), bf16[8,128,512]{2,1,0:T(8,128)(2,1)S(1)}, u32[]{:S(2)}, u32[]{:S(2)}) async-start(bf16[8,128,512]{2,1,0:T(8,128)(2,1)} %copy-done.9), calls=%async_computation.2 | async-start | bytes 2097152 | tf_op jit(solution)/shard_map/all_to_all | solution.py:321
  87.8 9.4 %collective-permute-start.11 = (bf16[2,640,128]{2,1,0:T(8,128)(2,1)S(1)}, bf16[2,640,128]{2,1,0:T(8,128)(2,1)S(1)}, u32[]{:S(2)}, u32[]{:S(2)}) collective-permute-start(bf16[2,640,128]{2,1,0:T(8,128)(2,1)S(1)} %get-tuple-element.31.refs_1_), channel_id=1, source_target_pairs={{0,4},{1,5},{2,6},{3,7},{4,0},{5,1},{6,2},{7,3},{8,12},{9,13},{10,... | collective-permute-start | bytes 983048 | tf_op jit(solution)/shard_map/ppermute | solution.py:277
  90.0 17.4 %collective-permute-start.12 = (bf16[2,640,128]{2,1,0:T(8,128)(2,1)S(1)}, bf16[2,640,128]{2,1,0:T(8,128)(2,1)S(1)}, u32[]{:S(2)}, u32[]{:S(2)}) collective-permute-start(bf16[2,640,128]{2,1,0:T(8,128)(2,1)S(1)} %get-tuple-element.31.refs_1_), channel_id=1, source_target_pairs={{0,1},{1,2},{2,3},{3,0},{4,5},{5,6},{6,7},{7,4},{8,9},{9,10},{10,1... | collective-permute-start | bytes 983048 | tf_op jit(solution)/shard_map/ppermute | solution.py:277
  97.1 12.1 %collective-permute-start.15 = (bf16[2,640,128]{2,1,0:T(8,128)(2,1)S(1)}, bf16[2,640,128]{2,1,0:T(8,128)(2,1)S(1)}, u32[]{:S(2)}, u32[]{:S(2)}) collective-permute-start(bf16[2,640,128]{2,1,0:T(8,128)(2,1)S(1)} %collective-permute-done.11.refs_2_), channel_id=1, source_target_pairs={{0,3},{1,0},{2,1},{3,2},{4,7},{5,4},{6,5},{7,6},{8,11},{9,8},{10,9... | collective-permute-start | bytes 983048 | tf_op jit(solution)/shard_map/ppermute | solution.py:277
  102.0 12.3 %collective-permute-start.14 = (bf16[2,640,128]{2,1,0:T(8,128)(2,1)S(1)}, bf16[2,640,128]{2,1,0:T(8,128)(2,1)S(1)}, u32[]{:S(2)}, u32[]{:S(2)}) collective-permute-start(bf16[2,640,128]{2,1,0:T(8,128)(2,1)S(1)} %get-tuple-element.31.refs_1_), channel_id=1, source_target_pairs={{0,3},{1,0},{2,1},{3,2},{4,7},{5,4},{6,5},{7,6},{8,11},{9,8},{10,9... | collective-permute-start | bytes 983048 | tf_op jit(solution)/shard_map/ppermute | solution.py:277
  104.3 10.0 %collective-permute-start.13 = (bf16[2,640,128]{2,1,0:T(8,128)(2,1)S(1)}, bf16[2,640,128]{2,1,0:T(8,128)(2,1)S(1)}, u32[]{:S(2)}, u32[]{:S(2)}) collective-permute-start(bf16[2,640,128]{2,1,0:T(8,128)(2,1)S(1)} %collective-permute-done.11.refs_2_), channel_id=1, source_target_pairs={{0,1},{1,2},{2,3},{3,0},{4,5},{5,6},{6,7},{7,4},{8,9},{9,10},{10,1... | collective-permute-start | bytes 983048 | tf_op jit(solution)/shard_map/ppermute | solution.py:277
  107.3 14.0 %collective-permute-start.16 = (bf16[2,640,128]{2,1,0:T(8,128)(2,1)S(1)}, bf16[2,640,128]{2,1,0:T(8,128)(2,1)S(1)}, u32[]{:S(2)}, u32[]{:S(2)}) collective-permute-start(bf16[2,640,128]{2,1,0:T(8,128)(2,1)S(1)} %collective-permute-done.12.refs_3_), channel_id=1, source_target_pairs={{0,1},{1,2},{2,3},{3,0},{4,5},{5,6},{6,7},{7,4},{8,9},{9,10},{10,1... | collective-permute-start | bytes 983048 | tf_op jit(solution)/shard_map/ppermute | solution.py:277
  109.3 12.1 %collective-permute-start.17 = (bf16[2,640,128]{2,1,0:T(8,128)(2,1)S(1)}, bf16[2,640,128]{2,1,0:T(8,128)(2,1)S(1)}, u32[]{:S(2)}, u32[]{:S(2)}) collective-permute-start(bf16[2,640,128]{2,1,0:T(8,128)(2,1)S(1)} %collective-permute-done.15.refs_6_), channel_id=1, source_target_pairs={{0,3},{1,0},{2,1},{3,2},{4,7},{5,4},{6,5},{7,6},{8,11},{9,8},{10,9... | collective-permute-start | bytes 983048 | tf_op jit(solution)/shard_map/ppermute | solution.py:277
  129.1 49.7 %all-to-all-start.1 = ((bf16[64,80,128]{2,1,0:T(8,128)(2,1)}), bf16[64,80,128]{2,1,0:T(8,128)(2,1)S(1)}, u32[]{:S(2)}, u32[]{:S(2)}) async-start(bf16[64,80,128]{2,1,0:T(8,128)(2,1)} %bitcast.16), calls=%async_computation.1 | async-start | bytes 2621440 | tf_op jit(solution)/shard_map/all_to_all | solution.py:321
  143.7 24.2 %collective-permute-start.18 = (bf16[512,512]{1,0:T(8,128)(2,1)S(1)}, bf16[512,512]{1,0:T(8,128)(2,1)S(1)}, u32[]{:S(2)}, u32[]{:S(2)}) collective-permute-start(bf16[512,512]{1,0:T(8,128)(2,1)S(1)} %get-tuple-element.35), channel_id=1, source_target_pairs={{0,8},{8,0},{16,24},{24,16},{32,40},{40,32},{48,56},{56,48},{64,72... | collective-permute-start | bytes 1572872 | tf_op jit(solution)/shard_map/ppermute | solution.py:277
  146.1 1.7 copy-start.4
  153.3 14.7 %copy-start = (bf16[2,1024,512]{2,1,0:T(8,128)(2,1)S(1)}, bf16[2,1024,512]{2,1,0:T(8,128)(2,1)}, u32[]{:S(2)}) copy-start(bf16[2,1024,512]{2,1,0:T(8,128)(2,1)} %shard_map.100.refs_5_) | copy-start | bytes 6291460
  153.3 14.7 %copy-start.19 = (s32[128,8]{0,1:T(8,128)S(1)}, s32[128,8]{0,1:T(8,128)}, u32[]{:S(2)}) copy-start(s32[128,8]{0,1:T(8,128)} %param.12) | copy-start | bytes 12292
  153.3 14.8 %copy-start.22 = (s32[128]{0:T(128)S(1)}, s32[128]{0:T(128)}, u32[]{:S(2)}) copy-start(s32[128]{0:T(128)} %param.13) | copy-start | bytes 1540
  153.3 23.3 %collective-permute-start.19 = (f32[16,512]{1,0:T(8,128)S(1)}, f32[16,512]{1,0:T(8,128)S(1)}, u32[]{:S(2)}, u32[]{:S(2)}) collective-permute-start(f32[16,512]{1,0:T(8,128)S(1)} %get-tuple-element.40), channel_id=1, source_target_pairs={{0,16},{8,24},{16,32},{24,40},{32,48},{40,56},{48,0},{56,8},{64,80... | collective-permute-start | bytes 98312 | tf_op jit(solution)/shard_map/ppermute | solution.py:277
  157.5 21.3 %collective-permute-start.20 = (f32[16,512]{1,0:T(8,128)S(1)}, f32[16,512]{1,0:T(8,128)S(1)}, u32[]{:S(2)}, u32[]{:S(2)}) collective-permute-start(f32[16,512]{1,0:T(8,128)S(1)} %get-tuple-element.41), channel_id=1, source_target_pairs={{0,32},{8,40},{16,48},{24,56},{32,0},{40,8},{48,16},{56,24},{64,96... | collective-permute-start | bytes 98312 | tf_op jit(solution)/shard_map/ppermute | solution.py:277
  162.7 16.1 %collective-permute-start.21 = (f32[16,512]{1,0:T(8,128)S(1)}, f32[16,512]{1,0:T(8,128)S(1)}, u32[]{:S(2)}, u32[]{:S(2)}) collective-permute-start(f32[16,512]{1,0:T(8,128)S(1)} %get-tuple-element.42), channel_id=1, source_target_pairs={{0,48},{8,56},{16,0},{24,8},{32,16},{40,24},{48,32},{56,40},{64,11... | collective-permute-start | bytes 98312 | tf_op jit(solution)/shard_map/ppermute | solution.py:277
  (16 other events, 16.3 us)

commit v3 on v2

--- a/solution.py
+++ b/solution.py
@@ -12,7 +12,7 @@
 BLOCK = 16
 BF16 = jnp.bfloat16
 F32 = jnp.float32
-VMEM_LIMIT = 48 * 1024 * 1024
+VMEM_LIMIT = 20 * 1024 * 1024
 
 
 def dot(a, b, contract=((1,), (0,))):
@@ -88,6 +88,13 @@
         scratch_shapes=list(scratch),
         compiler_params=pltpu.CompilerParams(vmem_limit_bytes=VMEM_LIMIT),
     )(*index, *args, *after)
+
+
+def started(pairs, semaphores):
+    copies = [pltpu.make_async_copy(*pair, semaphores.at[i]) for i, pair in enumerate(pairs)]
+    for copy in copies:
+        copy.start()
+    return copies
 
 
 def ready(*values):
@@ -137,10 +144,9 @@
 
 def prepare(
     plan, groups,
-    route_ref, slot_ref, delta_ref, input_ref, shared_ref,
-    out_ref, shared_out_ref,
+    route_ref, slot_ref, delta_ref, input_ref,
+    out_ref,
 ):
-    shared_out_ref[...] = shared_ref[...]
     place, place_flat = places(route_ref, slot_ref)
     slots, rows, dests = plan.group * plan.slots, plan.group * plan.packed, plan.group
     wide_expand = plan.expand(*plan.wide_index(slots))
@@ -149,10 +155,13 @@
     packed_expand = plan.expand(dest, at)
     _, block, at = plan.packed_index(LANES)
     packed_rank = plan.rank(at)
-    for g in range(groups):
-        value = dot(packed_expand, place[g * slots : (g + 1) * slots])
-        chosen = one_hot(value == packed_rank)
-        picked = by_block(plan, dot(chosen, input_ref[...]), block)
+    low, odd = block < 2, block % 2 == 1
+    halves = jnp.concatenate([input_ref[:, : 2 * LANES], input_ref[:, 2 * LANES :]], axis=0)
+    for g in range(groups):
+        hit = dot(packed_expand, place[g * slots : (g + 1) * slots]) == packed_rank
+        chosen = jnp.concatenate([one_hot(hit & low), one_hot(hit & ~low)], axis=1)
+        picked = dot(chosen, halves)
+        picked = jnp.where(odd, picked[:, LANES:], picked[:, :LANES]).astype(BF16)
         out_ref[g * dests : (g + 1) * dests, : plan.packed, :] = picked.reshape(dests, plan.packed, LANES)
         value = dot(wide_expand, place_flat[g * slots : (g + 1) * slots])
         picked = dot(one_hot(value == wide_rank), delta_ref[...]).astype(BF16)
@@ -225,17 +234,27 @@
             part_ref[y, rows + step * BLOCK : rows + (step + 1) * BLOCK, :] = ref[...]
 
 
-def project(plan, groups, index_ref, *refs):
-    delta_refs, (weight_ref, out_ref, kept_at, value_ref, sorted_ref, sems) = refs[:-6], refs[-6:]
-    copies = [pltpu.make_async_copy(ref, kept_at.at[m], sems.at[m]) for m, ref in enumerate(delta_refs)]
+def project_early(plan, late, index_ref, *refs):
+    delta_refs, (weight_ref, out_ref, late_ref, kept_at, sorted_ref, sems) = refs[:-6], refs[-6:]
+    copies = started([(ref, kept_at.at[m]) for m, ref in enumerate(delta_refs)], sems)
+    count = len(delta_refs)
+    for s in range(plan.slots):
+        for m in range(count):
+            sorted_ref[s, m * LANES : (m + 1) * LANES, :] = weight_ref[s, place_of(index_ref, m, LANES), :]
+        for m in range(late):
+            late_ref[s, m * LANES : (m + 1) * LANES, :] = weight_ref[s, place_of(index_ref, count + m, LANES), :]
+        out_ref[s] = dot(jnp.concatenate([ref[s] for ref in delta_refs], axis=1), sorted_ref[s])
     for copy in copies:
-        copy.start()
+        copy.wait()
+
+
+def project(plan, groups, *refs):
+    delta_refs, (weight_ref, early_ref, out_ref, kept_at, value_ref, sems) = refs[:-6], refs[-6:]
+    copies = started([(ref, kept_at.at[m]) for m, ref in enumerate(delta_refs)], sems)
     rows, part = plan.group * plan.packed, plan.slot_rows
     for s in range(plan.slots):
-        for m in range(len(delta_refs)):
-            sorted_ref[s, m * LANES : (m + 1) * LANES, :] = weight_ref[s, place_of(index_ref, m, LANES), :]
-        delta = jnp.concatenate([ref[s] for ref in delta_refs], axis=1)
-        value_ref[s] = dot(delta, sorted_ref[s]).astype(BF16)
+        value = dot(jnp.concatenate([ref[s] for ref in delta_refs], axis=1), weight_ref[s])
+        value_ref[s] = (early_ref[s] + value).astype(BF16)
     unsort = plan.packed_from_slot()
     block = plan.packed_index(LANES)[1]
     for g in range(groups):
@@ -245,7 +264,7 @@
         copy.wait()
 
 
-def weight_gradient(plan, groups, index_ref, delta_ref, input_ref, out_ref, sorted_ref):
+def weight_gradient(plan, groups, index_ref, early_ref, late_ref, input_ref, out_ref, sorted_ref):
     rows, part = plan.group * plan.packed, plan.slot_rows
     unsort = plan.packed_from_slot()
     mask = plan.block_mask()
@@ -255,9 +274,10 @@
         for s in range(plan.slots):
             sorted_ref[s, g * part : (g + 1) * part, :] = wide[s * part : (s + 1) * part]
     for s in range(plan.slots):
-        delta = jnp.concatenate([delta_ref[m, s] for m in range(delta_ref.shape[0])], axis=1)
+        parts = [ref[m, s] for ref in (early_ref, late_ref) for m in range(ref.shape[0])]
+        delta = jnp.concatenate(parts, axis=1)
         value = dot(delta, sorted_ref[s], ((0,), (0,))).astype(BF16)
-        for m in range(delta_ref.shape[0]):
+        for m in range(len(parts)):
             out_ref[s, place_of(index_ref, m, LANES), :] = value[m * LANES : (m + 1) * LANES]
 
 
@@ -320,22 +340,18 @@
     def exchanged(block, groups=None):
         return lax.all_to_all(block, "dp", split_axis=0, concat_axis=0, axis_index_groups=groups, tiled=True)
 
-    sent, own_delta = call(
+    sent = call(
         functools.partial(prepare, plan, groups),
-        (
-            jax.ShapeDtypeStruct((dp_count, plan.packed + plan.padded, LANES), BF16),
-            jax.ShapeDtypeStruct(shared_delta.shape, BF16),
-        ),
+        jax.ShapeDtypeStruct((dp_count, plan.packed + plan.padded, LANES), BF16),
         routing.T,
         slot_expert.reshape(1, -1),
         routed_delta.reshape(tokens * top, LANES),
         layer_input,
-        shared_delta,
     )
     sent, other_delta = ready(sent, moved(shared_delta, "tensor", other_z))
     arrived = exchanged(sent)
 
-    pair = (own_delta, other_delta)
+    pair = (shared_delta, other_delta)
     shared_all, keep, give, own_weight = call(
         shared_partial,
         (
@@ -381,16 +397,33 @@
         to_left(partner_right),
     ]
     parts = exchanged(parts, along_y)
-    outgoing, kept_deltas = call(
+    early, late = deltas[:6], deltas[6:]
+    early_rows, late_weight, kept_early = call(
+        functools.partial(project_early, plan, len(late)),
+        (
+            jax.ShapeDtypeStruct((slots, dp_count * MOST, columns), F32),
+            jax.ShapeDtypeStruct((slots, len(late) * LANES, columns), BF16),
+            jax.ShapeDtypeStruct((len(early),) + own_deltas.shape, BF16),
+        ),
+        *early,
+        expert_weight,
+        index=(holders,),
+        scratch=[
+            pltpu.VMEM((slots, len(early) * LANES, columns), BF16),
+            pltpu.SemaphoreType.DMA((len(early),)),
+        ],
+        out_specs=(IN_VMEM, IN_VMEM, ANYWHERE),
+    )
+    outgoing, kept_late = call(
         functools.partial(project, plan, groups),
         (
             jax.ShapeDtypeStruct((packed_rows, LANES), BF16),
-            jax.ShapeDtypeStruct((len(deltas),) + own_deltas.shape, BF16),
-        ),
-        *deltas,
-        expert_weight,
-        index=(holders,),
-        scratch=[value_rows, pltpu.VMEM(expert_weight.shape, BF16), pltpu.SemaphoreType.DMA((len(deltas),))],
+            jax.ShapeDtypeStruct((len(late),) + own_deltas.shape, BF16),
+        ),
+        *late,
+        late_weight,
+        early_rows,
+        scratch=[value_rows, pltpu.SemaphoreType.DMA((len(late),))],
         out_specs=(IN_VMEM, ANYWHERE),
     )
 
@@ -398,7 +431,8 @@
     expert_gradient = call(
         functools.partial(weight_gradient, plan, groups),
         jax.ShapeDtypeStruct(expert_weight.shape, BF16),
-        kept_deltas,
+        kept_early,
+        kept_late,
         arrived,
         index=(holders,),
         scratch=[value_rows],

time: 183 us -> 182 us (level)
  waiting for transfers between devices: 26 us -> 20 us
  local copies, waits for them, and re-layouts: 18.1 us -> 20.3 us
  starting transfers between devices: 115 us -> 117 us
    ppermute x22, waiting for transfers between devices: 26 us -> 20 us  [moved(): lax.ppermute(block, axis, [(i, target(i)) for i in range(lax.axis_size(ax...]
    unnamed x46 -> x52, local copies, waits for them, and re-layouts: 18 us -> 20.2 us
    pallas_call x8 -> x9, Pallas kernels: 21.7 us -> 22 us  [call(): pl.pallas_call(run, out_shape=outs, in_specs=[IN_SMEM] * len(index) + [IN...]
where the time goes in v3:
time: 182 us; the launch traced here: 180 us
  starting transfers between devices  117 us (64%)
  Pallas kernels  22 us (12%)
  local copies, waits for them, and re-layouts  20.3 us (11%)
  waiting for transfers between devices  20 us (11%)
    ppermute x22, starting transfers between devices, moved(): lax.ppermute(block, axis, [(i, target(i)) for i in range(lax.axis_size(ax...  79.6 us
    all_to_all x3, starting transfers between devices, exchanged(): lax.all_to_all(block, 'dp', split_axis=0, concat_axis=0, axis_index_group...  37.2 us
    pallas_call x9, Pallas kernels, call(): pl.pallas_call(run, out_shape=outs, in_specs=[IN_SMEM] * len(index) + [IN...  22 us
    unnamed x52, local copies, waits for them, and re-layouts  20.2 us
    ppermute x22, waiting for transfers between devices, moved(): lax.ppermute(block, axis, [(i, target(i)) for i in range(lax.axis_size(ax...  20 us
  transfers between devices with their start and end apart: 25, of which 7 were waited for; matrix products, arithmetic and copies ran while one was open for 0% of the time, Pallas kernels for 11%

profile of v3, /device:TPU:1, one launch (start us, length us, event | category | flops | bytes accessed | tf_op | source)
XLA Modules:
  0.0 180.4 jit_solution(11700823378601401233)
XLA Ops:
  0.6 4.8 %collective-permute-start = (bf16[16,1024]{1,0:T(8,128)(2,1)}, bf16[16,1024]{1,0:T(8,128)(2,1)S(1)}, u32[]{:S(2)}, u32[]{:S(2)}) collective-permute-start(bf16[16,1024]{1,0:T(8,128)(2,1)} %refs_2_.1), channel_id=1, source_target_pairs={{0,4},{1,5},{2,6},{3,7},{4,0},{5,1},{6,2},{7,3},{8,12},{9,13},{10,... | collective-permute-start | bytes 98312 | tf_op jit(solution)/shard_map/ppermute | solution.py:297
  8.7 4.9 %shard_map.94.refs_0_ = bf16[64,104,128]{2,1,0:T(8,128)(2,1)S(1)} custom-call(s32[8,128]{1,0:T(8,128)S(1)} %bitcast.18, s32[1,128]{1,0:T(1,128)S(1)} %bitcast.20, bf16[1024,128]{1,0:T(8,128)(2,1)S(1)} %bitcast.17, bf16[128,512]{1,0:T(8,128)(2,1)S(1)} %copy-done.15), custom_call_target="tpu_custom_call" | custom-call | tf_op jit(solution)/shard_map/pallas_call | solution.py:83
  15.4 16.3 %all-to-all-start = ((bf16[64,104,128]{2,1,0:T(8,128)(2,1)}), bf16[64,104,128]{2,1,0:T(8,128)(2,1)S(1)}, u32[]{:S(2)}, u32[]{:S(2)}) async-start(bf16[64,104,128]{2,1,0:T(8,128)(2,1)} %get-tuple-element.25), calls=%async_computation | async-start | bytes 3407872 | tf_op jit(solution)/shard_map/all_to_all | solution.py:341
  31.8 3.1 %collective-permute-start.1 = (bf16[16,1024]{1,0:T(8,128)(2,1)S(1)}, bf16[16,1024]{1,0:T(8,128)(2,1)S(1)}, u32[]{:S(2)}, u32[]{:S(2)}) collective-permute-start(bf16[16,1024]{1,0:T(8,128)(2,1)S(1)} %copy-done.20), channel_id=1, source_target_pairs={{0,1},{1,2},{2,3},{3,0},{4,5},{5,6},{6,7},{7,4},{8,9},{9,10},{10,1... | collective-permute-start | bytes 98312 | tf_op jit(solution)/shard_map/ppermute | solution.py:297
  34.9 3.4 %collective-permute-start.3 = (bf16[16,1024]{1,0:T(8,128)(2,1)S(1)}, bf16[16,1024]{1,0:T(8,128)(2,1)S(1)}, u32[]{:S(2)}, u32[]{:S(2)}) collective-permute-start(bf16[16,1024]{1,0:T(8,128)(2,1)S(1)} %copy-done.20), channel_id=1, source_target_pairs={{0,3},{1,0},{2,1},{3,2},{4,7},{5,4},{6,5},{7,6},{8,11},{9,8},{10,9... | collective-permute-start | bytes 98312 | tf_op jit(solution)/shard_map/ppermute | solution.py:297
  38.3 3.4 %collective-permute-start.5 = (bf16[16,1024]{1,0:T(8,128)(2,1)S(1)}, bf16[16,1024]{1,0:T(8,128)(2,1)S(1)}, u32[]{:S(2)}, u32[]{:S(2)}) collective-permute-start(bf16[16,1024]{1,0:T(8,128)(2,1)S(1)} %copy-done.20), channel_id=1, source_target_pairs={{0,2},{1,3},{2,0},{3,1},{4,6},{5,7},{6,4},{7,5},{8,10},{9,11},{10,... | collective-permute-start | bytes 98312 | tf_op jit(solution)/shard_map/ppermute | solution.py:297
  41.7 2.2 %collective-permute-start.2 = (bf16[16,1024]{1,0:T(8,128)(2,1)S(1)}, bf16[16,1024]{1,0:T(8,128)(2,1)S(1)}, u32[]{:S(2)}, u32[]{:S(2)}) collective-permute-start(bf16[16,1024]{1,0:T(8,128)(2,1)S(1)} %copy-done.19), channel_id=1, source_target_pairs={{0,1},{1,2},{2,3},{3,0},{4,5},{5,6},{6,7},{7,4},{8,9},{9,10},{10,1... | collective-permute-start | bytes 98312 | tf_op jit(solution)/shard_map/ppermute | solution.py:297
  44.0 4.3 %collective-permute-start.4 = (bf16[16,1024]{1,0:T(8,128)(2,1)S(1)}, bf16[16,1024]{1,0:T(8,128)(2,1)S(1)}, u32[]{:S(2)}, u32[]{:S(2)}) collective-permute-start(bf16[16,1024]{1,0:T(8,128)(2,1)S(1)} %copy-done.19), channel_id=1, source_target_pairs={{0,3},{1,0},{2,1},{3,2},{4,7},{5,4},{6,5},{7,6},{8,11},{9,8},{10,9... | collective-permute-start | bytes 98312 | tf_op jit(solution)/shard_map/ppermute | solution.py:297
  50.6 4.1 %collective-permute-done.6.refs_9_ = bf16[16,1024]{1,0:T(8,128)(2,1)S(1)} collective-permute-done((bf16[16,1024]{1,0:T(8,128)(2,1)S(1)}, bf16[16,1024]{1,0:T(8,128)(2,1)S(1)}, u32[]{:S(2)}, u32[]{:S(2)}) %collective-permute-start.6) | collective-permute-done | bytes 32800 | tf_op jit(solution)/shard_map/ppermute | solution.py:297
  55.9 4.6 %collective-permute-start.7 = (f32[512,512]{1,0:T(8,128)S(1)}, f32[512,512]{1,0:T(8,128)S(1)}, u32[]{:S(2)}, u32[]{:S(2)}) collective-permute-start(f32[512,512]{1,0:T(8,128)S(1)} %get-tuple-element.28), channel_id=1, source_target_pairs={{0,8},{8,0},{16,24},{24,16},{32,40},{40,32},{48,56},{56,48},{64,72... | collective-permute-start | bytes 3145736 | tf_op jit(solution)/shard_map/ppermute | solution.py:297
  60.5 5.3 %collective-permute-start.10 = (bf16[16,512]{1,0:T(8,128)(2,1)S(1)}, bf16[16,512]{1,0:T(8,128)(2,1)S(1)}, u32[]{:S(2)}, u32[]{:S(2)}) collective-permute-start(bf16[16,512]{1,0:T(8,128)(2,1)S(1)} %get-tuple-element.29.refs_3_), channel_id=1, source_target_pairs={{0,48},{8,56},{16,0},{24,8},{32,16},{40,24},{48,32},{56,40},{64,11... | collective-permute-start | bytes 49160 | tf_op jit(solution)/shard_map/ppermute | solution.py:297
  67.8 6.1 %collective-permute-start.9 = (bf16[16,512]{1,0:T(8,128)(2,1)S(1)}, bf16[16,512]{1,0:T(8,128)(2,1)S(1)}, u32[]{:S(2)}, u32[]{:S(2)}) collective-permute-start(bf16[16,512]{1,0:T(8,128)(2,1)S(1)} %get-tuple-element.29.refs_3_), channel_id=1, source_target_pairs={{0,32},{8,40},{16,48},{24,56},{32,0},{40,8},{48,16},{56,24},{64,96... | collective-permute-start | bytes 49160 | tf_op jit(solution)/shard_map/ppermute | solution.py:297
  73.8 2.3 %collective-permute-done.9.refs_5_ = bf16[16,512]{1,0:T(8,128)(2,1)S(1)} collective-permute-done((bf16[16,512]{1,0:T(8,128)(2,1)S(1)}, bf16[16,512]{1,0:T(8,128)(2,1)S(1)}, u32[]{:S(2)}, u32[]{:S(2)}) %collective-permute-start.9) | collective-permute-done | bytes 16416 | tf_op jit(solution)/shard_map/ppermute | solution.py:297
  79.8 6.5 %all-to-all-start.2 = ((bf16[8,128,512]{2,1,0:T(8,128)(2,1)}), bf16[8,128,512]{2,1,0:T(8,128)(2,1)S(1)}, u32[]{:S(2)}, u32[]{:S(2)}) async-start(bf16[8,128,512]{2,1,0:T(8,128)(2,1)} %copy-done.10), calls=%async_computation.2 | async-start | bytes 2097152 | tf_op jit(solution)/shard_map/all_to_all | solution.py:341
  86.3 2.2 %collective-permute-start.13 = (bf16[2,640,128]{2,1,0:T(8,128)(2,1)S(1)}, bf16[2,640,128]{2,1,0:T(8,128)(2,1)S(1)}, u32[]{:S(2)}, u32[]{:S(2)}) collective-permute-start(bf16[2,640,128]{2,1,0:T(8,128)(2,1)S(1)} %get-tuple-element.30.refs_1_), channel_id=1, source_target_pairs={{0,4},{1,5},{2,6},{3,7},{4,0},{5,1},{6,2},{7,3},{8,12},{9,13},{10,... | collective-permute-start | bytes 983048 | tf_op jit(solution)/shard_map/ppermute | solution.py:297
  88.5 2.6 %collective-permute-start.11 = (bf16[2,640,128]{2,1,0:T(8,128)(2,1)S(1)}, bf16[2,640,128]{2,1,0:T(8,128)(2,1)S(1)}, u32[]{:S(2)}, u32[]{:S(2)}) collective-permute-start(bf16[2,640,128]{2,1,0:T(8,128)(2,1)S(1)} %get-tuple-element.30.refs_1_), channel_id=1, source_target_pairs={{0,1},{1,2},{2,3},{3,0},{4,5},{5,6},{6,7},{7,4},{8,9},{9,10},{10,1... | collective-permute-start | bytes 983048 | tf_op jit(solution)/shard_map/ppermute | solution.py:297
  91.0 4.6 %collective-permute-done.13.refs_2_ = bf16[2,640,128]{2,1,0:T(8,128)(2,1)S(1)} collective-permute-done((bf16[2,640,128]{2,1,0:T(8,128)(2,1)S(1)}, bf16[2,640,128]{2,1,0:T(8,128)(2,1)S(1)}, u32[]{:S(2)}, u32[]{:S(2)}) %collective-permute-start.13) | collective-permute-done | bytes 327712 | tf_op jit(solution)/shard_map/ppermute | solution.py:297
  95.7 4.9 %collective-permute-start.14 = (bf16[2,640,128]{2,1,0:T(8,128)(2,1)S(1)}, bf16[2,640,128]{2,1,0:T(8,128)(2,1)S(1)}, u32[]{:S(2)}, u32[]{:S(2)}) collective-permute-start(bf16[2,640,128]{2,1,0:T(8,128)(2,1)S(1)} %collective-permute-done.13.refs_2_), channel_id=1, source_target_pairs={{0,3},{1,0},{2,1},{3,2},{4,7},{5,4},{6,5},{7,6},{8,11},{9,8},{10,9... | collective-permute-start | bytes 983048 | tf_op jit(solution)/shard_map/ppermute | solution.py:297
  100.5 2.3 %collective-permute-start.17 = (bf16[2,640,128]{2,1,0:T(8,128)(2,1)S(1)}, bf16[2,640,128]{2,1,0:T(8,128)(2,1)S(1)}, u32[]{:S(2)}, u32[]{:S(2)}) collective-permute-start(bf16[2,640,128]{2,1,0:T(8,128)(2,1)S(1)} %get-tuple-element.30.refs_1_), channel_id=1, source_target_pairs={{0,3},{1,0},{2,1},{3,2},{4,7},{5,4},{6,5},{7,6},{8,11},{9,8},{10,9... | collective-permute-start | bytes 983048 | tf_op jit(solution)/shard_map/ppermute | solution.py:297
  102.8 3.0 %collective-permute-start.16 = (bf16[2,640,128]{2,1,0:T(8,128)(2,1)S(1)}, bf16[2,640,128]{2,1,0:T(8,128)(2,1)S(1)}, u32[]{:S(2)}, u32[]{:S(2)}) collective-permute-start(bf16[2,640,128]{2,1,0:T(8,128)(2,1)S(1)} %collective-permute-done.13.refs_2_), channel_id=1, source_target_pairs={{0,1},{1,2},{2,3},{3,0},{4,5},{5,6},{6,7},{7,4},{8,9},{9,10},{10,1... | collective-permute-start | bytes 983048 | tf_op jit(solution)/shard_map/ppermute | solution.py:297
  107.8 4.6 %collective-permute-start.15 = (bf16[2,640,128]{2,1,0:T(8,128)(2,1)S(1)}, bf16[2,640,128]{2,1,0:T(8,128)(2,1)S(1)}, u32[]{:S(2)}, u32[]{:S(2)}) collective-permute-start(bf16[2,640,128]{2,1,0:T(8,128)(2,1)S(1)} %collective-permute-done.14.refs_6_), channel_id=1, source_target_pairs={{0,3},{1,0},{2,1},{3,2},{4,7},{5,4},{6,5},{7,6},{8,11},{9,8},{10,9... | collective-permute-start | bytes 983048 | tf_op jit(solution)/shard_map/ppermute | solution.py:297
  114.5 2.4 %shard_map.98 = (f32[2,640,512]{2,1,0:T(8,128)S(1)}, bf16[2,256,512]{2,1,0:T(8,128)(2,1)S(1)}, bf16[6,2,640,128]{3,2,1,0:T(8,128)(2,1)S(1)}) custom-call(s32[8]{0:T(128)S(1)} %stack.47.refs_1_.refs_0_, bf16[2,640,128]{2,1,0:T(8,128)(2,1)S(1)} %get-tuple-element.30.refs_1_, bf16[2,640,128]{2,1,0:T(8,128)(2,1)S(1)} %collective-permute-done.13.refs_2_, ...), custom_call_target="tpu_custom_call" | custom-call | tf_op jit(solution)/shard_map/pallas_call | solution.py:83
  119.9 2.7 %shard_map.99 = (bf16[5120,128]{1,0:T(8,128)(2,1)S(1)}, bf16[2,2,640,128]{3,2,1,0:T(8,128)(2,1)S(1)}) custom-call(bf16[2,640,128]{2,1,0:T(8,128)(2,1)S(1)} %collective-permute-done.12.refs_0_, bf16[2,640,128]{2,1,0:T(8,128)(2,1)S(1)} %collective-permute-done.15.refs_1_, bf16[2,256,512]{2,1,0:T(8,128)(2,1)S(1)} %get-tuple-element.31.refs_2_, ...), custom_call_target="tpu_custom_call" | custom-call | tf_op jit(solution)/shard_map/pallas_call | solution.py:83
  125.5 14.4 %all-to-all-start.1 = ((bf16[64,80,128]{2,1,0:T(8,128)(2,1)}), bf16[64,80,128]{2,1,0:T(8,128)(2,1)S(1)}, u32[]{:S(2)}, u32[]{:S(2)}) async-start(bf16[64,80,128]{2,1,0:T(8,128)(2,1)} %bitcast.16), calls=%async_computation.1 | async-start | bytes 2621440 | tf_op jit(solution)/shard_map/all_to_all | solution.py:341
  141.8 2.4 %collective-permute-start.18 = (bf16[512,512]{1,0:T(8,128)(2,1)S(1)}, bf16[512,512]{1,0:T(8,128)(2,1)S(1)}, u32[]{:S(2)}, u32[]{:S(2)}) collective-permute-start(bf16[512,512]{1,0:T(8,128)(2,1)S(1)} %get-tuple-element.36), channel_id=1, source_target_pairs={{0,8},{8,0},{16,24},{24,16},{32,40},{40,32},{48,56},{56,48},{64,72... | collective-permute-start | bytes 1572872 | tf_op jit(solution)/shard_map/ppermute | solution.py:297
  146.8 5.4 %shard_map.101.refs_5_ = bf16[2,1024,512]{2,1,0:T(8,128)(2,1)} custom-call(s32[8]{0:T(128)S(1)} %stack.47.refs_1_.refs_0_, bf16[6,2,640,128]{3,2,1,0:T(8,128)(2,1)S(1)} %copy-done.6, bf16[2,2,640,128]{3,2,1,0:T(8,128)(2,1)S(1)} %copy-done.14, bf16[64,104,128]{2,1,0:T(8,128)(2,1)S(1)} %all-to-all-done.refs_0_.refs_3_), custom_call_target="tpu_custom_call" | custom-call | tf_op jit(solution)/shard_map/pallas_call | solution.py:83
  152.2 4.2 %collective-permute-start.19 = (f32[16,512]{1,0:T(8,128)S(1)}, f32[16,512]{1,0:T(8,128)S(1)}, u32[]{:S(2)}, u32[]{:S(2)}) collective-permute-start(f32[16,512]{1,0:T(8,128)S(1)} %get-tuple-element.42), channel_id=1, source_target_pairs={{0,16},{8,24},{16,32},{24,40},{32,48},{40,56},{48,0},{56,8},{64,80... | collective-permute-start | bytes 98312 | tf_op jit(solution)/shard_map/ppermute | solution.py:297
  156.4 5.2 %collective-permute-start.20 = (f32[16,512]{1,0:T(8,128)S(1)}, f32[16,512]{1,0:T(8,128)S(1)}, u32[]{:S(2)}, u32[]{:S(2)}) collective-permute-start(f32[16,512]{1,0:T(8,128)S(1)} %get-tuple-element.43), channel_id=1, source_target_pairs={{0,32},{8,40},{16,48},{24,56},{32,0},{40,8},{48,16},{56,24},{64,96... | collective-permute-start | bytes 98312 | tf_op jit(solution)/shard_map/ppermute | solution.py:297
  161.7 5.2 %collective-permute-start.21 = (f32[16,512]{1,0:T(8,128)S(1)}, f32[16,512]{1,0:T(8,128)S(1)}, u32[]{:S(2)}, u32[]{:S(2)}) collective-permute-start(f32[16,512]{1,0:T(8,128)S(1)} %get-tuple-element.44), channel_id=1, source_target_pairs={{0,48},{8,56},{16,0},{24,8},{32,16},{40,24},{48,32},{56,40},{64,11... | collective-permute-start | bytes 98312 | tf_op jit(solution)/shard_map/ppermute | solution.py:297
  167.0 2.3 %shard_map.102 = (f32[128,512]{1,0:T(8,128)S(1)}, bf16[5120,128]{1,0:T(8,128)(2,1)S(1)}) custom-call(s32[2]{0:T(128)S(1)} %pad_add_fusion.refs_0_, bf16[128,1024]{1,0:T(8,128)(2,1)S(1)} %get-tuple-element.34.refs_1_, bf16[1024,512]{1,0:T(8,128)(2,1)S(1)} %pad_maximum_fusion.refs_2_, s32[8,128]{1,0:T(8,128)S(1)} %bitcast.19, s32[1,128]{1,0:T(1,128)S(1)} %bitcast.21, ...), custom_call_target="tpu_custom_call" | custom-call | tf_op jit(solution)/shard_map/pallas_call | solution.py:83
  170.3 4.3 %collective-permute-done.19.refs_4_ = f32[16,512]{1,0:T(8,128)S(1)} collective-permute-done((f32[16,512]{1,0:T(8,128)S(1)}, f32[16,512]{1,0:T(8,128)S(1)}, u32[]{:S(2)}, u32[]{:S(2)}) %collective-permute-start.19) | collective-permute-done | bytes 32800 | tf_op jit(solution)/shard_map/ppermute | solution.py:297
  174.6 2.4 %collective-permute-done.20.refs_5_ = f32[16,512]{1,0:T(8,128)S(1)} collective-permute-done((f32[16,512]{1,0:T(8,128)S(1)}, f32[16,512]{1,0:T(8,128)S(1)}, u32[]{:S(2)}, u32[]{:S(2)}) %collective-permute-start.20) | collective-permute-done | bytes 32800 | tf_op jit(solution)/shard_map/ppermute | solution.py:297
  (83 shorter events, 32.9 us)
Async XLA Ops:
  0.6 14.2 %collective-permute-start = (bf16[16,1024]{1,0:T(8,128)(2,1)}, bf16[16,1024]{1,0:T(8,128)(2,1)S(1)}, u32[]{:S(2)}, u32[]{:S(2)}) collective-permute-start(bf16[16,1024]{1,0:T(8,128)(2,1)} %refs_2_.1), channel_id=1, source_target_pairs={{0,4},{1,5},{2,6},{3,7},{4,0},{5,1},{6,2},{7,3},{8,12},{9,13},{10,... | collective-permute-start | bytes 98312 | tf_op jit(solution)/shard_map/ppermute | solution.py:297
  15.4 16.4 %copy-start.20 = (bf16[16,1024]{1,0:T(8,128)(2,1)S(1)}, bf16[16,1024]{1,0:T(8,128)(2,1)}, u32[]{:S(2)}) copy-start(bf16[16,1024]{1,0:T(8,128)(2,1)} %refs_2_.1) | copy-start | bytes 98308
  15.4 26.3 %copy-start.19 = (bf16[16,1024]{1,0:T(8,128)(2,1)S(1)}, bf16[16,1024]{1,0:T(8,128)(2,1)}, u32[]{:S(2)}) copy-start(bf16[16,1024]{1,0:T(8,128)(2,1)} %get-tuple-element.26.refs_3_) | copy-start | bytes 98308
  15.4 39.3 %copy-start.16 = (bf16[128,512]{1,0:T(8,128)(2,1)S(1)}, bf16[128,512]{1,0:T(8,128)(2,1)}, u32[]{:S(2)}) copy-start(bf16[128,512]{1,0:T(8,128)(2,1)} %refs_10_.1) | copy-start | bytes 393220
  15.4 39.3 %copy-start.23 = (bf16[16,512]{1,0:T(8,128)(2,1)S(1)}, bf16[16,512]{1,0:T(8,128)(2,1)}, u32[]{:S(2)}) copy-start(bf16[16,512]{1,0:T(8,128)(2,1)} %refs_11_.1) | copy-start | bytes 49156
  15.4 61.8 %all-to-all-start = ((bf16[64,104,128]{2,1,0:T(8,128)(2,1)}), bf16[64,104,128]{2,1,0:T(8,128)(2,1)S(1)}, u32[]{:S(2)}, u32[]{:S(2)}) async-start(bf16[64,104,128]{2,1,0:T(8,128)(2,1)} %get-tuple-element.25), calls=%async_computation | async-start | bytes 3407872 | tf_op jit(solution)/shard_map/all_to_all | solution.py:341
  31.8 16.5 %collective-permute-start.1 = (bf16[16,1024]{1,0:T(8,128)(2,1)S(1)}, bf16[16,1024]{1,0:T(8,128)(2,1)S(1)}, u32[]{:S(2)}, u32[]{:S(2)}) collective-permute-start(bf16[16,1024]{1,0:T(8,128)(2,1)S(1)} %copy-done.20), channel_id=1, source_target_pairs={{0,1},{1,2},{2,3},{3,0},{4,5},{5,6},{6,7},{7,4},{8,9},{9,10},{10,1... | collective-permute-start | bytes 98312 | tf_op jit(solution)/shard_map/ppermute | solution.py:297
  34.9 15.7 %collective-permute-start.3 = (bf16[16,1024]{1,0:T(8,128)(2,1)S(1)}, bf16[16,1024]{1,0:T(8,128)(2,1)S(1)}, u32[]{:S(2)}, u32[]{:S(2)}) collective-permute-start(bf16[16,1024]{1,0:T(8,128)(2,1)S(1)} %copy-done.20), channel_id=1, source_target_pairs={{0,3},{1,0},{2,1},{3,2},{4,7},{5,4},{6,5},{7,6},{8,11},{9,8},{10,9... | collective-permute-start | bytes 98312 | tf_op jit(solution)/shard_map/ppermute | solution.py:297
  38.3 12.3 %collective-permute-start.5 = (bf16[16,1024]{1,0:T(8,128)(2,1)S(1)}, bf16[16,1024]{1,0:T(8,128)(2,1)S(1)}, u32[]{:S(2)}, u32[]{:S(2)}) collective-permute-start(bf16[16,1024]{1,0:T(8,128)(2,1)S(1)} %copy-done.20), channel_id=1, source_target_pairs={{0,2},{1,3},{2,0},{3,1},{4,6},{5,7},{6,4},{7,5},{8,10},{9,11},{10,... | collective-permute-start | bytes 98312 | tf_op jit(solution)/shard_map/ppermute | solution.py:297
  41.7 8.8 %collective-permute-start.2 = (bf16[16,1024]{1,0:T(8,128)(2,1)S(1)}, bf16[16,1024]{1,0:T(8,128)(2,1)S(1)}, u32[]{:S(2)}, u32[]{:S(2)}) collective-permute-start(bf16[16,1024]{1,0:T(8,128)(2,1)S(1)} %copy-done.19), channel_id=1, source_target_pairs={{0,1},{1,2},{2,3},{3,0},{4,5},{5,6},{6,7},{7,4},{8,9},{9,10},{10,1... | collective-permute-start | bytes 98312 | tf_op jit(solution)/shard_map/ppermute | solution.py:297
  44.0 6.6 %collective-permute-start.4 = (bf16[16,1024]{1,0:T(8,128)(2,1)S(1)}, bf16[16,1024]{1,0:T(8,128)(2,1)S(1)}, u32[]{:S(2)}, u32[]{:S(2)}) collective-permute-start(bf16[16,1024]{1,0:T(8,128)(2,1)S(1)} %copy-done.19), channel_id=1, source_target_pairs={{0,3},{1,0},{2,1},{3,2},{4,7},{5,4},{6,5},{7,6},{8,11},{9,8},{10,9... | collective-permute-start | bytes 98312 | tf_op jit(solution)/shard_map/ppermute | solution.py:297
  48.3 6.5 %collective-permute-start.6 = (bf16[16,1024]{1,0:T(8,128)(2,1)S(1)}, bf16[16,1024]{1,0:T(8,128)(2,1)S(1)}, u32[]{:S(2)}, u32[]{:S(2)}) collective-permute-start(bf16[16,1024]{1,0:T(8,128)(2,1)S(1)} %copy-done.19), channel_id=1, source_target_pairs={{0,2},{1,3},{2,0},{3,1},{4,6},{5,7},{6,4},{7,5},{8,10},{9,11},{10,... | collective-permute-start | bytes 98312 | tf_op jit(solution)/shard_map/ppermute | solution.py:297
  55.9 20.3 %collective-permute-start.7 = (f32[512,512]{1,0:T(8,128)S(1)}, f32[512,512]{1,0:T(8,128)S(1)}, u32[]{:S(2)}, u32[]{:S(2)}) collective-permute-start(f32[512,512]{1,0:T(8,128)S(1)} %get-tuple-element.28), channel_id=1, source_target_pairs={{0,8},{8,0},{16,24},{24,16},{32,40},{40,32},{48,56},{56,48},{64,72... | collective-permute-start | bytes 3145736 | tf_op jit(solution)/shard_map/ppermute | solution.py:297
  60.5 13.3 %collective-permute-start.10 = (bf16[16,512]{1,0:T(8,128)(2,1)S(1)}, bf16[16,512]{1,0:T(8,128)(2,1)S(1)}, u32[]{:S(2)}, u32[]{:S(2)}) collective-permute-start(bf16[16,512]{1,0:T(8,128)(2,1)S(1)} %get-tuple-element.29.refs_3_), channel_id=1, source_target_pairs={{0,48},{8,56},{16,0},{24,8},{32,16},{40,24},{48,32},{56,40},{64,11... | collective-permute-start | bytes 49160 | tf_op jit(solution)/shard_map/ppermute | solution.py:297
  65.8 8.0 %collective-permute-start.8 = (bf16[16,512]{1,0:T(8,128)(2,1)S(1)}, bf16[16,512]{1,0:T(8,128)(2,1)S(1)}, u32[]{:S(2)}, u32[]{:S(2)}) collective-permute-start(bf16[16,512]{1,0:T(8,128)(2,1)S(1)} %get-tuple-element.29.refs_3_), channel_id=1, source_target_pairs={{0,16},{8,24},{16,32},{24,40},{32,48},{40,56},{48,0},{56,8},{64,80... | collective-permute-start | bytes 49160 | tf_op jit(solution)/shard_map/ppermute | solution.py:297
  67.8 8.4 %collective-permute-start.9 = (bf16[16,512]{1,0:T(8,128)(2,1)S(1)}, bf16[16,512]{1,0:T(8,128)(2,1)S(1)}, u32[]{:S(2)}, u32[]{:S(2)}) collective-permute-start(bf16[16,512]{1,0:T(8,128)(2,1)S(1)} %get-tuple-element.29.refs_3_), channel_id=1, source_target_pairs={{0,32},{8,40},{16,48},{24,56},{32,0},{40,8},{48,16},{56,24},{64,96... | collective-permute-start | bytes 49160 | tf_op jit(solution)/shard_map/ppermute | solution.py:297
  79.8 44.7 %all-to-all-start.2 = ((bf16[8,128,512]{2,1,0:T(8,128)(2,1)}), bf16[8,128,512]{2,1,0:T(8,128)(2,1)S(1)}, u32[]{:S(2)}, u32[]{:S(2)}) async-start(bf16[8,128,512]{2,1,0:T(8,128)(2,1)} %copy-done.10), calls=%async_computation.2 | async-start | bytes 2097152 | tf_op jit(solution)/shard_map/all_to_all | solution.py:341
  86.3 9.4 %collective-permute-start.13 = (bf16[2,640,128]{2,1,0:T(8,128)(2,1)S(1)}, bf16[2,640,128]{2,1,0:T(8,128)(2,1)S(1)}, u32[]{:S(2)}, u32[]{:S(2)}) collective-permute-start(bf16[2,640,128]{2,1,0:T(8,128)(2,1)S(1)} %get-tuple-element.30.refs_1_), channel_id=1, source_target_pairs={{0,4},{1,5},{2,6},{3,7},{4,0},{5,1},{6,2},{7,3},{8,12},{9,13},{10,... | collective-permute-start | bytes 983048 | tf_op jit(solution)/shard_map/ppermute | solution.py:297
  88.5 17.4 %collective-permute-start.11 = (bf16[2,640,128]{2,1,0:T(8,128)(2,1)S(1)}, bf16[2,640,128]{2,1,0:T(8,128)(2,1)S(1)}, u32[]{:S(2)}, u32[]{:S(2)}) collective-permute-start(bf16[2,640,128]{2,1,0:T(8,128)(2,1)S(1)} %get-tuple-element.30.refs_1_), channel_id=1, source_target_pairs={{0,1},{1,2},{2,3},{3,0},{4,5},{5,6},{6,7},{7,4},{8,9},{9,10},{10,1... | collective-permute-start | bytes 983048 | tf_op jit(solution)/shard_map/ppermute | solution.py:297
  95.7 12.1 %collective-permute-start.14 = (bf16[2,640,128]{2,1,0:T(8,128)(2,1)S(1)}, bf16[2,640,128]{2,1,0:T(8,128)(2,1)S(1)}, u32[]{:S(2)}, u32[]{:S(2)}) collective-permute-start(bf16[2,640,128]{2,1,0:T(8,128)(2,1)S(1)} %collective-permute-done.13.refs_2_), channel_id=1, source_target_pairs={{0,3},{1,0},{2,1},{3,2},{4,7},{5,4},{6,5},{7,6},{8,11},{9,8},{10,9... | collective-permute-start | bytes 983048 | tf_op jit(solution)/shard_map/ppermute | solution.py:297
  100.5 12.3 %collective-permute-start.17 = (bf16[2,640,128]{2,1,0:T(8,128)(2,1)S(1)}, bf16[2,640,128]{2,1,0:T(8,128)(2,1)S(1)}, u32[]{:S(2)}, u32[]{:S(2)}) collective-permute-start(bf16[2,640,128]{2,1,0:T(8,128)(2,1)S(1)} %get-tuple-element.30.refs_1_), channel_id=1, source_target_pairs={{0,3},{1,0},{2,1},{3,2},{4,7},{5,4},{6,5},{7,6},{8,11},{9,8},{10,9... | collective-permute-start | bytes 983048 | tf_op jit(solution)/shard_map/ppermute | solution.py:297
  102.8 10.0 %collective-permute-start.16 = (bf16[2,640,128]{2,1,0:T(8,128)(2,1)S(1)}, bf16[2,640,128]{2,1,0:T(8,128)(2,1)S(1)}, u32[]{:S(2)}, u32[]{:S(2)}) collective-permute-start(bf16[2,640,128]{2,1,0:T(8,128)(2,1)S(1)} %collective-permute-done.13.refs_2_), channel_id=1, source_target_pairs={{0,1},{1,2},{2,3},{3,0},{4,5},{5,6},{6,7},{7,4},{8,9},{9,10},{10,1... | collective-permute-start | bytes 983048 | tf_op jit(solution)/shard_map/ppermute | solution.py:297
  105.9 14.0 %collective-permute-start.12 = (bf16[2,640,128]{2,1,0:T(8,128)(2,1)S(1)}, bf16[2,640,128]{2,1,0:T(8,128)(2,1)S(1)}, u32[]{:S(2)}, u32[]{:S(2)}) collective-permute-start(bf16[2,640,128]{2,1,0:T(8,128)(2,1)S(1)} %collective-permute-done.11.refs_3_), channel_id=1, source_target_pairs={{0,1},{1,2},{2,3},{3,0},{4,5},{5,6},{6,7},{7,4},{8,9},{9,10},{10,1... | collective-permute-start | bytes 983048 | tf_op jit(solution)/shard_map/ppermute | solution.py:297
  107.8 12.1 %collective-permute-start.15 = (bf16[2,640,128]{2,1,0:T(8,128)(2,1)S(1)}, bf16[2,640,128]{2,1,0:T(8,128)(2,1)S(1)}, u32[]{:S(2)}, u32[]{:S(2)}) collective-permute-start(bf16[2,640,128]{2,1,0:T(8,128)(2,1)S(1)} %collective-permute-done.14.refs_6_), channel_id=1, source_target_pairs={{0,3},{1,0},{2,1},{3,2},{4,7},{5,4},{6,5},{7,6},{8,11},{9,8},{10,9... | collective-permute-start | bytes 983048 | tf_op jit(solution)/shard_map/ppermute | solution.py:297
  125.5 51.6 %all-to-all-start.1 = ((bf16[64,80,128]{2,1,0:T(8,128)(2,1)}), bf16[64,80,128]{2,1,0:T(8,128)(2,1)S(1)}, u32[]{:S(2)}, u32[]{:S(2)}) async-start(bf16[64,80,128]{2,1,0:T(8,128)(2,1)} %bitcast.16), calls=%async_computation.1 | async-start | bytes 2621440 | tf_op jit(solution)/shard_map/all_to_all | solution.py:341
  141.8 25.1 %collective-permute-start.18 = (bf16[512,512]{1,0:T(8,128)(2,1)S(1)}, bf16[512,512]{1,0:T(8,128)(2,1)S(1)}, u32[]{:S(2)}, u32[]{:S(2)}) collective-permute-start(bf16[512,512]{1,0:T(8,128)(2,1)S(1)} %get-tuple-element.36), channel_id=1, source_target_pairs={{0,8},{8,0},{16,24},{24,16},{32,40},{40,32},{48,56},{56,48},{64,72... | collective-permute-start | bytes 1572872 | tf_op jit(solution)/shard_map/ppermute | solution.py:297
  152.2 14.7 %copy-start.1 = (bf16[2,1024,512]{2,1,0:T(8,128)(2,1)S(1)}, bf16[2,1024,512]{2,1,0:T(8,128)(2,1)}, u32[]{:S(2)}) copy-start(bf16[2,1024,512]{2,1,0:T(8,128)(2,1)} %shard_map.101.refs_5_) | copy-start | bytes 6291460
  152.2 14.7 %copy-start.22 = (s32[128,8]{0,1:T(8,128)S(1)}, s32[128,8]{0,1:T(8,128)}, u32[]{:S(2)}) copy-start(s32[128,8]{0,1:T(8,128)} %param.12) | copy-start | bytes 12292
  152.2 14.8 %copy-start.25 = (s32[128]{0:T(128)S(1)}, s32[128]{0:T(128)}, u32[]{:S(2)}) copy-start(s32[128]{0:T(128)} %param.13) | copy-start | bytes 1540
  152.2 22.4 %collective-permute-start.19 = (f32[16,512]{1,0:T(8,128)S(1)}, f32[16,512]{1,0:T(8,128)S(1)}, u32[]{:S(2)}, u32[]{:S(2)}) collective-permute-start(f32[16,512]{1,0:T(8,128)S(1)} %get-tuple-element.42), channel_id=1, source_target_pairs={{0,16},{8,24},{16,32},{24,40},{32,48},{40,56},{48,0},{56,8},{64,80... | collective-permute-start | bytes 98312 | tf_op jit(solution)/shard_map/ppermute | solution.py:297
  156.4 20.6 %collective-permute-start.20 = (f32[16,512]{1,0:T(8,128)S(1)}, f32[16,512]{1,0:T(8,128)S(1)}, u32[]{:S(2)}, u32[]{:S(2)}) collective-permute-start(f32[16,512]{1,0:T(8,128)S(1)} %get-tuple-element.43), channel_id=1, source_target_pairs={{0,32},{8,40},{16,48},{24,56},{32,0},{40,8},{48,16},{56,24},{64,96... | collective-permute-start | bytes 98312 | tf_op jit(solution)/shard_map/ppermute | solution.py:297
  161.7 15.4 %collective-permute-start.21 = (f32[16,512]{1,0:T(8,128)S(1)}, f32[16,512]{1,0:T(8,128)S(1)}, u32[]{:S(2)}, u32[]{:S(2)}) collective-permute-start(f32[16,512]{1,0:T(8,128)S(1)} %get-tuple-element.44), channel_id=1, source_target_pairs={{0,48},{8,56},{16,0},{24,8},{32,16},{40,24},{48,32},{56,40},{64,11... | collective-permute-start | bytes 98312 | tf_op jit(solution)/shard_map/ppermute | solution.py:297
  (19 other events, 20.2 us)

commit v4 on v3

--- a/solution.py
+++ b/solution.py
@@ -216,7 +216,7 @@
     out_ref[...] = dot(delta_ref[...], sorted_ref[...])
 
 
-def arrange(plan, groups, arrived_ref, keep_ref, got_ref, *refs):
+def arrange(plan, groups, arrived_ref, shared_ref, *refs):
     weight_refs, (delta_ref, part_ref) = refs[:-2], refs[-2:]
     sort = plan.slot_from_wide()
     part = plan.slot_rows
@@ -226,10 +226,10 @@
         for s in range(plan.slots):
             delta_ref[s, g * part : (g + 1) * part, :] = wide[s * part : (s + 1) * part]
     count = part_ref.shape[0]
-    rows = keep_ref.shape[0] // count
+    rows = shared_ref.shape[0] // count
     for y in range(count):
         at = slice(y * rows, (y + 1) * rows)
-        part_ref[y, :rows, :] = (keep_ref[at, :] + got_ref[at, :]).astype(BF16)
+        part_ref[y, :rows, :] = shared_ref[at, :]
         for step, ref in enumerate(weight_refs):
             part_ref[y, rows + step * BLOCK : rows + (step + 1) * BLOCK, :] = ref[...]
 
@@ -369,7 +369,7 @@
         index=(my_place, holders),
         scratch=[pltpu.VMEM((shared_hidden, columns), F32)],
     )
-    got = moved(give, "dp", other_core)
+    shared_part = (keep + moved(give, "dp", other_core)).astype(BF16)
     weights = [own_weight] + [moved(own_weight, "dp", along_z(step)) for step in (1, 2, 3)]
 
     own_deltas, parts = call(
@@ -379,8 +379,7 @@
             jax.ShapeDtypeStruct((8, 8 * BLOCK, columns), BF16),
         ),
         arrived,
-        keep,
-        got,
+        shared_part,
         *weights,
     )
     partner_deltas = moved(own_deltas, "tensor", other_z)

time: 182 us -> 179 us (0.984)
  local copies, waits for them, and re-layouts: 20.3 us -> 18.1 us
    unnamed x52 -> x48, local copies, waits for them, and re-layouts: 20.2 us -> 18 us
where the time goes in v4:
time: 179 us; the launch traced here: 178 us
  starting transfers between devices  117 us (65%)
  Pallas kernels  21.9 us (12%)
  waiting for transfers between devices  19.6 us (11%)
  local copies, waits for them, and re-layouts  18.1 us (10%)
    ppermute x22, starting transfers between devices, moved(): lax.ppermute(block, axis, [(i, target(i)) for i in range(lax.axis_size(ax...  79.8 us
    all_to_all x3, starting transfers between devices, exchanged(): lax.all_to_all(block, 'dp', split_axis=0, concat_axis=0, axis_index_group...  37.1 us
    pallas_call x9, Pallas kernels, call(): pl.pallas_call(run, out_shape=outs, in_specs=[IN_SMEM] * len(index) + [IN...  21.9 us
    ppermute x22, waiting for transfers between devices, moved(): lax.ppermute(block, axis, [(i, target(i)) for i in range(lax.axis_size(ax...  19.6 us
    unnamed x48, local copies, waits for them, and re-layouts  18 us
  transfers between devices with their start and end apart: 25, of which 7 were waited for; matrix products, arithmetic and copies ran while one was open for 0% of the time, Pallas kernels for 11%

profile of v4, /device:TPU:1, one launch (start us, length us, event | category | flops | bytes accessed | tf_op | source)
XLA Modules:
  0.0 177.9 jit_solution(1500490920708476265)
XLA Ops:
  0.6 4.8 %collective-permute-start = (bf16[16,1024]{1,0:T(8,128)(2,1)}, bf16[16,1024]{1,0:T(8,128)(2,1)S(1)}, u32[]{:S(2)}, u32[]{:S(2)}) collective-permute-start(bf16[16,1024]{1,0:T(8,128)(2,1)} %refs_2_.1), channel_id=1, source_target_pairs={{0,4},{1,5},{2,6},{3,7},{4,0},{5,1},{6,2},{7,3},{8,12},{9,13},{10,... | collective-permute-start | bytes 98312 | tf_op jit(solution)/shard_map/ppermute | solution.py:297
  8.7 4.9 %shard_map.94.refs_0_ = bf16[64,104,128]{2,1,0:T(8,128)(2,1)S(1)} custom-call(s32[8,128]{1,0:T(8,128)S(1)} %bitcast.18, s32[1,128]{1,0:T(1,128)S(1)} %bitcast.20, bf16[1024,128]{1,0:T(8,128)(2,1)S(1)} %bitcast.17, bf16[128,512]{1,0:T(8,128)(2,1)S(1)} %copy-done.13), custom_call_target="tpu_custom_call" | custom-call | tf_op jit(solution)/shard_map/pallas_call | solution.py:83
  15.4 16.3 %all-to-all-start = ((bf16[64,104,128]{2,1,0:T(8,128)(2,1)}), bf16[64,104,128]{2,1,0:T(8,128)(2,1)S(1)}, u32[]{:S(2)}, u32[]{:S(2)}) async-start(bf16[64,104,128]{2,1,0:T(8,128)(2,1)} %get-tuple-element.25), calls=%async_computation | async-start | bytes 3407872 | tf_op jit(solution)/shard_map/all_to_all | solution.py:341
  31.8 3.1 %collective-permute-start.1 = (bf16[16,1024]{1,0:T(8,128)(2,1)S(1)}, bf16[16,1024]{1,0:T(8,128)(2,1)S(1)}, u32[]{:S(2)}, u32[]{:S(2)}) collective-permute-start(bf16[16,1024]{1,0:T(8,128)(2,1)S(1)} %copy-done.18), channel_id=1, source_target_pairs={{0,1},{1,2},{2,3},{3,0},{4,5},{5,6},{6,7},{7,4},{8,9},{9,10},{10,1... | collective-permute-start | bytes 98312 | tf_op jit(solution)/shard_map/ppermute | solution.py:297
  34.9 3.4 %collective-permute-start.3 = (bf16[16,1024]{1,0:T(8,128)(2,1)S(1)}, bf16[16,1024]{1,0:T(8,128)(2,1)S(1)}, u32[]{:S(2)}, u32[]{:S(2)}) collective-permute-start(bf16[16,1024]{1,0:T(8,128)(2,1)S(1)} %copy-done.18), channel_id=1, source_target_pairs={{0,3},{1,0},{2,1},{3,2},{4,7},{5,4},{6,5},{7,6},{8,11},{9,8},{10,9... | collective-permute-start | bytes 98312 | tf_op jit(solution)/shard_map/ppermute | solution.py:297
  38.3 3.4 %collective-permute-start.5 = (bf16[16,1024]{1,0:T(8,128)(2,1)S(1)}, bf16[16,1024]{1,0:T(8,128)(2,1)S(1)}, u32[]{:S(2)}, u32[]{:S(2)}) collective-permute-start(bf16[16,1024]{1,0:T(8,128)(2,1)S(1)} %copy-done.18), channel_id=1, source_target_pairs={{0,2},{1,3},{2,0},{3,1},{4,6},{5,7},{6,4},{7,5},{8,10},{9,11},{10,... | collective-permute-start | bytes 98312 | tf_op jit(solution)/shard_map/ppermute | solution.py:297
  41.7 2.2 %collective-permute-start.2 = (bf16[16,1024]{1,0:T(8,128)(2,1)S(1)}, bf16[16,1024]{1,0:T(8,128)(2,1)S(1)}, u32[]{:S(2)}, u32[]{:S(2)}) collective-permute-start(bf16[16,1024]{1,0:T(8,128)(2,1)S(1)} %copy-done.17), channel_id=1, source_target_pairs={{0,1},{1,2},{2,3},{3,0},{4,5},{5,6},{6,7},{7,4},{8,9},{9,10},{10,1... | collective-permute-start | bytes 98312 | tf_op jit(solution)/shard_map/ppermute | solution.py:297
  44.0 4.3 %collective-permute-start.4 = (bf16[16,1024]{1,0:T(8,128)(2,1)S(1)}, bf16[16,1024]{1,0:T(8,128)(2,1)S(1)}, u32[]{:S(2)}, u32[]{:S(2)}) collective-permute-start(bf16[16,1024]{1,0:T(8,128)(2,1)S(1)} %copy-done.17), channel_id=1, source_target_pairs={{0,3},{1,0},{2,1},{3,2},{4,7},{5,4},{6,5},{7,6},{8,11},{9,8},{10,9... | collective-permute-start | bytes 98312 | tf_op jit(solution)/shard_map/ppermute | solution.py:297
  48.3 2.1 %collective-permute-start.6 = (bf16[16,1024]{1,0:T(8,128)(2,1)S(1)}, bf16[16,1024]{1,0:T(8,128)(2,1)S(1)}, u32[]{:S(2)}, u32[]{:S(2)}) collective-permute-start(bf16[16,1024]{1,0:T(8,128)(2,1)S(1)} %copy-done.17), channel_id=1, source_target_pairs={{0,2},{1,3},{2,0},{3,1},{4,6},{5,7},{6,4},{7,5},{8,10},{9,11},{10,... | collective-permute-start | bytes 98312 | tf_op jit(solution)/shard_map/ppermute | solution.py:297
  50.6 4.1 %collective-permute-done.6.refs_9_ = bf16[16,1024]{1,0:T(8,128)(2,1)S(1)} collective-permute-done((bf16[16,1024]{1,0:T(8,128)(2,1)S(1)}, bf16[16,1024]{1,0:T(8,128)(2,1)S(1)}, u32[]{:S(2)}, u32[]{:S(2)}) %collective-permute-start.6) | collective-permute-done | bytes 32800 | tf_op jit(solution)/shard_map/ppermute | solution.py:297
  55.9 4.6 %collective-permute-start.7 = (f32[512,512]{1,0:T(8,128)S(1)}, f32[512,512]{1,0:T(8,128)S(1)}, u32[]{:S(2)}, u32[]{:S(2)}) collective-permute-start(f32[512,512]{1,0:T(8,128)S(1)} %get-tuple-element.28), channel_id=1, source_target_pairs={{0,8},{8,0},{16,24},{24,16},{32,40},{40,32},{48,56},{56,48},{64,72... | collective-permute-start | bytes 3145736 | tf_op jit(solution)/shard_map/ppermute | solution.py:297
  60.5 5.3 %collective-permute-start.10 = (bf16[16,512]{1,0:T(8,128)(2,1)S(1)}, bf16[16,512]{1,0:T(8,128)(2,1)S(1)}, u32[]{:S(2)}, u32[]{:S(2)}) collective-permute-start(bf16[16,512]{1,0:T(8,128)(2,1)S(1)} %get-tuple-element.29.refs_2_), channel_id=1, source_target_pairs={{0,48},{8,56},{16,0},{24,8},{32,16},{40,24},{48,32},{56,40},{64,11... | collective-permute-start | bytes 49160 | tf_op jit(solution)/shard_map/ppermute | solution.py:297
  67.8 6.1 %collective-permute-start.9 = (bf16[16,512]{1,0:T(8,128)(2,1)S(1)}, bf16[16,512]{1,0:T(8,128)(2,1)S(1)}, u32[]{:S(2)}, u32[]{:S(2)}) collective-permute-start(bf16[16,512]{1,0:T(8,128)(2,1)S(1)} %get-tuple-element.29.refs_2_), channel_id=1, source_target_pairs={{0,32},{8,40},{16,48},{24,56},{32,0},{40,8},{48,16},{56,24},{64,96... | collective-permute-start | bytes 49160 | tf_op jit(solution)/shard_map/ppermute | solution.py:297
  77.5 6.5 %all-to-all-start.2 = ((bf16[8,128,512]{2,1,0:T(8,128)(2,1)}), bf16[8,128,512]{2,1,0:T(8,128)(2,1)S(1)}, u32[]{:S(2)}, u32[]{:S(2)}) async-start(bf16[8,128,512]{2,1,0:T(8,128)(2,1)} %copy-done.10), calls=%async_computation.2 | async-start | bytes 2097152 | tf_op jit(solution)/shard_map/all_to_all | solution.py:341
  84.0 2.2 %collective-permute-start.13 = (bf16[2,640,128]{2,1,0:T(8,128)(2,1)S(1)}, bf16[2,640,128]{2,1,0:T(8,128)(2,1)S(1)}, u32[]{:S(2)}, u32[]{:S(2)}) collective-permute-start(bf16[2,640,128]{2,1,0:T(8,128)(2,1)S(1)} %get-tuple-element.30.refs_1_), channel_id=1, source_target_pairs={{0,4},{1,5},{2,6},{3,7},{4,0},{5,1},{6,2},{7,3},{8,12},{9,13},{10,... | collective-permute-start | bytes 983048 | tf_op jit(solution)/shard_map/ppermute | solution.py:297
  86.2 2.5 %collective-permute-start.11 = (bf16[2,640,128]{2,1,0:T(8,128)(2,1)S(1)}, bf16[2,640,128]{2,1,0:T(8,128)(2,1)S(1)}, u32[]{:S(2)}, u32[]{:S(2)}) collective-permute-start(bf16[2,640,128]{2,1,0:T(8,128)(2,1)S(1)} %get-tuple-element.30.refs_1_), channel_id=1, source_target_pairs={{0,1},{1,2},{2,3},{3,0},{4,5},{5,6},{6,7},{7,4},{8,9},{9,10},{10,1... | collective-permute-start | bytes 983048 | tf_op jit(solution)/shard_map/ppermute | solution.py:297
  88.8 4.6 %collective-permute-done.13.refs_2_ = bf16[2,640,128]{2,1,0:T(8,128)(2,1)S(1)} collective-permute-done((bf16[2,640,128]{2,1,0:T(8,128)(2,1)S(1)}, bf16[2,640,128]{2,1,0:T(8,128)(2,1)S(1)}, u32[]{:S(2)}, u32[]{:S(2)}) %collective-permute-start.13) | collective-permute-done | bytes 327712 | tf_op jit(solution)/shard_map/ppermute | solution.py:297
  93.4 4.8 %collective-permute-start.14 = (bf16[2,640,128]{2,1,0:T(8,128)(2,1)S(1)}, bf16[2,640,128]{2,1,0:T(8,128)(2,1)S(1)}, u32[]{:S(2)}, u32[]{:S(2)}) collective-permute-start(bf16[2,640,128]{2,1,0:T(8,128)(2,1)S(1)} %collective-permute-done.13.refs_2_), channel_id=1, source_target_pairs={{0,3},{1,0},{2,1},{3,2},{4,7},{5,4},{6,5},{7,6},{8,11},{9,8},{10,9... | collective-permute-start | bytes 983048 | tf_op jit(solution)/shard_map/ppermute | solution.py:297
  98.3 2.3 %collective-permute-start.17 = (bf16[2,640,128]{2,1,0:T(8,128)(2,1)S(1)}, bf16[2,640,128]{2,1,0:T(8,128)(2,1)S(1)}, u32[]{:S(2)}, u32[]{:S(2)}) collective-permute-start(bf16[2,640,128]{2,1,0:T(8,128)(2,1)S(1)} %get-tuple-element.30.refs_1_), channel_id=1, source_target_pairs={{0,3},{1,0},{2,1},{3,2},{4,7},{5,4},{6,5},{7,6},{8,11},{9,8},{10,9... | collective-permute-start | bytes 983048 | tf_op jit(solution)/shard_map/ppermute | solution.py:297
  100.5 3.0 %collective-permute-start.16 = (bf16[2,640,128]{2,1,0:T(8,128)(2,1)S(1)}, bf16[2,640,128]{2,1,0:T(8,128)(2,1)S(1)}, u32[]{:S(2)}, u32[]{:S(2)}) collective-permute-start(bf16[2,640,128]{2,1,0:T(8,128)(2,1)S(1)} %collective-permute-done.13.refs_2_), channel_id=1, source_target_pairs={{0,1},{1,2},{2,3},{3,0},{4,5},{5,6},{6,7},{7,4},{8,9},{9,10},{10,1... | collective-permute-start | bytes 983048 | tf_op jit(solution)/shard_map/ppermute | solution.py:297
  105.5 4.8 %collective-permute-start.15 = (bf16[2,640,128]{2,1,0:T(8,128)(2,1)S(1)}, bf16[2,640,128]{2,1,0:T(8,128)(2,1)S(1)}, u32[]{:S(2)}, u32[]{:S(2)}) collective-permute-start(bf16[2,640,128]{2,1,0:T(8,128)(2,1)S(1)} %collective-permute-done.14.refs_6_), channel_id=1, source_target_pairs={{0,3},{1,0},{2,1},{3,2},{4,7},{5,4},{6,5},{7,6},{8,11},{9,8},{10,9... | collective-permute-start | bytes 983048 | tf_op jit(solution)/shard_map/ppermute | solution.py:297
  112.2 2.4 %shard_map.98 = (f32[2,640,512]{2,1,0:T(8,128)S(1)}, bf16[2,256,512]{2,1,0:T(8,128)(2,1)S(1)}, bf16[6,2,640,128]{3,2,1,0:T(8,128)(2,1)S(1)}) custom-call(s32[8]{0:T(128)S(1)} %stack.47.refs_1_.refs_0_, bf16[2,640,128]{2,1,0:T(8,128)(2,1)S(1)} %get-tuple-element.30.refs_1_, bf16[2,640,128]{2,1,0:T(8,128)(2,1)S(1)} %collective-permute-done.13.refs_2_, ...), custom_call_target="tpu_custom_call" | custom-call | tf_op jit(solution)/shard_map/pallas_call | solution.py:83
  117.6 2.7 %shard_map.99 = (bf16[5120,128]{1,0:T(8,128)(2,1)S(1)}, bf16[2,2,640,128]{3,2,1,0:T(8,128)(2,1)S(1)}) custom-call(bf16[2,640,128]{2,1,0:T(8,128)(2,1)S(1)} %collective-permute-done.12.refs_0_, bf16[2,640,128]{2,1,0:T(8,128)(2,1)S(1)} %collective-permute-done.15.refs_1_, bf16[2,256,512]{2,1,0:T(8,128)(2,1)S(1)} %get-tuple-element.31.refs_2_, ...), custom_call_target="tpu_custom_call" | custom-call | tf_op jit(solution)/shard_map/pallas_call | solution.py:83
  123.2 14.3 %all-to-all-start.1 = ((bf16[64,80,128]{2,1,0:T(8,128)(2,1)}), bf16[64,80,128]{2,1,0:T(8,128)(2,1)S(1)}, u32[]{:S(2)}, u32[]{:S(2)}) async-start(bf16[64,80,128]{2,1,0:T(8,128)(2,1)} %bitcast.16), calls=%async_computation.1 | async-start | bytes 2621440 | tf_op jit(solution)/shard_map/all_to_all | solution.py:341
  139.3 2.4 %collective-permute-start.18 = (bf16[512,512]{1,0:T(8,128)(2,1)S(1)}, bf16[512,512]{1,0:T(8,128)(2,1)S(1)}, u32[]{:S(2)}, u32[]{:S(2)}) collective-permute-start(bf16[512,512]{1,0:T(8,128)(2,1)S(1)} %get-tuple-element.36), channel_id=1, source_target_pairs={{0,8},{8,0},{16,24},{24,16},{32,40},{40,32},{48,56},{56,48},{64,72... | collective-permute-start | bytes 1572872 | tf_op jit(solution)/shard_map/ppermute | solution.py:297
  144.3 5.4 %shard_map.101.refs_5_ = bf16[2,1024,512]{2,1,0:T(8,128)(2,1)} custom-call(s32[8]{0:T(128)S(1)} %stack.47.refs_1_.refs_0_, bf16[6,2,640,128]{3,2,1,0:T(8,128)(2,1)S(1)} %copy-done.6, bf16[2,2,640,128]{3,2,1,0:T(8,128)(2,1)S(1)} %copy-done.12, bf16[64,104,128]{2,1,0:T(8,128)(2,1)S(1)} %all-to-all-done.refs_0_.refs_3_), custom_call_target="tpu_custom_call" | custom-call | tf_op jit(solution)/shard_map/pallas_call | solution.py:83
  149.8 4.2 %collective-permute-start.19 = (f32[16,512]{1,0:T(8,128)S(1)}, f32[16,512]{1,0:T(8,128)S(1)}, u32[]{:S(2)}, u32[]{:S(2)}) collective-permute-start(f32[16,512]{1,0:T(8,128)S(1)} %get-tuple-element.42), channel_id=1, source_target_pairs={{0,16},{8,24},{16,32},{24,40},{32,48},{40,56},{48,0},{56,8},{64,80... | collective-permute-start | bytes 98312 | tf_op jit(solution)/shard_map/ppermute | solution.py:297
  154.0 5.2 %collective-permute-start.20 = (f32[16,512]{1,0:T(8,128)S(1)}, f32[16,512]{1,0:T(8,128)S(1)}, u32[]{:S(2)}, u32[]{:S(2)}) collective-permute-start(f32[16,512]{1,0:T(8,128)S(1)} %get-tuple-element.43), channel_id=1, source_target_pairs={{0,32},{8,40},{16,48},{24,56},{32,0},{40,8},{48,16},{56,24},{64,96... | collective-permute-start | bytes 98312 | tf_op jit(solution)/shard_map/ppermute | solution.py:297
  159.2 5.2 %collective-permute-start.21 = (f32[16,512]{1,0:T(8,128)S(1)}, f32[16,512]{1,0:T(8,128)S(1)}, u32[]{:S(2)}, u32[]{:S(2)}) collective-permute-start(f32[16,512]{1,0:T(8,128)S(1)} %get-tuple-element.44), channel_id=1, source_target_pairs={{0,48},{8,56},{16,0},{24,8},{32,16},{40,24},{48,32},{56,40},{64,11... | collective-permute-start | bytes 98312 | tf_op jit(solution)/shard_map/ppermute | solution.py:297
  164.6 2.3 %shard_map.102 = (f32[128,512]{1,0:T(8,128)S(1)}, bf16[5120,128]{1,0:T(8,128)(2,1)S(1)}) custom-call(s32[2]{0:T(128)S(1)} %pad_add_fusion.refs_0_, bf16[128,1024]{1,0:T(8,128)(2,1)S(1)} %get-tuple-element.34.refs_1_, bf16[1024,512]{1,0:T(8,128)(2,1)S(1)} %pad_maximum_fusion.refs_2_, s32[8,128]{1,0:T(8,128)S(1)} %bitcast.19, s32[1,128]{1,0:T(1,128)S(1)} %bitcast.21, ...), custom_call_target="tpu_custom_call" | custom-call | tf_op jit(solution)/shard_map/pallas_call | solution.py:83
  167.9 4.2 %collective-permute-done.19.refs_4_ = f32[16,512]{1,0:T(8,128)S(1)} collective-permute-done((f32[16,512]{1,0:T(8,128)S(1)}, f32[16,512]{1,0:T(8,128)S(1)}, u32[]{:S(2)}, u32[]{:S(2)}) %collective-permute-start.19) | collective-permute-done | bytes 32800 | tf_op jit(solution)/shard_map/ppermute | solution.py:297
  172.2 2.4 %collective-permute-done.20.refs_5_ = f32[16,512]{1,0:T(8,128)S(1)} collective-permute-done((f32[16,512]{1,0:T(8,128)S(1)}, f32[16,512]{1,0:T(8,128)S(1)}, u32[]{:S(2)}, u32[]{:S(2)}) %collective-permute-start.20) | collective-permute-done | bytes 32800 | tf_op jit(solution)/shard_map/ppermute | solution.py:297
  (80 shorter events, 30.6 us)
Async XLA Ops:
  0.6 14.2 %collective-permute-start = (bf16[16,1024]{1,0:T(8,128)(2,1)}, bf16[16,1024]{1,0:T(8,128)(2,1)S(1)}, u32[]{:S(2)}, u32[]{:S(2)}) collective-permute-start(bf16[16,1024]{1,0:T(8,128)(2,1)} %refs_2_.1), channel_id=1, source_target_pairs={{0,4},{1,5},{2,6},{3,7},{4,0},{5,1},{6,2},{7,3},{8,12},{9,13},{10,... | collective-permute-start | bytes 98312 | tf_op jit(solution)/shard_map/ppermute | solution.py:297
  15.4 16.4 %copy-start.18 = (bf16[16,1024]{1,0:T(8,128)(2,1)S(1)}, bf16[16,1024]{1,0:T(8,128)(2,1)}, u32[]{:S(2)}) copy-start(bf16[16,1024]{1,0:T(8,128)(2,1)} %refs_2_.1) | copy-start | bytes 98308
  15.4 26.3 %copy-start.17 = (bf16[16,1024]{1,0:T(8,128)(2,1)S(1)}, bf16[16,1024]{1,0:T(8,128)(2,1)}, u32[]{:S(2)}) copy-start(bf16[16,1024]{1,0:T(8,128)(2,1)} %get-tuple-element.26.refs_3_) | copy-start | bytes 98308
  15.4 39.3 %copy-start.14 = (bf16[128,512]{1,0:T(8,128)(2,1)S(1)}, bf16[128,512]{1,0:T(8,128)(2,1)}, u32[]{:S(2)}) copy-start(bf16[128,512]{1,0:T(8,128)(2,1)} %refs_10_.1) | copy-start | bytes 393220
  15.4 39.3 %copy-start.21 = (bf16[16,512]{1,0:T(8,128)(2,1)S(1)}, bf16[16,512]{1,0:T(8,128)(2,1)}, u32[]{:S(2)}) copy-start(bf16[16,512]{1,0:T(8,128)(2,1)} %refs_11_.1) | copy-start | bytes 49156
  15.4 60.7 %all-to-all-start = ((bf16[64,104,128]{2,1,0:T(8,128)(2,1)}), bf16[64,104,128]{2,1,0:T(8,128)(2,1)S(1)}, u32[]{:S(2)}, u32[]{:S(2)}) async-start(bf16[64,104,128]{2,1,0:T(8,128)(2,1)} %get-tuple-element.25), calls=%async_computation | async-start | bytes 3407872 | tf_op jit(solution)/shard_map/all_to_all | solution.py:341
  31.8 16.5 %collective-permute-start.1 = (bf16[16,1024]{1,0:T(8,128)(2,1)S(1)}, bf16[16,1024]{1,0:T(8,128)(2,1)S(1)}, u32[]{:S(2)}, u32[]{:S(2)}) collective-permute-start(bf16[16,1024]{1,0:T(8,128)(2,1)S(1)} %copy-done.18), channel_id=1, source_target_pairs={{0,1},{1,2},{2,3},{3,0},{4,5},{5,6},{6,7},{7,4},{8,9},{9,10},{10,1... | collective-permute-start | bytes 98312 | tf_op jit(solution)/shard_map/ppermute | solution.py:297
  34.9 15.7 %collective-permute-start.3 = (bf16[16,1024]{1,0:T(8,128)(2,1)S(1)}, bf16[16,1024]{1,0:T(8,128)(2,1)S(1)}, u32[]{:S(2)}, u32[]{:S(2)}) collective-permute-start(bf16[16,1024]{1,0:T(8,128)(2,1)S(1)} %copy-done.18), channel_id=1, source_target_pairs={{0,3},{1,0},{2,1},{3,2},{4,7},{5,4},{6,5},{7,6},{8,11},{9,8},{10,9... | collective-permute-start | bytes 98312 | tf_op jit(solution)/shard_map/ppermute | solution.py:297
  38.3 12.3 %collective-permute-start.5 = (bf16[16,1024]{1,0:T(8,128)(2,1)S(1)}, bf16[16,1024]{1,0:T(8,128)(2,1)S(1)}, u32[]{:S(2)}, u32[]{:S(2)}) collective-permute-start(bf16[16,1024]{1,0:T(8,128)(2,1)S(1)} %copy-done.18), channel_id=1, source_target_pairs={{0,2},{1,3},{2,0},{3,1},{4,6},{5,7},{6,4},{7,5},{8,10},{9,11},{10,... | collective-permute-start | bytes 98312 | tf_op jit(solution)/shard_map/ppermute | solution.py:297
  41.7 8.8 %collective-permute-start.2 = (bf16[16,1024]{1,0:T(8,128)(2,1)S(1)}, bf16[16,1024]{1,0:T(8,128)(2,1)S(1)}, u32[]{:S(2)}, u32[]{:S(2)}) collective-permute-start(bf16[16,1024]{1,0:T(8,128)(2,1)S(1)} %copy-done.17), channel_id=1, source_target_pairs={{0,1},{1,2},{2,3},{3,0},{4,5},{5,6},{6,7},{7,4},{8,9},{9,10},{10,1... | collective-permute-start | bytes 98312 | tf_op jit(solution)/shard_map/ppermute | solution.py:297
  44.0 6.6 %collective-permute-start.4 = (bf16[16,1024]{1,0:T(8,128)(2,1)S(1)}, bf16[16,1024]{1,0:T(8,128)(2,1)S(1)}, u32[]{:S(2)}, u32[]{:S(2)}) collective-permute-start(bf16[16,1024]{1,0:T(8,128)(2,1)S(1)} %copy-done.17), channel_id=1, source_target_pairs={{0,3},{1,0},{2,1},{3,2},{4,7},{5,4},{6,5},{7,6},{8,11},{9,8},{10,9... | collective-permute-start | bytes 98312 | tf_op jit(solution)/shard_map/ppermute | solution.py:297
  48.3 6.5 %collective-permute-start.6 = (bf16[16,1024]{1,0:T(8,128)(2,1)S(1)}, bf16[16,1024]{1,0:T(8,128)(2,1)S(1)}, u32[]{:S(2)}, u32[]{:S(2)}) collective-permute-start(bf16[16,1024]{1,0:T(8,128)(2,1)S(1)} %copy-done.17), channel_id=1, source_target_pairs={{0,2},{1,3},{2,0},{3,1},{4,6},{5,7},{6,4},{7,5},{8,10},{9,11},{10,... | collective-permute-start | bytes 98312 | tf_op jit(solution)/shard_map/ppermute | solution.py:297
  55.9 17.9 %collective-permute-start.7 = (f32[512,512]{1,0:T(8,128)S(1)}, f32[512,512]{1,0:T(8,128)S(1)}, u32[]{:S(2)}, u32[]{:S(2)}) collective-permute-start(f32[512,512]{1,0:T(8,128)S(1)} %get-tuple-element.28), channel_id=1, source_target_pairs={{0,8},{8,0},{16,24},{24,16},{32,40},{40,32},{48,56},{56,48},{64,72... | collective-permute-start | bytes 3145736 | tf_op jit(solution)/shard_map/ppermute | solution.py:297
  60.5 13.6 %collective-permute-start.10 = (bf16[16,512]{1,0:T(8,128)(2,1)S(1)}, bf16[16,512]{1,0:T(8,128)(2,1)S(1)}, u32[]{:S(2)}, u32[]{:S(2)}) collective-permute-start(bf16[16,512]{1,0:T(8,128)(2,1)S(1)} %get-tuple-element.29.refs_2_), channel_id=1, source_target_pairs={{0,48},{8,56},{16,0},{24,8},{32,16},{40,24},{48,32},{56,40},{64,11... | collective-permute-start | bytes 49160 | tf_op jit(solution)/shard_map/ppermute | solution.py:297
  65.8 8.3 %collective-permute-start.8 = (bf16[16,512]{1,0:T(8,128)(2,1)S(1)}, bf16[16,512]{1,0:T(8,128)(2,1)S(1)}, u32[]{:S(2)}, u32[]{:S(2)}) collective-permute-start(bf16[16,512]{1,0:T(8,128)(2,1)S(1)} %get-tuple-element.29.refs_2_), channel_id=1, source_target_pairs={{0,16},{8,24},{16,32},{24,40},{32,48},{40,56},{48,0},{56,8},{64,80... | collective-permute-start | bytes 49160 | tf_op jit(solution)/shard_map/ppermute | solution.py:297
  67.8 8.4 %collective-permute-start.9 = (bf16[16,512]{1,0:T(8,128)(2,1)S(1)}, bf16[16,512]{1,0:T(8,128)(2,1)S(1)}, u32[]{:S(2)}, u32[]{:S(2)}) collective-permute-start(bf16[16,512]{1,0:T(8,128)(2,1)S(1)} %get-tuple-element.29.refs_2_), channel_id=1, source_target_pairs={{0,32},{8,40},{16,48},{24,56},{32,0},{40,8},{48,16},{56,24},{64,96... | collective-permute-start | bytes 49160 | tf_op jit(solution)/shard_map/ppermute | solution.py:297
  77.5 44.7 %all-to-all-start.2 = ((bf16[8,128,512]{2,1,0:T(8,128)(2,1)}), bf16[8,128,512]{2,1,0:T(8,128)(2,1)S(1)}, u32[]{:S(2)}, u32[]{:S(2)}) async-start(bf16[8,128,512]{2,1,0:T(8,128)(2,1)} %copy-done.10), calls=%async_computation.2 | async-start | bytes 2097152 | tf_op jit(solution)/shard_map/all_to_all | solution.py:341
  84.0 9.4 %collective-permute-start.13 = (bf16[2,640,128]{2,1,0:T(8,128)(2,1)S(1)}, bf16[2,640,128]{2,1,0:T(8,128)(2,1)S(1)}, u32[]{:S(2)}, u32[]{:S(2)}) collective-permute-start(bf16[2,640,128]{2,1,0:T(8,128)(2,1)S(1)} %get-tuple-element.30.refs_1_), channel_id=1, source_target_pairs={{0,4},{1,5},{2,6},{3,7},{4,0},{5,1},{6,2},{7,3},{8,12},{9,13},{10,... | collective-permute-start | bytes 983048 | tf_op jit(solution)/shard_map/ppermute | solution.py:297
  86.2 17.3 %collective-permute-start.11 = (bf16[2,640,128]{2,1,0:T(8,128)(2,1)S(1)}, bf16[2,640,128]{2,1,0:T(8,128)(2,1)S(1)}, u32[]{:S(2)}, u32[]{:S(2)}) collective-permute-start(bf16[2,640,128]{2,1,0:T(8,128)(2,1)S(1)} %get-tuple-element.30.refs_1_), channel_id=1, source_target_pairs={{0,1},{1,2},{2,3},{3,0},{4,5},{5,6},{6,7},{7,4},{8,9},{9,10},{10,1... | collective-permute-start | bytes 983048 | tf_op jit(solution)/shard_map/ppermute | solution.py:297
  93.4 12.1 %collective-permute-start.14 = (bf16[2,640,128]{2,1,0:T(8,128)(2,1)S(1)}, bf16[2,640,128]{2,1,0:T(8,128)(2,1)S(1)}, u32[]{:S(2)}, u32[]{:S(2)}) collective-permute-start(bf16[2,640,128]{2,1,0:T(8,128)(2,1)S(1)} %collective-permute-done.13.refs_2_), channel_id=1, source_target_pairs={{0,3},{1,0},{2,1},{3,2},{4,7},{5,4},{6,5},{7,6},{8,11},{9,8},{10,9... | collective-permute-start | bytes 983048 | tf_op jit(solution)/shard_map/ppermute | solution.py:297
  98.3 12.3 %collective-permute-start.17 = (bf16[2,640,128]{2,1,0:T(8,128)(2,1)S(1)}, bf16[2,640,128]{2,1,0:T(8,128)(2,1)S(1)}, u32[]{:S(2)}, u32[]{:S(2)}) collective-permute-start(bf16[2,640,128]{2,1,0:T(8,128)(2,1)S(1)} %get-tuple-element.30.refs_1_), channel_id=1, source_target_pairs={{0,3},{1,0},{2,1},{3,2},{4,7},{5,4},{6,5},{7,6},{8,11},{9,8},{10,9... | collective-permute-start | bytes 983048 | tf_op jit(solution)/shard_map/ppermute | solution.py:297
  100.5 10.0 %collective-permute-start.16 = (bf16[2,640,128]{2,1,0:T(8,128)(2,1)S(1)}, bf16[2,640,128]{2,1,0:T(8,128)(2,1)S(1)}, u32[]{:S(2)}, u32[]{:S(2)}) collective-permute-start(bf16[2,640,128]{2,1,0:T(8,128)(2,1)S(1)} %collective-permute-done.13.refs_2_), channel_id=1, source_target_pairs={{0,1},{1,2},{2,3},{3,0},{4,5},{5,6},{6,7},{7,4},{8,9},{9,10},{10,1... | collective-permute-start | bytes 983048 | tf_op jit(solution)/shard_map/ppermute | solution.py:297
  103.6 14.0 %collective-permute-start.12 = (bf16[2,640,128]{2,1,0:T(8,128)(2,1)S(1)}, bf16[2,640,128]{2,1,0:T(8,128)(2,1)S(1)}, u32[]{:S(2)}, u32[]{:S(2)}) collective-permute-start(bf16[2,640,128]{2,1,0:T(8,128)(2,1)S(1)} %collective-permute-done.11.refs_3_), channel_id=1, source_target_pairs={{0,1},{1,2},{2,3},{3,0},{4,5},{5,6},{6,7},{7,4},{8,9},{9,10},{10,1... | collective-permute-start | bytes 983048 | tf_op jit(solution)/shard_map/ppermute | solution.py:297
  105.5 12.1 %collective-permute-start.15 = (bf16[2,640,128]{2,1,0:T(8,128)(2,1)S(1)}, bf16[2,640,128]{2,1,0:T(8,128)(2,1)S(1)}, u32[]{:S(2)}, u32[]{:S(2)}) collective-permute-start(bf16[2,640,128]{2,1,0:T(8,128)(2,1)S(1)} %collective-permute-done.14.refs_6_), channel_id=1, source_target_pairs={{0,3},{1,0},{2,1},{3,2},{4,7},{5,4},{6,5},{7,6},{8,11},{9,8},{10,9... | collective-permute-start | bytes 983048 | tf_op jit(solution)/shard_map/ppermute | solution.py:297
  123.2 51.4 %all-to-all-start.1 = ((bf16[64,80,128]{2,1,0:T(8,128)(2,1)}), bf16[64,80,128]{2,1,0:T(8,128)(2,1)S(1)}, u32[]{:S(2)}, u32[]{:S(2)}) async-start(bf16[64,80,128]{2,1,0:T(8,128)(2,1)} %bitcast.16), calls=%async_computation.1 | async-start | bytes 2621440 | tf_op jit(solution)/shard_map/all_to_all | solution.py:341
  139.3 25.1 %collective-permute-start.18 = (bf16[512,512]{1,0:T(8,128)(2,1)S(1)}, bf16[512,512]{1,0:T(8,128)(2,1)S(1)}, u32[]{:S(2)}, u32[]{:S(2)}) collective-permute-start(bf16[512,512]{1,0:T(8,128)(2,1)S(1)} %get-tuple-element.36), channel_id=1, source_target_pairs={{0,8},{8,0},{16,24},{24,16},{32,40},{40,32},{48,56},{56,48},{64,72... | collective-permute-start | bytes 1572872 | tf_op jit(solution)/shard_map/ppermute | solution.py:297
  149.8 14.7 %copy-start.1 = (bf16[2,1024,512]{2,1,0:T(8,128)(2,1)S(1)}, bf16[2,1024,512]{2,1,0:T(8,128)(2,1)}, u32[]{:S(2)}) copy-start(bf16[2,1024,512]{2,1,0:T(8,128)(2,1)} %shard_map.101.refs_5_) | copy-start | bytes 6291460
  149.8 14.7 %copy-start.20 = (s32[128,8]{0,1:T(8,128)S(1)}, s32[128,8]{0,1:T(8,128)}, u32[]{:S(2)}) copy-start(s32[128,8]{0,1:T(8,128)} %param.12) | copy-start | bytes 12292
  149.8 14.8 %copy-start.23 = (s32[128]{0:T(128)S(1)}, s32[128]{0:T(128)}, u32[]{:S(2)}) copy-start(s32[128]{0:T(128)} %param.13) | copy-start | bytes 1540
  149.8 22.4 %collective-permute-start.19 = (f32[16,512]{1,0:T(8,128)S(1)}, f32[16,512]{1,0:T(8,128)S(1)}, u32[]{:S(2)}, u32[]{:S(2)}) collective-permute-start(f32[16,512]{1,0:T(8,128)S(1)} %get-tuple-element.42), channel_id=1, source_target_pairs={{0,16},{8,24},{16,32},{24,40},{32,48},{40,56},{48,0},{56,8},{64,80... | collective-permute-start | bytes 98312 | tf_op jit(solution)/shard_map/ppermute | solution.py:297
  154.0 20.6 %collective-permute-start.20 = (f32[16,512]{1,0:T(8,128)S(1)}, f32[16,512]{1,0:T(8,128)S(1)}, u32[]{:S(2)}, u32[]{:S(2)}) collective-permute-start(f32[16,512]{1,0:T(8,128)S(1)} %get-tuple-element.43), channel_id=1, source_target_pairs={{0,32},{8,40},{16,48},{24,56},{32,0},{40,8},{48,16},{56,24},{64,96... | collective-permute-start | bytes 98312 | tf_op jit(solution)/shard_map/ppermute | solution.py:297
  159.2 15.4 %collective-permute-start.21 = (f32[16,512]{1,0:T(8,128)S(1)}, f32[16,512]{1,0:T(8,128)S(1)}, u32[]{:S(2)}, u32[]{:S(2)}) collective-permute-start(f32[16,512]{1,0:T(8,128)S(1)} %get-tuple-element.44), channel_id=1, source_target_pairs={{0,48},{8,56},{16,0},{24,8},{32,16},{40,24},{48,32},{56,40},{64,11... | collective-permute-start | bytes 98312 | tf_op jit(solution)/shard_map/ppermute | solution.py:297
  (17 other events, 18.0 us)

commit v5 on v4

--- a/solution.py
+++ b/solution.py
@@ -206,10 +206,11 @@
     place = places(route_ref, slot_ref)[0]
     slots, rows = plan.group * plan.slots, plan.group * plan.packed
     dest, _, at = plan.packed_index(slots)
-    expand, rank = plan.expand(dest, at), plan.rank(plan.packed_index(LANES)[2])
-    for g in range(groups):
-        value = dot(expand, place[g * slots : (g + 1) * slots])
-        chosen_ref[g * rows : (g + 1) * rows, :] = one_hot(value == rank)
+    expand = plan.expand(dest, at)
+    rank = (lax.broadcasted_iota(jnp.int32, (place.shape[1], rows), 1) % plan.packed % plan.rows % MOST).astype(F32)
+    for g in range(groups):
+        value = dot(place[g * slots : (g + 1) * slots], expand, ((0,), (1,)))
+        chosen_ref[:, g * rows : (g + 1) * rows] = one_hot(value == rank)
     for k in range(weight_ref.shape[0] // BLOCK):
         core, z = place_ref[1] ^ (k % 2), (place_ref[0] - (k // 2) % 4) & 3
         sorted_ref[k * BLOCK : (k + 1) * BLOCK, :] = weight_ref[place_at((core * 8 + k // 8) * 4 + z, BLOCK), :]
@@ -288,7 +289,7 @@
     total = shared_ref[...]
     for g in range(groups):
         at = slice(g * rows, (g + 1) * rows)
-        total = total + dot(chosen_ref[at, :], widened(plan, returned_ref[at, :], mask), ((0,), (0,)))
+        total = total + dot(chosen_ref[:, at], widened(plan, returned_ref[at, :], mask))
     out_ref[...] = total.astype(BF16)
     sum_ref[...] = part_refs[0][...] + part_refs[1][...] + part_refs[2][...] + part_refs[3][...]
 
@@ -447,7 +448,7 @@
     weight_all = jnp.concatenate([weight_part, moved(weight_part, "dp", other_core)], axis=0)
     shared_term, chosen = call(
         functools.partial(shared_rows, plan, groups),
-        (jax.ShapeDtypeStruct((tokens, columns), F32), jax.ShapeDtypeStruct((packed_rows, tokens), BF16)),
+        (jax.ShapeDtypeStruct((tokens, columns), F32), jax.ShapeDtypeStruct((tokens, packed_rows), BF16)),
         shared_all,
         weight_all,
         routing.T,

time: 179 us -> 179 us (level)
  no operation moved by 1% of the time
where the time goes in v5:
time: 179 us; the launch traced here: 178 us
  starting transfers between devices  117 us (65%)
  Pallas kernels  22 us (12%)
  waiting for transfers between devices  19.5 us (11%)
  local copies, waits for them, and re-layouts  18.1 us (10%)
    ppermute x22, starting transfers between devices, moved(): lax.ppermute(block, axis, [(i, target(i)) for i in range(lax.axis_size(ax...  79.8 us
    all_to_all x3, starting transfers between devices, exchanged(): lax.all_to_all(block, 'dp', split_axis=0, concat_axis=0, axis_index_group...  37.1 us
    pallas_call x9, Pallas kernels, call(): pl.pallas_call(run, out_shape=outs, in_specs=[IN_SMEM] * len(index) + [IN...  22 us
    ppermute x22, waiting for transfers between devices, moved(): lax.ppermute(block, axis, [(i, target(i)) for i in range(lax.axis_size(ax...  19.5 us
    unnamed x48, local copies, waits for them, and re-layouts  18 us
  transfers between devices with their start and end apart: 25, of which 7 were waited for; matrix products, arithmetic and copies ran while one was open for 0% of the time, Pallas kernels for 11%

profile of v5, /device:TPU:1, one launch (start us, length us, event | category | flops | bytes accessed | tf_op | source)
XLA Modules:
  0.0 177.9 jit_solution(10087431616657900500)
XLA Ops:
  0.6 4.8 %collective-permute-start = (bf16[16,1024]{1,0:T(8,128)(2,1)}, bf16[16,1024]{1,0:T(8,128)(2,1)S(1)}, u32[]{:S(2)}, u32[]{:S(2)}) collective-permute-start(bf16[16,1024]{1,0:T(8,128)(2,1)} %refs_2_.1), channel_id=1, source_target_pairs={{0,4},{1,5},{2,6},{3,7},{4,0},{5,1},{6,2},{7,3},{8,12},{9,13},{10,... | collective-permute-start | bytes 98312 | tf_op jit(solution)/shard_map/ppermute | solution.py:298
  8.7 4.9 %shard_map.94.refs_0_ = bf16[64,104,128]{2,1,0:T(8,128)(2,1)S(1)} custom-call(s32[8,128]{1,0:T(8,128)S(1)} %bitcast.18, s32[1,128]{1,0:T(1,128)S(1)} %bitcast.20, bf16[1024,128]{1,0:T(8,128)(2,1)S(1)} %bitcast.17, bf16[128,512]{1,0:T(8,128)(2,1)S(1)} %copy-done.13), custom_call_target="tpu_custom_call" | custom-call | tf_op jit(solution)/shard_map/pallas_call | solution.py:83
  15.4 16.3 %all-to-all-start = ((bf16[64,104,128]{2,1,0:T(8,128)(2,1)}), bf16[64,104,128]{2,1,0:T(8,128)(2,1)S(1)}, u32[]{:S(2)}, u32[]{:S(2)}) async-start(bf16[64,104,128]{2,1,0:T(8,128)(2,1)} %get-tuple-element.25), calls=%async_computation | async-start | bytes 3407872 | tf_op jit(solution)/shard_map/all_to_all | solution.py:342
  31.8 3.1 %collective-permute-start.1 = (bf16[16,1024]{1,0:T(8,128)(2,1)S(1)}, bf16[16,1024]{1,0:T(8,128)(2,1)S(1)}, u32[]{:S(2)}, u32[]{:S(2)}) collective-permute-start(bf16[16,1024]{1,0:T(8,128)(2,1)S(1)} %copy-done.18), channel_id=1, source_target_pairs={{0,1},{1,2},{2,3},{3,0},{4,5},{5,6},{6,7},{7,4},{8,9},{9,10},{10,1... | collective-permute-start | bytes 98312 | tf_op jit(solution)/shard_map/ppermute | solution.py:298
  34.9 3.4 %collective-permute-start.3 = (bf16[16,1024]{1,0:T(8,128)(2,1)S(1)}, bf16[16,1024]{1,0:T(8,128)(2,1)S(1)}, u32[]{:S(2)}, u32[]{:S(2)}) collective-permute-start(bf16[16,1024]{1,0:T(8,128)(2,1)S(1)} %copy-done.18), channel_id=1, source_target_pairs={{0,3},{1,0},{2,1},{3,2},{4,7},{5,4},{6,5},{7,6},{8,11},{9,8},{10,9... | collective-permute-start | bytes 98312 | tf_op jit(solution)/shard_map/ppermute | solution.py:298
  38.3 3.4 %collective-permute-start.5 = (bf16[16,1024]{1,0:T(8,128)(2,1)S(1)}, bf16[16,1024]{1,0:T(8,128)(2,1)S(1)}, u32[]{:S(2)}, u32[]{:S(2)}) collective-permute-start(bf16[16,1024]{1,0:T(8,128)(2,1)S(1)} %copy-done.18), channel_id=1, source_target_pairs={{0,2},{1,3},{2,0},{3,1},{4,6},{5,7},{6,4},{7,5},{8,10},{9,11},{10,... | collective-permute-start | bytes 98312 | tf_op jit(solution)/shard_map/ppermute | solution.py:298
  41.7 2.2 %collective-permute-start.2 = (bf16[16,1024]{1,0:T(8,128)(2,1)S(1)}, bf16[16,1024]{1,0:T(8,128)(2,1)S(1)}, u32[]{:S(2)}, u32[]{:S(2)}) collective-permute-start(bf16[16,1024]{1,0:T(8,128)(2,1)S(1)} %copy-done.17), channel_id=1, source_target_pairs={{0,1},{1,2},{2,3},{3,0},{4,5},{5,6},{6,7},{7,4},{8,9},{9,10},{10,1... | collective-permute-start | bytes 98312 | tf_op jit(solution)/shard_map/ppermute | solution.py:298
  44.0 4.3 %collective-permute-start.4 = (bf16[16,1024]{1,0:T(8,128)(2,1)S(1)}, bf16[16,1024]{1,0:T(8,128)(2,1)S(1)}, u32[]{:S(2)}, u32[]{:S(2)}) collective-permute-start(bf16[16,1024]{1,0:T(8,128)(2,1)S(1)} %copy-done.17), channel_id=1, source_target_pairs={{0,3},{1,0},{2,1},{3,2},{4,7},{5,4},{6,5},{7,6},{8,11},{9,8},{10,9... | collective-permute-start | bytes 98312 | tf_op jit(solution)/shard_map/ppermute | solution.py:298
  48.3 2.1 %collective-permute-start.6 = (bf16[16,1024]{1,0:T(8,128)(2,1)S(1)}, bf16[16,1024]{1,0:T(8,128)(2,1)S(1)}, u32[]{:S(2)}, u32[]{:S(2)}) collective-permute-start(bf16[16,1024]{1,0:T(8,128)(2,1)S(1)} %copy-done.17), channel_id=1, source_target_pairs={{0,2},{1,3},{2,0},{3,1},{4,6},{5,7},{6,4},{7,5},{8,10},{9,11},{10,... | collective-permute-start | bytes 98312 | tf_op jit(solution)/shard_map/ppermute | solution.py:298
  50.6 4.1 %collective-permute-done.6.refs_9_ = bf16[16,1024]{1,0:T(8,128)(2,1)S(1)} collective-permute-done((bf16[16,1024]{1,0:T(8,128)(2,1)S(1)}, bf16[16,1024]{1,0:T(8,128)(2,1)S(1)}, u32[]{:S(2)}, u32[]{:S(2)}) %collective-permute-start.6) | collective-permute-done | bytes 32800 | tf_op jit(solution)/shard_map/ppermute | solution.py:298
  55.9 4.6 %collective-permute-start.7 = (f32[512,512]{1,0:T(8,128)S(1)}, f32[512,512]{1,0:T(8,128)S(1)}, u32[]{:S(2)}, u32[]{:S(2)}) collective-permute-start(f32[512,512]{1,0:T(8,128)S(1)} %get-tuple-element.28), channel_id=1, source_target_pairs={{0,8},{8,0},{16,24},{24,16},{32,40},{40,32},{48,56},{56,48},{64,72... | collective-permute-start | bytes 3145736 | tf_op jit(solution)/shard_map/ppermute | solution.py:298
  60.5 5.3 %collective-permute-start.10 = (bf16[16,512]{1,0:T(8,128)(2,1)S(1)}, bf16[16,512]{1,0:T(8,128)(2,1)S(1)}, u32[]{:S(2)}, u32[]{:S(2)}) collective-permute-start(bf16[16,512]{1,0:T(8,128)(2,1)S(1)} %get-tuple-element.29.refs_2_), channel_id=1, source_target_pairs={{0,48},{8,56},{16,0},{24,8},{32,16},{40,24},{48,32},{56,40},{64,11... | collective-permute-start | bytes 49160 | tf_op jit(solution)/shard_map/ppermute | solution.py:298
  67.8 6.1 %collective-permute-start.9 = (bf16[16,512]{1,0:T(8,128)(2,1)S(1)}, bf16[16,512]{1,0:T(8,128)(2,1)S(1)}, u32[]{:S(2)}, u32[]{:S(2)}) collective-permute-start(bf16[16,512]{1,0:T(8,128)(2,1)S(1)} %get-tuple-element.29.refs_2_), channel_id=1, source_target_pairs={{0,32},{8,40},{16,48},{24,56},{32,0},{40,8},{48,16},{56,24},{64,96... | collective-permute-start | bytes 49160 | tf_op jit(solution)/shard_map/ppermute | solution.py:298
  77.5 6.5 %all-to-all-start.2 = ((bf16[8,128,512]{2,1,0:T(8,128)(2,1)}), bf16[8,128,512]{2,1,0:T(8,128)(2,1)S(1)}, u32[]{:S(2)}, u32[]{:S(2)}) async-start(bf16[8,128,512]{2,1,0:T(8,128)(2,1)} %copy-done.10), calls=%async_computation.2 | async-start | bytes 2097152 | tf_op jit(solution)/shard_map/all_to_all | solution.py:342
  84.0 2.2 %collective-permute-start.13 = (bf16[2,640,128]{2,1,0:T(8,128)(2,1)S(1)}, bf16[2,640,128]{2,1,0:T(8,128)(2,1)S(1)}, u32[]{:S(2)}, u32[]{:S(2)}) collective-permute-start(bf16[2,640,128]{2,1,0:T(8,128)(2,1)S(1)} %get-tuple-element.30.refs_1_), channel_id=1, source_target_pairs={{0,4},{1,5},{2,6},{3,7},{4,0},{5,1},{6,2},{7,3},{8,12},{9,13},{10,... | collective-permute-start | bytes 983048 | tf_op jit(solution)/shard_map/ppermute | solution.py:298
  86.2 2.5 %collective-permute-start.11 = (bf16[2,640,128]{2,1,0:T(8,128)(2,1)S(1)}, bf16[2,640,128]{2,1,0:T(8,128)(2,1)S(1)}, u32[]{:S(2)}, u32[]{:S(2)}) collective-permute-start(bf16[2,640,128]{2,1,0:T(8,128)(2,1)S(1)} %get-tuple-element.30.refs_1_), channel_id=1, source_target_pairs={{0,1},{1,2},{2,3},{3,0},{4,5},{5,6},{6,7},{7,4},{8,9},{9,10},{10,1... | collective-permute-start | bytes 983048 | tf_op jit(solution)/shard_map/ppermute | solution.py:298
  88.8 4.6 %collective-permute-done.13.refs_2_ = bf16[2,640,128]{2,1,0:T(8,128)(2,1)S(1)} collective-permute-done((bf16[2,640,128]{2,1,0:T(8,128)(2,1)S(1)}, bf16[2,640,128]{2,1,0:T(8,128)(2,1)S(1)}, u32[]{:S(2)}, u32[]{:S(2)}) %collective-permute-start.13) | collective-permute-done | bytes 327712 | tf_op jit(solution)/shard_map/ppermute | solution.py:298
  93.4 4.8 %collective-permute-start.14 = (bf16[2,640,128]{2,1,0:T(8,128)(2,1)S(1)}, bf16[2,640,128]{2,1,0:T(8,128)(2,1)S(1)}, u32[]{:S(2)}, u32[]{:S(2)}) collective-permute-start(bf16[2,640,128]{2,1,0:T(8,128)(2,1)S(1)} %collective-permute-done.13.refs_2_), channel_id=1, source_target_pairs={{0,3},{1,0},{2,1},{3,2},{4,7},{5,4},{6,5},{7,6},{8,11},{9,8},{10,9... | collective-permute-start | bytes 983048 | tf_op jit(solution)/shard_map/ppermute | solution.py:298
  98.3 2.3 %collective-permute-start.17 = (bf16[2,640,128]{2,1,0:T(8,128)(2,1)S(1)}, bf16[2,640,128]{2,1,0:T(8,128)(2,1)S(1)}, u32[]{:S(2)}, u32[]{:S(2)}) collective-permute-start(bf16[2,640,128]{2,1,0:T(8,128)(2,1)S(1)} %get-tuple-element.30.refs_1_), channel_id=1, source_target_pairs={{0,3},{1,0},{2,1},{3,2},{4,7},{5,4},{6,5},{7,6},{8,11},{9,8},{10,9... | collective-permute-start | bytes 983048 | tf_op jit(solution)/shard_map/ppermute | solution.py:298
  100.5 3.0 %collective-permute-start.16 = (bf16[2,640,128]{2,1,0:T(8,128)(2,1)S(1)}, bf16[2,640,128]{2,1,0:T(8,128)(2,1)S(1)}, u32[]{:S(2)}, u32[]{:S(2)}) collective-permute-start(bf16[2,640,128]{2,1,0:T(8,128)(2,1)S(1)} %collective-permute-done.13.refs_2_), channel_id=1, source_target_pairs={{0,1},{1,2},{2,3},{3,0},{4,5},{5,6},{6,7},{7,4},{8,9},{9,10},{10,1... | collective-permute-start | bytes 983048 | tf_op jit(solution)/shard_map/ppermute | solution.py:298
  105.5 4.8 %collective-permute-start.15 = (bf16[2,640,128]{2,1,0:T(8,128)(2,1)S(1)}, bf16[2,640,128]{2,1,0:T(8,128)(2,1)S(1)}, u32[]{:S(2)}, u32[]{:S(2)}) collective-permute-start(bf16[2,640,128]{2,1,0:T(8,128)(2,1)S(1)} %collective-permute-done.14.refs_6_), channel_id=1, source_target_pairs={{0,3},{1,0},{2,1},{3,2},{4,7},{5,4},{6,5},{7,6},{8,11},{9,8},{10,9... | collective-permute-start | bytes 983048 | tf_op jit(solution)/shard_map/ppermute | solution.py:298
  112.2 2.4 %shard_map.98 = (f32[2,640,512]{2,1,0:T(8,128)S(1)}, bf16[2,256,512]{2,1,0:T(8,128)(2,1)S(1)}, bf16[6,2,640,128]{3,2,1,0:T(8,128)(2,1)S(1)}) custom-call(s32[8]{0:T(128)S(1)} %stack.47.refs_1_.refs_0_, bf16[2,640,128]{2,1,0:T(8,128)(2,1)S(1)} %get-tuple-element.30.refs_1_, bf16[2,640,128]{2,1,0:T(8,128)(2,1)S(1)} %collective-permute-done.13.refs_2_, ...), custom_call_target="tpu_custom_call" | custom-call | tf_op jit(solution)/shard_map/pallas_call | solution.py:83
  117.6 2.7 %shard_map.99 = (bf16[5120,128]{1,0:T(8,128)(2,1)S(1)}, bf16[2,2,640,128]{3,2,1,0:T(8,128)(2,1)S(1)}) custom-call(bf16[2,640,128]{2,1,0:T(8,128)(2,1)S(1)} %collective-permute-done.12.refs_0_, bf16[2,640,128]{2,1,0:T(8,128)(2,1)S(1)} %collective-permute-done.15.refs_1_, bf16[2,256,512]{2,1,0:T(8,128)(2,1)S(1)} %get-tuple-element.31.refs_2_, ...), custom_call_target="tpu_custom_call" | custom-call | tf_op jit(solution)/shard_map/pallas_call | solution.py:83
  123.2 14.3 %all-to-all-start.1 = ((bf16[64,80,128]{2,1,0:T(8,128)(2,1)}), bf16[64,80,128]{2,1,0:T(8,128)(2,1)S(1)}, u32[]{:S(2)}, u32[]{:S(2)}) async-start(bf16[64,80,128]{2,1,0:T(8,128)(2,1)} %bitcast.16), calls=%async_computation.1 | async-start | bytes 2621440 | tf_op jit(solution)/shard_map/all_to_all | solution.py:342
  139.3 2.4 %collective-permute-start.18 = (bf16[512,512]{1,0:T(8,128)(2,1)S(1)}, bf16[512,512]{1,0:T(8,128)(2,1)S(1)}, u32[]{:S(2)}, u32[]{:S(2)}) collective-permute-start(bf16[512,512]{1,0:T(8,128)(2,1)S(1)} %get-tuple-element.36), channel_id=1, source_target_pairs={{0,8},{8,0},{16,24},{24,16},{32,40},{40,32},{48,56},{56,48},{64,72... | collective-permute-start | bytes 1572872 | tf_op jit(solution)/shard_map/ppermute | solution.py:298
  144.3 5.4 %shard_map.101.refs_5_ = bf16[2,1024,512]{2,1,0:T(8,128)(2,1)} custom-call(s32[8]{0:T(128)S(1)} %stack.47.refs_1_.refs_0_, bf16[6,2,640,128]{3,2,1,0:T(8,128)(2,1)S(1)} %copy-done.6, bf16[2,2,640,128]{3,2,1,0:T(8,128)(2,1)S(1)} %copy-done.12, bf16[64,104,128]{2,1,0:T(8,128)(2,1)S(1)} %all-to-all-done.refs_0_.refs_3_), custom_call_target="tpu_custom_call" | custom-call | tf_op jit(solution)/shard_map/pallas_call | solution.py:83
  149.8 4.2 %collective-permute-start.19 = (f32[16,512]{1,0:T(8,128)S(1)}, f32[16,512]{1,0:T(8,128)S(1)}, u32[]{:S(2)}, u32[]{:S(2)}) collective-permute-start(f32[16,512]{1,0:T(8,128)S(1)} %get-tuple-element.42), channel_id=1, source_target_pairs={{0,16},{8,24},{16,32},{24,40},{32,48},{40,56},{48,0},{56,8},{64,80... | collective-permute-start | bytes 98312 | tf_op jit(solution)/shard_map/ppermute | solution.py:298
  154.0 5.2 %collective-permute-start.20 = (f32[16,512]{1,0:T(8,128)S(1)}, f32[16,512]{1,0:T(8,128)S(1)}, u32[]{:S(2)}, u32[]{:S(2)}) collective-permute-start(f32[16,512]{1,0:T(8,128)S(1)} %get-tuple-element.43), channel_id=1, source_target_pairs={{0,32},{8,40},{16,48},{24,56},{32,0},{40,8},{48,16},{56,24},{64,96... | collective-permute-start | bytes 98312 | tf_op jit(solution)/shard_map/ppermute | solution.py:298
  159.2 5.2 %collective-permute-start.21 = (f32[16,512]{1,0:T(8,128)S(1)}, f32[16,512]{1,0:T(8,128)S(1)}, u32[]{:S(2)}, u32[]{:S(2)}) collective-permute-start(f32[16,512]{1,0:T(8,128)S(1)} %get-tuple-element.44), channel_id=1, source_target_pairs={{0,48},{8,56},{16,0},{24,8},{32,16},{40,24},{48,32},{56,40},{64,11... | collective-permute-start | bytes 98312 | tf_op jit(solution)/shard_map/ppermute | solution.py:298
  164.6 2.4 %shard_map.102 = (f32[128,512]{1,0:T(8,128)S(1)}, bf16[128,5120]{1,0:T(8,128)(2,1)S(1)}) custom-call(s32[2]{0:T(128)S(1)} %pad_add_fusion.refs_0_, bf16[128,1024]{1,0:T(8,128)(2,1)S(1)} %get-tuple-element.34.refs_1_, bf16[1024,512]{1,0:T(8,128)(2,1)S(1)} %pad_maximum_fusion.refs_2_, s32[8,128]{1,0:T(8,128)S(1)} %bitcast.19, s32[1,128]{1,0:T(1,128)S(1)} %bitcast.21, ...), custom_call_target="tpu_custom_call" | custom-call | tf_op jit(solution)/shard_map/pallas_call | solution.py:83
  168.0 4.2 %collective-permute-done.19.refs_4_ = f32[16,512]{1,0:T(8,128)S(1)} collective-permute-done((f32[16,512]{1,0:T(8,128)S(1)}, f32[16,512]{1,0:T(8,128)S(1)}, u32[]{:S(2)}, u32[]{:S(2)}) %collective-permute-start.19) | collective-permute-done | bytes 32800 | tf_op jit(solution)/shard_map/ppermute | solution.py:298
  172.2 2.4 %collective-permute-done.20.refs_5_ = f32[16,512]{1,0:T(8,128)S(1)} collective-permute-done((f32[16,512]{1,0:T(8,128)S(1)}, f32[16,512]{1,0:T(8,128)S(1)}, u32[]{:S(2)}, u32[]{:S(2)}) %collective-permute-start.20) | collective-permute-done | bytes 32800 | tf_op jit(solution)/shard_map/ppermute | solution.py:298
  (80 shorter events, 30.6 us)
Async XLA Ops:
  0.6 14.2 %collective-permute-start = (bf16[16,1024]{1,0:T(8,128)(2,1)}, bf16[16,1024]{1,0:T(8,128)(2,1)S(1)}, u32[]{:S(2)}, u32[]{:S(2)}) collective-permute-start(bf16[16,1024]{1,0:T(8,128)(2,1)} %refs_2_.1), channel_id=1, source_target_pairs={{0,4},{1,5},{2,6},{3,7},{4,0},{5,1},{6,2},{7,3},{8,12},{9,13},{10,... | collective-permute-start | bytes 98312 | tf_op jit(solution)/shard_map/ppermute | solution.py:298
  15.4 16.4 %copy-start.18 = (bf16[16,1024]{1,0:T(8,128)(2,1)S(1)}, bf16[16,1024]{1,0:T(8,128)(2,1)}, u32[]{:S(2)}) copy-start(bf16[16,1024]{1,0:T(8,128)(2,1)} %refs_2_.1) | copy-start | bytes 98308
  15.4 26.3 %copy-start.17 = (bf16[16,1024]{1,0:T(8,128)(2,1)S(1)}, bf16[16,1024]{1,0:T(8,128)(2,1)}, u32[]{:S(2)}) copy-start(bf16[16,1024]{1,0:T(8,128)(2,1)} %get-tuple-element.26.refs_3_) | copy-start | bytes 98308
  15.4 39.3 %copy-start.14 = (bf16[128,512]{1,0:T(8,128)(2,1)S(1)}, bf16[128,512]{1,0:T(8,128)(2,1)}, u32[]{:S(2)}) copy-start(bf16[128,512]{1,0:T(8,128)(2,1)} %refs_10_.1) | copy-start | bytes 393220
  15.4 39.3 %copy-start.21 = (bf16[16,512]{1,0:T(8,128)(2,1)S(1)}, bf16[16,512]{1,0:T(8,128)(2,1)}, u32[]{:S(2)}) copy-start(bf16[16,512]{1,0:T(8,128)(2,1)} %refs_11_.1) | copy-start | bytes 49156
  15.4 60.7 %all-to-all-start = ((bf16[64,104,128]{2,1,0:T(8,128)(2,1)}), bf16[64,104,128]{2,1,0:T(8,128)(2,1)S(1)}, u32[]{:S(2)}, u32[]{:S(2)}) async-start(bf16[64,104,128]{2,1,0:T(8,128)(2,1)} %get-tuple-element.25), calls=%async_computation | async-start | bytes 3407872 | tf_op jit(solution)/shard_map/all_to_all | solution.py:342
  31.8 16.5 %collective-permute-start.1 = (bf16[16,1024]{1,0:T(8,128)(2,1)S(1)}, bf16[16,1024]{1,0:T(8,128)(2,1)S(1)}, u32[]{:S(2)}, u32[]{:S(2)}) collective-permute-start(bf16[16,1024]{1,0:T(8,128)(2,1)S(1)} %copy-done.18), channel_id=1, source_target_pairs={{0,1},{1,2},{2,3},{3,0},{4,5},{5,6},{6,7},{7,4},{8,9},{9,10},{10,1... | collective-permute-start | bytes 98312 | tf_op jit(solution)/shard_map/ppermute | solution.py:298
  34.9 15.7 %collective-permute-start.3 = (bf16[16,1024]{1,0:T(8,128)(2,1)S(1)}, bf16[16,1024]{1,0:T(8,128)(2,1)S(1)}, u32[]{:S(2)}, u32[]{:S(2)}) collective-permute-start(bf16[16,1024]{1,0:T(8,128)(2,1)S(1)} %copy-done.18), channel_id=1, source_target_pairs={{0,3},{1,0},{2,1},{3,2},{4,7},{5,4},{6,5},{7,6},{8,11},{9,8},{10,9... | collective-permute-start | bytes 98312 | tf_op jit(solution)/shard_map/ppermute | solution.py:298
  38.3 12.3 %collective-permute-start.5 = (bf16[16,1024]{1,0:T(8,128)(2,1)S(1)}, bf16[16,1024]{1,0:T(8,128)(2,1)S(1)}, u32[]{:S(2)}, u32[]{:S(2)}) collective-permute-start(bf16[16,1024]{1,0:T(8,128)(2,1)S(1)} %copy-done.18), channel_id=1, source_target_pairs={{0,2},{1,3},{2,0},{3,1},{4,6},{5,7},{6,4},{7,5},{8,10},{9,11},{10,... | collective-permute-start | bytes 98312 | tf_op jit(solution)/shard_map/ppermute | solution.py:298
  41.7 8.8 %collective-permute-start.2 = (bf16[16,1024]{1,0:T(8,128)(2,1)S(1)}, bf16[16,1024]{1,0:T(8,128)(2,1)S(1)}, u32[]{:S(2)}, u32[]{:S(2)}) collective-permute-start(bf16[16,1024]{1,0:T(8,128)(2,1)S(1)} %copy-done.17), channel_id=1, source_target_pairs={{0,1},{1,2},{2,3},{3,0},{4,5},{5,6},{6,7},{7,4},{8,9},{9,10},{10,1... | collective-permute-start | bytes 98312 | tf_op jit(solution)/shard_map/ppermute | solution.py:298
  44.0 6.6 %collective-permute-start.4 = (bf16[16,1024]{1,0:T(8,128)(2,1)S(1)}, bf16[16,1024]{1,0:T(8,128)(2,1)S(1)}, u32[]{:S(2)}, u32[]{:S(2)}) collective-permute-start(bf16[16,1024]{1,0:T(8,128)(2,1)S(1)} %copy-done.17), channel_id=1, source_target_pairs={{0,3},{1,0},{2,1},{3,2},{4,7},{5,4},{6,5},{7,6},{8,11},{9,8},{10,9... | collective-permute-start | bytes 98312 | tf_op jit(solution)/shard_map/ppermute | solution.py:298
  48.3 6.5 %collective-permute-start.6 = (bf16[16,1024]{1,0:T(8,128)(2,1)S(1)}, bf16[16,1024]{1,0:T(8,128)(2,1)S(1)}, u32[]{:S(2)}, u32[]{:S(2)}) collective-permute-start(bf16[16,1024]{1,0:T(8,128)(2,1)S(1)} %copy-done.17), channel_id=1, source_target_pairs={{0,2},{1,3},{2,0},{3,1},{4,6},{5,7},{6,4},{7,5},{8,10},{9,11},{10,... | collective-permute-start | bytes 98312 | tf_op jit(solution)/shard_map/ppermute | solution.py:298
  55.9 17.9 %collective-permute-start.7 = (f32[512,512]{1,0:T(8,128)S(1)}, f32[512,512]{1,0:T(8,128)S(1)}, u32[]{:S(2)}, u32[]{:S(2)}) collective-permute-start(f32[512,512]{1,0:T(8,128)S(1)} %get-tuple-element.28), channel_id=1, source_target_pairs={{0,8},{8,0},{16,24},{24,16},{32,40},{40,32},{48,56},{56,48},{64,72... | collective-permute-start | bytes 3145736 | tf_op jit(solution)/shard_map/ppermute | solution.py:298
  60.5 13.6 %collective-permute-start.10 = (bf16[16,512]{1,0:T(8,128)(2,1)S(1)}, bf16[16,512]{1,0:T(8,128)(2,1)S(1)}, u32[]{:S(2)}, u32[]{:S(2)}) collective-permute-start(bf16[16,512]{1,0:T(8,128)(2,1)S(1)} %get-tuple-element.29.refs_2_), channel_id=1, source_target_pairs={{0,48},{8,56},{16,0},{24,8},{32,16},{40,24},{48,32},{56,40},{64,11... | collective-permute-start | bytes 49160 | tf_op jit(solution)/shard_map/ppermute | solution.py:298
  65.8 8.3 %collective-permute-start.8 = (bf16[16,512]{1,0:T(8,128)(2,1)S(1)}, bf16[16,512]{1,0:T(8,128)(2,1)S(1)}, u32[]{:S(2)}, u32[]{:S(2)}) collective-permute-start(bf16[16,512]{1,0:T(8,128)(2,1)S(1)} %get-tuple-element.29.refs_2_), channel_id=1, source_target_pairs={{0,16},{8,24},{16,32},{24,40},{32,48},{40,56},{48,0},{56,8},{64,80... | collective-permute-start | bytes 49160 | tf_op jit(solution)/shard_map/ppermute | solution.py:298
  67.8 8.4 %collective-permute-start.9 = (bf16[16,512]{1,0:T(8,128)(2,1)S(1)}, bf16[16,512]{1,0:T(8,128)(2,1)S(1)}, u32[]{:S(2)}, u32[]{:S(2)}) collective-permute-start(bf16[16,512]{1,0:T(8,128)(2,1)S(1)} %get-tuple-element.29.refs_2_), channel_id=1, source_target_pairs={{0,32},{8,40},{16,48},{24,56},{32,0},{40,8},{48,16},{56,24},{64,96... | collective-permute-start | bytes 49160 | tf_op jit(solution)/shard_map/ppermute | solution.py:298
  77.5 44.7 %all-to-all-start.2 = ((bf16[8,128,512]{2,1,0:T(8,128)(2,1)}), bf16[8,128,512]{2,1,0:T(8,128)(2,1)S(1)}, u32[]{:S(2)}, u32[]{:S(2)}) async-start(bf16[8,128,512]{2,1,0:T(8,128)(2,1)} %copy-done.10), calls=%async_computation.2 | async-start | bytes 2097152 | tf_op jit(solution)/shard_map/all_to_all | solution.py:342
  84.0 9.4 %collective-permute-start.13 = (bf16[2,640,128]{2,1,0:T(8,128)(2,1)S(1)}, bf16[2,640,128]{2,1,0:T(8,128)(2,1)S(1)}, u32[]{:S(2)}, u32[]{:S(2)}) collective-permute-start(bf16[2,640,128]{2,1,0:T(8,128)(2,1)S(1)} %get-tuple-element.30.refs_1_), channel_id=1, source_target_pairs={{0,4},{1,5},{2,6},{3,7},{4,0},{5,1},{6,2},{7,3},{8,12},{9,13},{10,... | collective-permute-start | bytes 983048 | tf_op jit(solution)/shard_map/ppermute | solution.py:298
  86.2 17.3 %collective-permute-start.11 = (bf16[2,640,128]{2,1,0:T(8,128)(2,1)S(1)}, bf16[2,640,128]{2,1,0:T(8,128)(2,1)S(1)}, u32[]{:S(2)}, u32[]{:S(2)}) collective-permute-start(bf16[2,640,128]{2,1,0:T(8,128)(2,1)S(1)} %get-tuple-element.30.refs_1_), channel_id=1, source_target_pairs={{0,1},{1,2},{2,3},{3,0},{4,5},{5,6},{6,7},{7,4},{8,9},{9,10},{10,1... | collective-permute-start | bytes 983048 | tf_op jit(solution)/shard_map/ppermute | solution.py:298
  93.4 12.1 %collective-permute-start.14 = (bf16[2,640,128]{2,1,0:T(8,128)(2,1)S(1)}, bf16[2,640,128]{2,1,0:T(8,128)(2,1)S(1)}, u32[]{:S(2)}, u32[]{:S(2)}) collective-permute-start(bf16[2,640,128]{2,1,0:T(8,128)(2,1)S(1)} %collective-permute-done.13.refs_2_), channel_id=1, source_target_pairs={{0,3},{1,0},{2,1},{3,2},{4,7},{5,4},{6,5},{7,6},{8,11},{9,8},{10,9... | collective-permute-start | bytes 983048 | tf_op jit(solution)/shard_map/ppermute | solution.py:298
  98.3 12.3 %collective-permute-start.17 = (bf16[2,640,128]{2,1,0:T(8,128)(2,1)S(1)}, bf16[2,640,128]{2,1,0:T(8,128)(2,1)S(1)}, u32[]{:S(2)}, u32[]{:S(2)}) collective-permute-start(bf16[2,640,128]{2,1,0:T(8,128)(2,1)S(1)} %get-tuple-element.30.refs_1_), channel_id=1, source_target_pairs={{0,3},{1,0},{2,1},{3,2},{4,7},{5,4},{6,5},{7,6},{8,11},{9,8},{10,9... | collective-permute-start | bytes 983048 | tf_op jit(solution)/shard_map/ppermute | solution.py:298
  100.5 10.0 %collective-permute-start.16 = (bf16[2,640,128]{2,1,0:T(8,128)(2,1)S(1)}, bf16[2,640,128]{2,1,0:T(8,128)(2,1)S(1)}, u32[]{:S(2)}, u32[]{:S(2)}) collective-permute-start(bf16[2,640,128]{2,1,0:T(8,128)(2,1)S(1)} %collective-permute-done.13.refs_2_), channel_id=1, source_target_pairs={{0,1},{1,2},{2,3},{3,0},{4,5},{5,6},{6,7},{7,4},{8,9},{9,10},{10,1... | collective-permute-start | bytes 983048 | tf_op jit(solution)/shard_map/ppermute | solution.py:298
  103.6 14.0 %collective-permute-start.12 = (bf16[2,640,128]{2,1,0:T(8,128)(2,1)S(1)}, bf16[2,640,128]{2,1,0:T(8,128)(2,1)S(1)}, u32[]{:S(2)}, u32[]{:S(2)}) collective-permute-start(bf16[2,640,128]{2,1,0:T(8,128)(2,1)S(1)} %collective-permute-done.11.refs_3_), channel_id=1, source_target_pairs={{0,1},{1,2},{2,3},{3,0},{4,5},{5,6},{6,7},{7,4},{8,9},{9,10},{10,1... | collective-permute-start | bytes 983048 | tf_op jit(solution)/shard_map/ppermute | solution.py:298
  105.5 12.1 %collective-permute-start.15 = (bf16[2,640,128]{2,1,0:T(8,128)(2,1)S(1)}, bf16[2,640,128]{2,1,0:T(8,128)(2,1)S(1)}, u32[]{:S(2)}, u32[]{:S(2)}) collective-permute-start(bf16[2,640,128]{2,1,0:T(8,128)(2,1)S(1)} %collective-permute-done.14.refs_6_), channel_id=1, source_target_pairs={{0,3},{1,0},{2,1},{3,2},{4,7},{5,4},{6,5},{7,6},{8,11},{9,8},{10,9... | collective-permute-start | bytes 983048 | tf_op jit(solution)/shard_map/ppermute | solution.py:298
  123.2 51.4 %all-to-all-start.1 = ((bf16[64,80,128]{2,1,0:T(8,128)(2,1)}), bf16[64,80,128]{2,1,0:T(8,128)(2,1)S(1)}, u32[]{:S(2)}, u32[]{:S(2)}) async-start(bf16[64,80,128]{2,1,0:T(8,128)(2,1)} %bitcast.16), calls=%async_computation.1 | async-start | bytes 2621440 | tf_op jit(solution)/shard_map/all_to_all | solution.py:342
  139.3 25.1 %collective-permute-start.18 = (bf16[512,512]{1,0:T(8,128)(2,1)S(1)}, bf16[512,512]{1,0:T(8,128)(2,1)S(1)}, u32[]{:S(2)}, u32[]{:S(2)}) collective-permute-start(bf16[512,512]{1,0:T(8,128)(2,1)S(1)} %get-tuple-element.36), channel_id=1, source_target_pairs={{0,8},{8,0},{16,24},{24,16},{32,40},{40,32},{48,56},{56,48},{64,72... | collective-permute-start | bytes 1572872 | tf_op jit(solution)/shard_map/ppermute | solution.py:298
  149.8 14.7 %copy-start.1 = (bf16[2,1024,512]{2,1,0:T(8,128)(2,1)S(1)}, bf16[2,1024,512]{2,1,0:T(8,128)(2,1)}, u32[]{:S(2)}) copy-start(bf16[2,1024,512]{2,1,0:T(8,128)(2,1)} %shard_map.101.refs_5_) | copy-start | bytes 6291460
  149.8 14.7 %copy-start.20 = (s32[128,8]{0,1:T(8,128)S(1)}, s32[128,8]{0,1:T(8,128)}, u32[]{:S(2)}) copy-start(s32[128,8]{0,1:T(8,128)} %param.12) | copy-start | bytes 12292
  149.8 14.8 %copy-start.23 = (s32[128]{0:T(128)S(1)}, s32[128]{0:T(128)}, u32[]{:S(2)}) copy-start(s32[128]{0:T(128)} %param.13) | copy-start | bytes 1540
  149.8 22.4 %collective-permute-start.19 = (f32[16,512]{1,0:T(8,128)S(1)}, f32[16,512]{1,0:T(8,128)S(1)}, u32[]{:S(2)}, u32[]{:S(2)}) collective-permute-start(f32[16,512]{1,0:T(8,128)S(1)} %get-tuple-element.42), channel_id=1, source_target_pairs={{0,16},{8,24},{16,32},{24,40},{32,48},{40,56},{48,0},{56,8},{64,80... | collective-permute-start | bytes 98312 | tf_op jit(solution)/shard_map/ppermute | solution.py:298
  154.0 20.6 %collective-permute-start.20 = (f32[16,512]{1,0:T(8,128)S(1)}, f32[16,512]{1,0:T(8,128)S(1)}, u32[]{:S(2)}, u32[]{:S(2)}) collective-permute-start(f32[16,512]{1,0:T(8,128)S(1)} %get-tuple-element.43), channel_id=1, source_target_pairs={{0,32},{8,40},{16,48},{24,56},{32,0},{40,8},{48,16},{56,24},{64,96... | collective-permute-start | bytes 98312 | tf_op jit(solution)/shard_map/ppermute | solution.py:298
  159.2 15.4 %collective-permute-start.21 = (f32[16,512]{1,0:T(8,128)S(1)}, f32[16,512]{1,0:T(8,128)S(1)}, u32[]{:S(2)}, u32[]{:S(2)}) collective-permute-start(f32[16,512]{1,0:T(8,128)S(1)} %get-tuple-element.44), channel_id=1, source_target_pairs={{0,48},{8,56},{16,0},{24,8},{32,16},{40,24},{48,32},{56,40},{64,11... | collective-permute-start | bytes 98312 | tf_op jit(solution)/shard_map/ppermute | solution.py:298
  (17 other events, 18.0 us)
